TPU v7x, 128 devices: a whole 4x4x4 slice. The times are simulated.
128 devices in a mesh: dp: 8 (over x, core), vocab: 16 (over z, y).
Axes of the slice: x: 4, y: 4, z: 4, core: 2. Of those that a mesh axis runs over, the one named last changes fastest.
Arguments:
- hidden: bfloat16 [2048, 7168], P('dp'), may hold values from -6 to 6
- head_weight: bfloat16 [7168, 8192], P('dp', 'vocab'), may hold values from -0.0625 to 0.0625
- proj_mid: bfloat16 [7168, 1792], P('dp', 'vocab'), may hold values from -0.0625 to 0.0625
- proj_tail: bfloat16 [7168, 448], P('dp', 'vocab'), may hold values from -0.0625 to 0.0625
- mid_weight: bfloat16 [1792, 20480], P('dp', 'vocab'), may hold values from -0.125 to 0.125
- tail_weight: bfloat16 [448, 36864], P('dp', 'vocab'), may hold values from -0.25 to 0.25
- target_head: bfloat16 [2048, 8192], P('dp', 'vocab'), may hold values from -20 to 420
- target_mid: bfloat16 [2048, 20480], P('dp', 'vocab'), may hold values from -20 to 420
- target_tail: bfloat16 [2048, 36864], P('dp', 'vocab'), may hold values from -20 to 420
- top_ids: int32 [2048], P('dp'), may hold values from 0 to 65535
- tier_of: int32 [65536], replicated, may hold values from 0 to 65535, each once
Outputs:
- head_grad: bfloat16 [7168, 8192], P('dp', 'vocab')
- proj_mid_grad: bfloat16 [7168, 1792], P('dp', 'vocab')
- proj_tail_grad: bfloat16 [7168, 448], P('dp', 'vocab')
- mid_grad: bfloat16 [1792, 20480], P('dp', 'vocab')
- tail_grad: bfloat16 [448, 36864], P('dp', 'vocab')
- hidden_grad: bfloat16 [2048, 7168], P('dp', 'vocab')
- row_loss: float32 [2048], P('dp')
Inputs may be any that keep to these rules, and one draw needn't show every extreme that they name: `tier_of`: ids below 8192 in tier order are the head tier, then 20480 of the middle tier, then the last tier.
All inputs are finite; a program needn't handle non-finite values.
Results may differ from a plain program's by a relative error of at most 0.03.
Values may be sent and summed in bfloat16 or wider, within the bound.
No kernel may reach another device: no remote copies, remote signals or barrier semaphores. Data moves between devices by JAX's collectives and lax.ppermute only.
A program may use at most 128 MiB of HBM per device.

v0:
```python
import functools

import jax
import jax.numpy as jnp
from jax import lax
from jax.experimental import pallas as pl
from jax.experimental.pallas import tpu as pltpu
from jax.sharding import PartitionSpec as P

BF16 = jnp.bfloat16
F32 = jnp.float32


def dot(left, right, left_dim, right_dim):
    return lax.dot_general(
        left, right, (((left_dim,), (right_dim,)), ((), ())), preferred_element_type=F32
    )


def swap(block, flip):
    return lax.ppermute(block, "dp", [(i, i ^ flip) for i in range(lax.axis_size("dp"))])


def place_kernel(axis, me_ref, *refs):
    blocks, out, sems = refs[:-2], refs[-2], refs[-1]
    copies = []
    for flip, block in enumerate(blocks):
        size = block.shape[axis]
        start = pl.multiple_of((me_ref[0] ^ flip) * size, size)
        spot = out.at[pl.ds(start, size)] if axis == 0 else out.at[:, pl.ds(start, size)]
        copies.append(pltpu.make_async_copy(block, spot, sems.at[flip]))
    for copy in copies:
        copy.start()
    for copy in copies:
        copy.wait()


def place(blocks, axis):
    shape = list(blocks[0].shape)
    shape[axis] *= len(blocks)
    moved = 2 * len(blocks) * blocks[0].size * blocks[0].dtype.itemsize
    return pl.pallas_call(
        functools.partial(place_kernel, axis),
        out_shape=jax.ShapeDtypeStruct(tuple(shape), blocks[0].dtype),
        in_specs=[pl.BlockSpec(memory_space=pltpu.SMEM)]
        + [pl.BlockSpec(memory_space=pltpu.VMEM)] * len(blocks),
        out_specs=pl.BlockSpec(memory_space=pl.ANY),
        scratch_shapes=[pltpu.SemaphoreType.DMA((len(blocks),))],
        compiler_params=pltpu.CompilerParams(vmem_limit_bytes=16 << 20),
        cost_estimate=pl.CostEstimate(flops=0, bytes_accessed=moved, transcendentals=0),
    )(lax.axis_index("dp").astype(jnp.int32).reshape(1), *blocks)


def gather_dp(block, axis):
    half = block.shape[0] // 32 * 16
    near = swap(block, 2)
    other = swap(block, 6)
    far = jnp.concatenate([swap(other[:half], 2), swap(near[half:], 6)], axis=0)
    parts = [block, near, far, other]
    return place([p for part in parts for p in (part, swap(part, 1))], axis)


def spread_vocab(block):
    size = lax.axis_size("vocab")
    return lax.all_to_all(jnp.broadcast_to(block[None], (size,) + block.shape), "vocab", 0, 0)


def per_device(
    hidden,
    head_weight,
    proj_mid,
    proj_tail,
    mid_weight,
    tail_weight,
    target_head,
    target_mid,
    target_tail,
    top_ids,
    tier_of,
):
    n_vocab = lax.axis_size("vocab")
    n_dp = lax.axis_size("dp")
    v = lax.axis_index("vocab")
    rows, width = hidden.shape
    depth = head_weight.shape[0]
    rank_mid, rank_tail = proj_mid.shape[1], proj_tail.shape[1]
    ranks = rank_mid + rank_tail

    with jax.named_scope("gather_proj"):
        pad = -ranks % 16
        proj_t = jnp.concatenate(
            [proj_mid.T, proj_tail.T, jnp.zeros((pad, depth), BF16)], axis=0
        )
        proj_full = gather_dp(proj_t, 1)
    with jax.named_scope("gather_mid_tail"):
        mid_full = lax.all_gather(mid_weight, "dp", axis=0, tiled=True)
        tail_full = lax.all_gather(tail_weight, "dp", axis=0, tiled=True)
    with jax.named_scope("codes"):
        codes = dot(proj_full, hidden, 1, 1).astype(BF16)
    with jax.named_scope("spread_codes"):
        codes_all = spread_vocab(codes)
        z_mid = codes_all[:, :rank_mid].reshape(n_vocab * rank_mid, rows)
        z_tail = codes_all[:, rank_mid:ranks].reshape(n_vocab * rank_tail, rows)
    with jax.named_scope("gather_head"):
        head_full = gather_dp(head_weight, 0)
    with jax.named_scope("spread_hidden"):
        piece = rows // n_vocab
        mine = lax.dynamic_slice_in_dim(hidden, v * piece, piece, 0)
        mine = mine.reshape(piece, n_dp, depth).transpose(1, 0, 2)
        mine = lax.all_to_all(mine, "dp", 0, 0)
        x_all = spread_vocab(mine)
        x_all = x_all.transpose(1, 0, 2, 3).reshape(n_dp * rows, depth)

    with jax.named_scope("logits"):
        logits = (
            dot(hidden, head_full, 1, 0),
            dot(z_mid, mid_full, 0, 0),
            dot(z_tail, tail_full, 0, 0),
        )
    with jax.named_scope("statistics"):
        targets = (target_head.astype(F32), target_mid.astype(F32), target_tail.astype(F32))
        widths = (head_weight.shape[1], mid_weight.shape[1], tail_weight.shape[1])
        starts = (0, widths[0] * n_vocab, (widths[0] + widths[1]) * n_vocab)
        positions = jnp.take(tier_of, top_ids)
        hits = [
            positions[:, None] == (start + v * w + jnp.arange(w, dtype=jnp.int32))[None, :]
            for start, w in zip(starts, widths)
        ]

        def top(blocks):
            return jnp.max(jnp.stack([jnp.max(block, axis=1) for block in blocks]), axis=0)

        near_s, near_t = top(logits), top(targets)
        mass_s = sum(jnp.sum(jnp.exp(s - near_s[:, None]), axis=1) for s in logits)
        mass_t = sum(jnp.sum(jnp.exp(t - near_t[:, None]), axis=1) for t in targets)
        cross = sum(
            jnp.sum(jnp.exp(t - near_t[:, None]) * (t - s), axis=1)
            for s, t in zip(logits, targets)
        )
        picked = sum(
            jnp.sum(jnp.where(hit, s, 0.0), axis=1) for s, hit in zip(logits, hits)
        )
        zero = jnp.zeros_like(picked)
        packed = jnp.stack([near_s, near_t, mass_s, mass_t, cross, picked, zero, zero])
    with jax.named_scope("spread_statistics"):
        packed, x_all = lax.optimization_barrier((packed, x_all))
        packed = spread_vocab(packed)
        near_s, near_t, mass_s, mass_t, cross, picked = (packed[:, k] for k in range(6))
        top_s, top_t = jnp.max(near_s, axis=0), jnp.max(near_t, axis=0)
        scale_s, scale_t = jnp.exp(near_s - top_s[None]), jnp.exp(near_t - top_t[None])
        mass_s = jnp.sum(mass_s * scale_s, axis=0)
        mass_t = jnp.sum(mass_t * scale_t, axis=0)
        cross = jnp.sum(cross * scale_t, axis=0)
        picked = jnp.sum(picked, axis=0)
        lse_s = top_s + jnp.log(mass_s)
        lse_t = top_t + jnp.log(mass_t)
        row_loss = cross / mass_t - lse_t + 2.0 * lse_s - picked
    with jax.named_scope("grad_logits"):
        g_head, g_mid, g_tail = tuple(
            (
                2.0 * jnp.exp(s - lse_s[:, None])
                - jnp.exp(t - lse_t[:, None])
                - jnp.where(hit, 1.0, 0.0)
            ).astype(BF16)
            for s, t, hit in zip(logits, targets, hits)
        )

    with jax.named_scope("code_grads"):
        dz = jnp.concatenate(
            [
                dot(mid_full, g_mid, 1, 1).astype(BF16).reshape(n_vocab, rank_mid, rows),
                dot(tail_full, g_tail, 1, 1).astype(BF16).reshape(n_vocab, rank_tail, rows),
                jnp.zeros((n_vocab, pad, rows), BF16),
            ],
            axis=1,
        )
        dz = lax.all_to_all(dz, "vocab", 0, 0)
        dz = jnp.sum(dz.astype(F32), axis=0).astype(BF16)
    with jax.named_scope("mid_tail_grads"):
        mid_grad = lax.psum_scatter(
            dot(z_mid, g_mid, 1, 0).astype(BF16), "dp", scatter_dimension=0, tiled=True
        )
        tail_grad = lax.psum_scatter(
            dot(z_tail, g_tail, 1, 0).astype(BF16), "dp", scatter_dimension=0, tiled=True
        )
    with jax.named_scope("hidden_grad"):
        term = dot(head_full, g_head, 1, 1) + dot(proj_full, dz, 0, 0)
        term = term.astype(BF16).reshape(n_vocab, width // n_vocab, rows)
        term = lax.all_to_all(term, "vocab", 0, 0)
        hidden_grad = jnp.sum(term.astype(F32), axis=0).astype(BF16).T
    with jax.named_scope("head_proj_grads"):
        g_all = gather_dp(g_head, 0)
        head_grad = dot(x_all, g_all, 0, 0).astype(BF16)
        dz_all = gather_dp(dz, 1)
        proj_grad = dot(x_all, dz_all, 0, 1).astype(BF16)
    return (
        head_grad,
        proj_grad[:, :rank_mid],
        proj_grad[:, rank_mid:ranks],
        mid_grad,
        tail_grad,
        hidden_grad,
        row_loss,
    )


def solution(mesh):
    split = P("dp", "vocab")
    in_specs = (P("dp", None),) + (split,) * 8 + (P("dp"), P())
    out_specs = (split,) * 6 + (P("dp"),)
    return jax.shard_map(
        per_device, mesh=mesh, in_specs=in_specs, out_specs=out_specs, check_vma=False
    )
```

profile of v0, /device:TPU:0, one launch (start us, length us, event | category | flops | bytes accessed | tf_op | source)
XLA Modules:
  0.0 268.6 jit_solution(12466172309450267554)
XLA Ops:
  8.8 1.1 maximum_maximum_fusion.1.refs_0_
  9.8 2.9 %collective-permute-start.11 = (bf16[144,896]{1,0:T(8,128)(2,1)S(1)}, bf16[144,896]{1,0:T(8,128)(2,1)S(1)}, u32[]{:S(2)}, u32[]{:S(2)}) collective-permute-start(bf16[144,896]{1,0:T(8,128)(2,1)S(1)} %maximum_maximum_fusion.1.refs_0_), channel_id=1, source_target_pairs={{0,96},{16,112},{32,64},{48,80},{64,32},{80,48},{96,0},{112,16},{1... | collective-permute-start | bytes 774152 | tf_op jit(solution)/shard_map/gather_proj/ppermute | solution.py:21
  13.0 6.0 %collective-permute-done.11.refs_6_ = bf16[144,896]{1,0:T(8,128)(2,1)S(1)} collective-permute-done((bf16[144,896]{1,0:T(8,128)(2,1)S(1)}, bf16[144,896]{1,0:T(8,128)(2,1)S(1)}, u32[]{:S(2)}, u32[]{:S(2)}) %collective-permute-start.11) | collective-permute-done | bytes 258080 | tf_op jit(solution)/shard_map/gather_proj/ppermute | solution.py:21
  19.5 0.9 collective-permute-done.9.refs_2_
  20.5 1.7 collective-permute-start.13
  22.7 1.2 collective-permute-done.12
  23.9 5.5 %collective-permute-done.13 = bf16[80,896]{1,0:T(8,128)(2,1)S(1)} collective-permute-done((bf16[80,896]{1,0:T(8,128)(2,1)S(1)}, bf16[80,896]{1,0:T(8,128)(2,1)S(1)}, u32[]{:S(2)}, u32[]{:S(2)}) %collective-permute-start.13) | collective-permute-done | bytes 143392 | tf_op jit(solution)/shard_map/gather_proj/ppermute | solution.py:21
  29.5 1.0 constant_dynamic-slice_fusion
  31.2 3.4 %all-to-all-start.1 = ((bf16[8,16,896]{2,1,0:T(8,128)(2,1)}), bf16[8,16,896]{2,1,0:T(8,128)(2,1)S(1)}, u32[]{:S(2)}, u32[]{:S(2)}) async-start(bf16[8,16,896]{2,1,0:T(8,128)(2,1)} %copy.41), calls=%async_computation.1 | async-start | bytes 458752 | tf_op jit(solution)/shard_map/spread_hidden/all_to_all | solution.py:110
  35.1 1.4 copy-done.3
  36.4 1.0 copy-done.16
  37.5 1.4 convolution_convert_fusion.6
  38.8 2.9 %all-to-all-done.1 = bf16[8,16,896]{2,1,0:T(8,128)(2,1)S(1)} async-done(((bf16[8,16,896]{2,1,0:T(8,128)(2,1)}), bf16[8,16,896]{2,1,0:T(8,128)(2,1)S(1)}, u32[]{:S(2)}, u32[]{:S(2)}) %all-to-all-start.1) | async-done | bytes 229408 | tf_op jit(solution)/shard_map/spread_hidden/all_to_all | solution.py:110
  41.7 1.1 broadcast_in_dim.43
  42.9 9.1 %all-to-all-start = ((bf16[16,144,256]{2,1,0:T(8,128)(2,1)}), bf16[16,144,256]{2,1,0:T(8,128)(2,1)S(1)}, u32[]{:S(2)}, u32[]{:S(2)}) async-start(bf16[16,144,256]{2,1,0:T(8,128)(2,1)} %broadcast_in_dim.43), calls=%async_computation | async-start | bytes 2359296 | tf_op jit(solution)/shard_map/spread_codes/all_to_all | solution.py:65
  52.0 1.2 collective-permute-start.3
  53.2 17.6 %all-to-all-done = bf16[16,144,256]{2,1,0:T(8,128)(2,1)S(1)} async-done(((bf16[16,144,256]{2,1,0:T(8,128)(2,1)}), bf16[16,144,256]{2,1,0:T(8,128)(2,1)S(1)}, u32[]{:S(2)}, u32[]{:S(2)}) %all-to-all-start) | async-done | bytes 1179680 | tf_op jit(solution)/shard_map/spread_codes/all_to_all | solution.py:65
  70.9 2.2 broadcast_in_dim.53
  73.1 4.5 %all-to-all-start.2 = ((bf16[16,8,16,896]{3,2,1,0:T(8,128)(2,1)}), bf16[16,8,16,896]{3,2,1,0:T(8,128)(2,1)}, u32[]{:S(2)}, u32[]{:S(2)}) async-start(bf16[16,8,16,896]{3,2,1,0:T(8,128)(2,1)} %broadcast_in_dim.53), calls=%async_computation.2 | async-start | bytes 7340032 | tf_op jit(solution)/shard_map/spread_hidden/all_to_all | solution.py:65
  77.7 14.8 %collective-permute-done.3.refs_6_ = bf16[896,512]{1,0:T(8,128)(2,1)S(1)} collective-permute-done((bf16[896,512]{1,0:T(8,128)(2,1)}, bf16[896,512]{1,0:T(8,128)(2,1)S(1)}, u32[]{:S(2)}, u32[]{:S(2)}) %collective-permute-start.3) | collective-permute-done | bytes 917536 | tf_op jit(solution)/shard_map/gather_head/ppermute | solution.py:21
  92.9 1.2 collective-permute-start.5
  94.6 9.9 %collective-permute-done.4 = bf16[448,512]{1,0:T(8,128)(2,1)S(1)} collective-permute-done((bf16[448,512]{1,0:T(8,128)(2,1)S(1)}, bf16[448,512]{1,0:T(8,128)(2,1)S(1)}, u32[]{:S(2)}, u32[]{:S(2)}) %collective-permute-start.4) | collective-permute-done | bytes 458784 | tf_op jit(solution)/shard_map/gather_head/ppermute | solution.py:21
  104.6 1.3 collective-permute-done.5
  106.9 1.5 reduce_max.170
  108.4 1.3 reduce_max.167
  109.7 1.7 gather_fusion
  111.6 2.2 slice.78
  113.8 4.3 %gather_head.1 = bf16[7168,512]{1,0:T(8,128)(2,1)S(1)} custom-call(s32[1]{0:T(128)} %bitcast.me_ref, bf16[896,512]{1,0:T(8,128)(2,1)} %refs_0_.1, bf16[896,512]{1,0:T(8,128)(2,1)} %collective-permute-done.refs_1_, bf16[896,512]{1,0:T(8,128)(2,1)S(1)} %collective-permute-done.1.refs_2_, bf16[896,512]{1,0:T(8,128)(2,1)} %collective-permute-done.2.refs_3_, ...), custom_call_target="tpu_custom_call" | custom-call | bytes 14680064 | tf_op jit(solution)/shard_map/gather_head/pallas_call | solution.py:42
  118.1 2.1 fusion.47
  121.0 1.0 copy.40
  122.0 2.5 fusion.46
  124.5 1.9 all-to-all-done.2
  126.4 4.1 %copy.42 = bf16[16,8,16,896]{3,2,0,1:T(8,128)(2,1)} copy(bf16[16,8,16,896]{3,2,1,0:T(8,128)(2,1)} %all-to-all-done.2) | data formatting | bytes 7340032 | tf_op jit(solution)/shard_map/spread_hidden/all_to_all | solution.py:65
  130.5 3.9 %fusion.48 = (f32[256]{0:T(256)S(1)}, f32[256,1280]{1,0:T(8,128)S(1)}) fusion(bf16[1792,256]{1,0:T(8,128)(2,1)S(1)} %bitcast.98, bf16[1792,1280]{1,0:T(8,128)(2,1)} %all-gather.3.cloned.1.call-done), kind=kOutput, calls=%fused_computation.107 | convolution fusion | flops 1174732544 | bytes 6816768 | tf_op jit(solution)/shard_map/logits/dot_general | solution.py:15
  134.4 1.5 fusion.2
  135.9 0.9 fusion.11
  139.2 12.9 %all_to_all.30 = f32[16,8,256]{2,1,0:T(8,128)S(1)} all-to-all(f32[16,8,256]{2,1,0:T(8,128)S(1)} %broadcast_in_dim.54), channel_id=1, replica_groups=mesh['dp'=8,'vocab'=16] {'vocab'}, dimensions={0} | all-to-all | bytes 262144 | tf_op jit(solution)/shard_map/spread_statistics/all_to_all | solution.py:65
  152.9 2.4 fusion.4
  155.2 1.0 copy-done.14
  156.3 2.1 convolution_convert_fusion.1
  159.9 3.7 %convolution_convert_fusion = bf16[1792,1280]{1,0:T(8,128)(2,1)} fusion(bf16[1792,256]{1,0:T(8,128)(2,1)S(1)} %bitcast.99, bf16[256,1280]{1,0:T(8,128)(2,1)S(1)} %copy-done.8, f32[256,1280]{1,0:T(8,128)S(1)} %copy-done.10, f32[256]{0:T(256)S(1)} %get-tuple-element.38, f32[256]{0:T(256)S(1)} %get-tuple-element.29, s32[1280]{0:T(1024)S(1)} %iota_add_fusion.1, ...), kind=kOutput, calls=%fused_computation.3 | convolution fusion | flops 1179648000 | bytes 7479296 | tf_op jit(solution)/shard_map/mid_tail_grads/dot_general | solution.py:15
  163.7 5.2 %fusion.1 = bf16[1792,256]{0,1:T(8,128)(2,1)} fusion(bf16[1792,1280]{1,0:T(8,128)(2,1)} %all-gather.3.cloned.1.call-done, bf16[256,1280]{1,0:T(8,128)(2,1)S(1)} %copy-done.8, f32[256,1280]{1,0:T(8,128)S(1)} %copy-done.10, f32[256]{0:T(256)S(1)} %get-tuple-element.38, f32[256]{0:T(256)S(1)} %get-tuple-element.29, s32[1280]{0:T(1024)S(1)} %iota_add_fusion.1, ...), kind=kOutput, calls=%fused_computation.11 | convolution fusion | flops 1177812992 | bytes 7479296 | tf_op jit(solution)/shard_map/code_grads/dot_general | solution.py:15
  168.9 1.5 copy.46
  170.4 2.3 fusion.20
  172.8 1.6 maximum_maximum_fusion
  174.4 4.4 %all-to-all-start.4 = ((bf16[16,144,256]{2,1,0:T(8,128)(2,1)}), bf16[16,144,256]{2,1,0:T(8,128)(2,1)}, u32[]{:S(2)}, u32[]{:S(2)}) async-start(bf16[16,144,256]{2,1,0:T(8,128)(2,1)} %maximum_maximum_fusion), calls=%async_computation.4 | async-start | bytes 2359296 | tf_op jit(solution)/shard_map/code_grads/all_to_all | solution.py:177
  179.1 18.5 %all-to-all-done.4 = bf16[16,144,256]{2,1,0:T(8,128)(2,1)} async-done(((bf16[16,144,256]{2,1,0:T(8,128)(2,1)}), bf16[16,144,256]{2,1,0:T(8,128)(2,1)}, u32[]{:S(2)}, u32[]{:S(2)}) %all-to-all-start.4) | async-done | bytes 1179680 | tf_op jit(solution)/shard_map/code_grads/all_to_all | solution.py:177
  197.6 1.6 reduce_sum.182.refs_0_
  199.2 2.9 %fusion.49 = f32[7168,256]{1,0:T(8,128)S(1)} fusion(bf16[144,7168]{1,0:T(8,128)(2,1)} %copy-done.3, bf16[144,256]{1,0:T(8,128)(2,1)S(1)} %reduce_sum.182.refs_0_), kind=kOutput, calls=%fused_computation.108 | convolution fusion | flops 528482304 | bytes 9478144 | tf_op jit(solution)/shard_map/hidden_grad/dot_general | solution.py:15
  202.5 4.1 %fusion = bf16[7168,256]{1,0:T(8,128)(2,1)} fusion(f32[7168,256]{1,0:T(8,128)S(1)} %fusion.49, bf16[7168,512]{1,0:T(8,128)(2,1)S(1)} %bitcast.94, bf16[256,512]{1,0:T(8,128)(2,1)S(1)} %fusion.23.refs_0_), kind=kOutput, calls=%fused_computation.2 | convolution fusion | flops 1882718208 | bytes 18612224 | tf_op jit(solution)/shard_map/hidden_grad/dot_general | solution.py:15
  206.7 4.5 %all-to-all-start.5 = ((bf16[16,448,256]{2,1,0:T(8,128)(2,1)}), bf16[16,448,256]{2,1,0:T(8,128)(2,1)}, u32[]{:S(2)}, u32[]{:S(2)}) async-start(bf16[16,448,256]{2,1,0:T(8,128)(2,1)} %bitcast.95), calls=%async_computation.7 | async-start | bytes 7340032 | tf_op jit(solution)/shard_map/hidden_grad/all_to_all | solution.py:189
  212.0 10.6 %collective-permute-done.19.refs_6_ = bf16[256,512]{1,0:T(8,128)(2,1)S(1)} collective-permute-done((bf16[256,512]{1,0:T(8,128)(2,1)S(1)}, bf16[256,512]{1,0:T(8,128)(2,1)S(1)}, u32[]{:S(2)}, u32[]{:S(2)}) %collective-permute-start.19) | collective-permute-done | bytes 262176 | tf_op jit(solution)/shard_map/head_proj_grads/ppermute | solution.py:21
  222.7 2.8 %collective-permute-start.21 = (bf16[128,512]{1,0:T(8,128)(2,1)S(1)}, bf16[128,512]{1,0:T(8,128)(2,1)S(1)}, u32[]{:S(2)}, u32[]{:S(2)}) collective-permute-start(bf16[128,512]{1,0:T(8,128)(2,1)S(1)} %slice.85), channel_id=1, source_target_pairs={{0,96},{16,112},{32,64},{48,80},{64,32},{80,48},{96,0},{112,16},{1... | collective-permute-start | bytes 393224 | tf_op jit(solution)/shard_map/head_proj_grads/ppermute | solution.py:21
  226.0 3.1 %collective-permute-done.20 = bf16[128,512]{1,0:T(8,128)(2,1)S(1)} collective-permute-done((bf16[128,512]{1,0:T(8,128)(2,1)S(1)}, bf16[128,512]{1,0:T(8,128)(2,1)S(1)}, u32[]{:S(2)}, u32[]{:S(2)}) %collective-permute-start.20) | collective-permute-done | bytes 131104 | tf_op jit(solution)/shard_map/head_proj_grads/ppermute | solution.py:21
  229.1 1.3 collective-permute-done.21
  230.5 2.4 collective-permute-start.27
  233.0 4.4 %collective-permute-done.27.refs_6_ = bf16[144,256]{1,0:T(8,128)(2,1)S(1)} collective-permute-done((bf16[144,256]{1,0:T(8,128)(2,1)S(1)}, bf16[144,256]{1,0:T(8,128)(2,1)S(1)}, u32[]{:S(2)}, u32[]{:S(2)}) %collective-permute-start.27) | collective-permute-done | bytes 73760 | tf_op jit(solution)/shard_map/head_proj_grads/ppermute | solution.py:21
  237.4 2.1 collective-permute-start.28
  240.1 1.6 collective-permute-done.25.refs_2_
  241.8 2.3 collective-permute-start.29
  244.6 2.4 collective-permute-done.29
  247.0 3.0 %convolution_convert_fusion.3 = bf16[896,512]{1,0:T(8,128)(2,1)} fusion(bf16[2048,896]{1,0:T(8,128)(2,1)S(1)} %bitcast.96, bf16[2048,512]{1,0:T(8,128)(2,1)S(1)} %head_proj_grads.2), kind=kOutput, calls=%fused_computation.27 | convolution fusion | flops 1879506944 | bytes 6684672 | tf_op jit(solution)/shard_map/head_proj_grads/dot_general | solution.py:15
  252.3 6.4 %all-to-all-done.5 = bf16[16,448,256]{2,1,0:T(8,128)(2,1)} async-done(((bf16[16,448,256]{2,1,0:T(8,128)(2,1)}), bf16[16,448,256]{2,1,0:T(8,128)(2,1)}, u32[]{:S(2)}, u32[]{:S(2)}) %all-to-all-start.5) | async-done | bytes 3670048 | tf_op jit(solution)/shard_map/hidden_grad/all_to_all | solution.py:189
  258.7 3.3 %reduce_sum.183 = bf16[448,256]{1,0:T(8,128)(2,1)} reduce(bf16[16,448,256]{2,1,0:T(8,128)(2,1)} %all-to-all-done.5, bf16[]{:T(256)} %constant.23.clone.1), dimensions={0}, to_apply=%region_25.26 | reduce | flops 1720320 | bytes 3899394 | tf_op jit(solution)/shard_map/hidden_grad/reduce_sum | solution.py:190
  (157 shorter events, 17.4 us)
Async XLA Ops:
  7.2 102.5 %copy-start = (s32[65536]{0:T(1024)S(1)}, s32[65536]{0:T(1024)}, u32[]{:S(2)}) copy-start(s32[65536]{0:T(1024)} %param.21) | copy-start | bytes 786436
  7.2 114.9 %all-gather.5.cloned.1.call-start = ((), (), s32[]{:S(2)}) async-start(), calls=%async_computation.9 | async-start | bytes 2322432 | tf_op jit(solution)/shard_map/gather_mid_tail/all_gather | solution.py:97
  7.9 122.6 %all-gather.3.cloned.1.call-start = ((), (), s32[]{:S(2)}) async-start(), calls=%async_computation.8 | async-start | bytes 5160960 | tf_op jit(solution)/shard_map/gather_mid_tail/all_gather | solution.py:96
  8.8 13.4 %copy-start.22 = (bf16[144]{0:T(256)(128)(2,1)}, bf16[144]{0:T(256)(128)(2,1)S(1)}, u32[]{:S(2)}) copy-start(bf16[144]{0:T(256)(128)(2,1)S(1)} %pad.5.clone) | copy-start | bytes 868
  9.8 9.1 %collective-permute-start.11 = (bf16[144,896]{1,0:T(8,128)(2,1)S(1)}, bf16[144,896]{1,0:T(8,128)(2,1)S(1)}, u32[]{:S(2)}, u32[]{:S(2)}) collective-permute-start(bf16[144,896]{1,0:T(8,128)(2,1)S(1)} %maximum_maximum_fusion.1.refs_0_), channel_id=1, source_target_pairs={{0,96},{16,112},{32,64},{48,80},{64,32},{80,48},{96,0},{112,16},{1... | collective-permute-start | bytes 774152 | tf_op jit(solution)/shard_map/gather_proj/ppermute | solution.py:21
  12.8 7.7 %collective-permute-start.9 = (bf16[144,896]{1,0:T(8,128)(2,1)S(1)}, bf16[144,896]{1,0:T(8,128)(2,1)S(1)}, u32[]{:S(2)}, u32[]{:S(2)}) collective-permute-start(bf16[144,896]{1,0:T(8,128)(2,1)S(1)} %maximum_maximum_fusion.1.refs_0_), channel_id=1, source_target_pairs={{0,32},{16,48},{32,0},{48,16},{64,96},{80,112},{96,64},{112,80},{1... | collective-permute-start | bytes 774152 | tf_op jit(solution)/shard_map/gather_proj/ppermute | solution.py:21
  19.0 4.9 %collective-permute-start.12 = (bf16[64,896]{1,0:T(8,128)(2,1)S(1)}, bf16[64,896]{1,0:T(8,128)(2,1)S(1)}, u32[]{:S(2)}, u32[]{:S(2)}) collective-permute-start(bf16[64,896]{1,0:T(8,128)(2,1)S(1)} %slice.76), channel_id=1, source_target_pairs={{0,32},{16,48},{32,0},{48,16},{64,96},{80,112},{96,64},{112,80},{1... | collective-permute-start | bytes 344072 | tf_op jit(solution)/shard_map/gather_proj/ppermute | solution.py:21
  20.5 8.9 %collective-permute-start.13 = (bf16[80,896]{1,0:T(8,128)(2,1)S(1)}, bf16[80,896]{1,0:T(8,128)(2,1)S(1)}, u32[]{:S(2)}, u32[]{:S(2)}) collective-permute-start(bf16[80,896]{1,0:T(8,128)(2,1)S(1)} %slice.77), channel_id=1, source_target_pairs={{0,96},{16,112},{32,64},{48,80},{64,32},{80,48},{96,0},{112,16},{1... | collective-permute-start | bytes 430088 | tf_op jit(solution)/shard_map/gather_proj/ppermute | solution.py:21
  22.1 12.5 %collective-permute-start.8 = (bf16[144,896]{1,0:T(8,128)(2,1)S(1)}, bf16[144,896]{1,0:T(8,128)(2,1)S(1)}, u32[]{:S(2)}, u32[]{:S(2)}) collective-permute-start(bf16[144,896]{1,0:T(8,128)(2,1)S(1)} %maximum_maximum_fusion.1.refs_0_), channel_id=1, source_target_pairs={{0,16},{16,0},{32,48},{48,32},{64,80},{80,64},{96,112},{112,96},{1... | collective-permute-start | bytes 774152 | tf_op jit(solution)/shard_map/gather_proj/ppermute | solution.py:21
  22.1 12.5 %collective-permute-start.15 = (bf16[144,896]{1,0:T(8,128)(2,1)S(1)}, bf16[144,896]{1,0:T(8,128)(2,1)S(1)}, u32[]{:S(2)}, u32[]{:S(2)}) collective-permute-start(bf16[144,896]{1,0:T(8,128)(2,1)S(1)} %collective-permute-done.11.refs_6_), channel_id=1, source_target_pairs={{0,16},{16,0},{32,48},{48,32},{64,80},{80,64},{96,112},{112,96},{1... | collective-permute-start | bytes 774152 | tf_op jit(solution)/shard_map/gather_proj/ppermute | solution.py:21
  22.7 12.0 %collective-permute-start.10 = (bf16[144,896]{1,0:T(8,128)(2,1)S(1)}, bf16[144,896]{1,0:T(8,128)(2,1)S(1)}, u32[]{:S(2)}, u32[]{:S(2)}) collective-permute-start(bf16[144,896]{1,0:T(8,128)(2,1)S(1)} %collective-permute-done.9.refs_2_), channel_id=1, source_target_pairs={{0,16},{16,0},{32,48},{48,32},{64,80},{80,64},{96,112},{112,96},{1... | collective-permute-start | bytes 774152 | tf_op jit(solution)/shard_map/gather_proj/ppermute | solution.py:21
  29.4 5.3 %collective-permute-start.14 = (bf16[144,896]{1,0:T(8,128)(2,1)S(1)}, bf16[144,896]{1,0:T(8,128)(2,1)S(1)}, u32[]{:S(2)}, u32[]{:S(2)}) collective-permute-start(bf16[144,896]{1,0:T(8,128)(2,1)S(1)} %constant_dynamic-update-slice_fusion.2.refs_4_), channel_id=1, source_target_pairs={{0,16},{16,0},{32,48},{48,32},{64,80},{80,64},{96,112},{112,96},{1... | collective-permute-start | bytes 774152 | tf_op jit(solution)/shard_map/gather_proj/ppermute | solution.py:21
  31.2 10.5 %all-to-all-start.1 = ((bf16[8,16,896]{2,1,0:T(8,128)(2,1)}), bf16[8,16,896]{2,1,0:T(8,128)(2,1)S(1)}, u32[]{:S(2)}, u32[]{:S(2)}) async-start(bf16[8,16,896]{2,1,0:T(8,128)(2,1)} %copy.41), calls=%async_computation.1 | async-start | bytes 458752 | tf_op jit(solution)/shard_map/spread_hidden/all_to_all | solution.py:110
  34.7 2.8 %copy-start.16 = (bf16[256,7168]{1,0:T(8,128)(2,1)S(1)}, bf16[256,7168]{1,0:T(8,128)(2,1)}, u32[]{:S(2)}) copy-start(bf16[256,7168]{1,0:T(8,128)(2,1)} %param.11) | copy-start | bytes 11010052
  42.9 28.0 %all-to-all-start = ((bf16[16,144,256]{2,1,0:T(8,128)(2,1)}), bf16[16,144,256]{2,1,0:T(8,128)(2,1)S(1)}, u32[]{:S(2)}, u32[]{:S(2)}) async-start(bf16[16,144,256]{2,1,0:T(8,128)(2,1)} %broadcast_in_dim.43), calls=%async_computation | async-start | bytes 2359296 | tf_op jit(solution)/shard_map/spread_codes/all_to_all | solution.py:65
  52.0 40.5 %collective-permute-start.3 = (bf16[896,512]{1,0:T(8,128)(2,1)}, bf16[896,512]{1,0:T(8,128)(2,1)S(1)}, u32[]{:S(2)}, u32[]{:S(2)}) collective-permute-start(bf16[896,512]{1,0:T(8,128)(2,1)} %refs_0_.1), channel_id=1, source_target_pairs={{0,96},{16,112},{32,64},{48,80},{64,32},{80,48},{96,0},{112,16},{1... | collective-permute-start | bytes 2752520 | tf_op jit(solution)/shard_map/gather_head/ppermute | solution.py:21
  53.2 39.6 %collective-permute-start.1 = (bf16[896,512]{1,0:T(8,128)(2,1)}, bf16[896,512]{1,0:T(8,128)(2,1)S(1)}, u32[]{:S(2)}, u32[]{:S(2)}) collective-permute-start(bf16[896,512]{1,0:T(8,128)(2,1)} %refs_0_.1), channel_id=1, source_target_pairs={{0,32},{16,48},{32,0},{48,16},{64,96},{80,112},{96,64},{112,80},{1... | collective-permute-start | bytes 2752520 | tf_op jit(solution)/shard_map/gather_head/ppermute | solution.py:21
  70.9 2.2 copy-start.13
  73.1 53.3 %all-to-all-start.2 = ((bf16[16,8,16,896]{3,2,1,0:T(8,128)(2,1)}), bf16[16,8,16,896]{3,2,1,0:T(8,128)(2,1)}, u32[]{:S(2)}, u32[]{:S(2)}) async-start(bf16[16,8,16,896]{3,2,1,0:T(8,128)(2,1)} %broadcast_in_dim.53), calls=%async_computation.2 | async-start | bytes 7340032 | tf_op jit(solution)/shard_map/spread_hidden/all_to_all | solution.py:65
  77.6 28.6 %copy-start.21 = (s32[256]{0:T(256)S(1)}, s32[256]{0:T(256)}, u32[]{:S(2)}) copy-start(s32[256]{0:T(256)} %param.20) | copy-start | bytes 3076
  77.6 28.6 %copy-start.18 = (bf16[256,512]{1,0:T(8,128)(2,1)S(1)}, bf16[256,512]{1,0:T(8,128)(2,1)}, u32[]{:S(2)}) copy-start(bf16[256,512]{1,0:T(8,128)(2,1)} %param.17) | copy-start | bytes 786436
  77.6 184.4 %reduce-scatter.5.cloned.1.call-start = ((), (), s32[]{:S(2)}) async-start(), calls=%async_computation.11 | async-start | bytes 2322432 | tf_op jit(solution)/shard_map/mid_tail_grads/reduce_scatter | solution.py:183
  92.5 12.0 %collective-permute-start.4 = (bf16[448,512]{1,0:T(8,128)(2,1)S(1)}, bf16[448,512]{1,0:T(8,128)(2,1)S(1)}, u32[]{:S(2)}, u32[]{:S(2)}) collective-permute-start(bf16[448,512]{1,0:T(8,128)(2,1)S(1)} %slice.74), channel_id=1, source_target_pairs={{0,32},{16,48},{32,0},{48,16},{64,96},{80,112},{96,64},{112,80},{1... | collective-permute-start | bytes 1376264 | tf_op jit(solution)/shard_map/gather_head/ppermute | solution.py:21
  92.9 13.0 %collective-permute-start.5 = (bf16[448,512]{1,0:T(8,128)(2,1)S(1)}, bf16[448,512]{1,0:T(8,128)(2,1)S(1)}, u32[]{:S(2)}, u32[]{:S(2)}) collective-permute-start(bf16[448,512]{1,0:T(8,128)(2,1)S(1)} %slice.75), channel_id=1, source_target_pairs={{0,96},{16,112},{32,64},{48,80},{64,32},{80,48},{96,0},{112,16},{1... | collective-permute-start | bytes 1376264 | tf_op jit(solution)/shard_map/gather_head/ppermute | solution.py:21
  94.1 19.6 %collective-permute-start = (bf16[896,512]{1,0:T(8,128)(2,1)}, bf16[896,512]{1,0:T(8,128)(2,1)}, u32[]{:S(2)}, u32[]{:S(2)}) collective-permute-start(bf16[896,512]{1,0:T(8,128)(2,1)} %refs_0_.1), channel_id=1, source_target_pairs={{0,16},{16,0},{32,48},{48,32},{64,80},{80,64},{96,112},{112,96},{1... | collective-permute-start | bytes 2752520 | tf_op jit(solution)/shard_map/gather_head/ppermute | solution.py:21
  94.1 19.6 %collective-permute-start.2 = (bf16[896,512]{1,0:T(8,128)(2,1)S(1)}, bf16[896,512]{1,0:T(8,128)(2,1)}, u32[]{:S(2)}, u32[]{:S(2)}) collective-permute-start(bf16[896,512]{1,0:T(8,128)(2,1)S(1)} %collective-permute-done.1.refs_2_), channel_id=1, source_target_pairs={{0,16},{16,0},{32,48},{48,32},{64,80},{80,64},{96,112},{112,96},{1... | collective-permute-start | bytes 2752520 | tf_op jit(solution)/shard_map/gather_head/ppermute | solution.py:21
  94.6 19.1 %collective-permute-start.7 = (bf16[896,512]{1,0:T(8,128)(2,1)S(1)}, bf16[896,512]{1,0:T(8,128)(2,1)}, u32[]{:S(2)}, u32[]{:S(2)}) collective-permute-start(bf16[896,512]{1,0:T(8,128)(2,1)S(1)} %collective-permute-done.3.refs_6_), channel_id=1, source_target_pairs={{0,16},{16,0},{32,48},{48,32},{64,80},{80,64},{96,112},{112,96},{1... | collective-permute-start | bytes 2752520 | tf_op jit(solution)/shard_map/gather_head/ppermute | solution.py:21
  105.9 5.6 %slice-start.2 = ((bf16[16,144,256]{2,1,0:T(8,128)(2,1)}), bf16[16,28,256]{2,1,0:T(8,128)(2,1)S(1)}, s32[]{:S(2)}) async-start(bf16[16,144,256]{2,1,0:T(8,128)(2,1)} %copy-done.13), calls=%async_computation.14 | async-start | bytes 524288 | tf_op jit(solution)/shard_map/spread_codes/slice | solution.py:103
  105.9 7.8 %collective-permute-start.6 = (bf16[896,512]{1,0:T(8,128)(2,1)S(1)}, bf16[896,512]{1,0:T(8,128)(2,1)}, u32[]{:S(2)}, u32[]{:S(2)}) collective-permute-start(bf16[896,512]{1,0:T(8,128)(2,1)S(1)} %constant_dynamic-update-slice_fusion.refs_4_), channel_id=1, source_target_pairs={{0,16},{16,0},{32,48},{48,32},{64,80},{80,64},{96,112},{112,96},{1... | collective-permute-start | bytes 2752520 | tf_op jit(solution)/shard_map/gather_head/ppermute | solution.py:21
  106.9 4.6 %copy-start.24 = (bf16[256]{0:T(256)(128)(2,1)S(1)}, bf16[256]{0:T(256)(128)(2,1)}, u32[]{:S(2)}) copy-start(bf16[256]{0:T(256)(128)(2,1)} %reduce_max.165) | copy-start | bytes 1540
  113.7 4.3 %copy-start.17 = (bf16[256,7168]{1,0:T(8,128)(2,1)S(1)}, bf16[256,7168]{1,0:T(8,128)(2,1)}, u32[]{:S(2)}) copy-start(bf16[256,7168]{1,0:T(8,128)(2,1)} %param.11) | copy-start | bytes 11010052
  118.1 2.9 %copy-start.2 = (bf16[7168,512]{1,0:T(8,128)(2,1)}, bf16[7168,512]{1,0:T(8,128)(2,1)S(1)}, u32[]{:S(2)}) copy-start(bf16[7168,512]{1,0:T(8,128)(2,1)S(1)} %gather_head.1) | copy-start | bytes 22020100
  124.5 6.0 %copy-start.6 = (bf16[16,112,256]{2,1,0:T(8,128)(2,1)S(1)}, bf16[16,112,256]{2,1,0:T(8,128)(2,1)}, u32[]{:S(2)}) copy-start(bf16[16,112,256]{2,1,0:T(8,128)(2,1)} %slice.78) | copy-start | bytes 2752516
  130.5 3.9 %copy-start.5 = (bf16[256,2304]{1,0:T(8,128)(2,1)S(1)}, bf16[256,2304]{1,0:T(8,128)(2,1)}, u32[]{:S(2)}) copy-start(bf16[256,2304]{1,0:T(8,128)(2,1)} %param.19) | copy-start | bytes 3538948
  134.4 2.4 copy-start.9
  134.4 2.4 copy-start.11
  134.4 2.4 copy-start.19
  158.4 103.6 %reduce-scatter.3.cloned.1.call-start = ((), (), s32[]{:S(2)}) async-start(), calls=%async_computation.10 | async-start | bytes 5160960 | tf_op jit(solution)/shard_map/mid_tail_grads/reduce_scatter | solution.py:180
  163.7 6.7 %copy-start.15 = (bf16[256,2304]{1,0:T(8,128)(2,1)S(1)}, bf16[256,2304]{1,0:T(8,128)(2,1)}, u32[]{:S(2)}) copy-start(bf16[256,2304]{1,0:T(8,128)(2,1)} %copy-done.14) | copy-start | bytes 3538948
  170.4 2.4 copy-start.23
  172.8 6.0 %copy-start.12 = (f32[512,256]{0,1:T(8,128)S(1)}, f32[512,256]{0,1:T(8,128)}, u32[]{:S(2)}) copy-start(f32[512,256]{0,1:T(8,128)} %copy.40) | copy-start | bytes 1572868
  172.8 6.0 %copy-start.20 = (bf16[256,512]{1,0:T(8,128)(2,1)S(1)}, bf16[256,512]{1,0:T(8,128)(2,1)}, u32[]{:S(2)}) copy-start(bf16[256,512]{1,0:T(8,128)(2,1)} %param.17) | copy-start | bytes 786436
  174.4 23.2 %all-to-all-start.4 = ((bf16[16,144,256]{2,1,0:T(8,128)(2,1)}), bf16[16,144,256]{2,1,0:T(8,128)(2,1)}, u32[]{:S(2)}, u32[]{:S(2)}) async-start(bf16[16,144,256]{2,1,0:T(8,128)(2,1)} %maximum_maximum_fusion), calls=%async_computation.4 | async-start | bytes 2359296 | tf_op jit(solution)/shard_map/code_grads/all_to_all | solution.py:177
  197.6 4.5 %slice-start = ((s8[7340032]{0:T(1024)(128)(4,1)}), s8[3145728]{0:T(1024)(128)(4,1)S(1)}, s32[]{:S(2)}) async-start(s8[7340032]{0:T(1024)(128)(4,1)} %bitcast.93), calls=%async_computation.12 | async-start | bytes 6291456
  199.2 3.3 %slice-start.1 = ((s8[7340032]{0:T(1024)(128)(4,1)}), s8[4194304]{0:T(1024)(128)(4,1)S(1)}, s32[]{:S(2)}) async-start(s8[7340032]{0:T(1024)(128)(4,1)} %bitcast.93), calls=%async_computation.13 | async-start | bytes 8388608
  206.7 52.1 %all-to-all-start.5 = ((bf16[16,448,256]{2,1,0:T(8,128)(2,1)}), bf16[16,448,256]{2,1,0:T(8,128)(2,1)}, u32[]{:S(2)}, u32[]{:S(2)}) async-start(bf16[16,448,256]{2,1,0:T(8,128)(2,1)} %bitcast.95), calls=%async_computation.7 | async-start | bytes 7340032 | tf_op jit(solution)/shard_map/hidden_grad/all_to_all | solution.py:189
  211.2 11.3 %collective-permute-start.19 = (bf16[256,512]{1,0:T(8,128)(2,1)S(1)}, bf16[256,512]{1,0:T(8,128)(2,1)S(1)}, u32[]{:S(2)}, u32[]{:S(2)}) collective-permute-start(bf16[256,512]{1,0:T(8,128)(2,1)S(1)} %fusion.23.refs_0_), channel_id=1, source_target_pairs={{0,96},{16,112},{32,64},{48,80},{64,32},{80,48},{96,0},{112,16},{1... | collective-permute-start | bytes 786440 | tf_op jit(solution)/shard_map/head_proj_grads/ppermute | solution.py:21
  212.0 10.7 %collective-permute-start.17 = (bf16[256,512]{1,0:T(8,128)(2,1)S(1)}, bf16[256,512]{1,0:T(8,128)(2,1)S(1)}, u32[]{:S(2)}, u32[]{:S(2)}) collective-permute-start(bf16[256,512]{1,0:T(8,128)(2,1)S(1)} %fusion.23.refs_0_), channel_id=1, source_target_pairs={{0,32},{16,48},{32,0},{48,16},{64,96},{80,112},{96,64},{112,80},{1... | collective-permute-start | bytes 786440 | tf_op jit(solution)/shard_map/head_proj_grads/ppermute | solution.py:21
  222.6 6.5 %collective-permute-start.20 = (bf16[128,512]{1,0:T(8,128)(2,1)S(1)}, bf16[128,512]{1,0:T(8,128)(2,1)S(1)}, u32[]{:S(2)}, u32[]{:S(2)}) collective-permute-start(bf16[128,512]{1,0:T(8,128)(2,1)S(1)} %slice.84), channel_id=1, source_target_pairs={{0,32},{16,48},{32,0},{48,16},{64,96},{80,112},{96,64},{112,80},{1... | collective-permute-start | bytes 393224 | tf_op jit(solution)/shard_map/head_proj_grads/ppermute | solution.py:21
  222.7 7.7 %collective-permute-start.21 = (bf16[128,512]{1,0:T(8,128)(2,1)S(1)}, bf16[128,512]{1,0:T(8,128)(2,1)S(1)}, u32[]{:S(2)}, u32[]{:S(2)}) collective-permute-start(bf16[128,512]{1,0:T(8,128)(2,1)S(1)} %slice.85), channel_id=1, source_target_pairs={{0,96},{16,112},{32,64},{48,80},{64,32},{80,48},{96,0},{112,16},{1... | collective-permute-start | bytes 393224 | tf_op jit(solution)/shard_map/head_proj_grads/ppermute | solution.py:21
  225.5 11.9 %collective-permute-start.16 = (bf16[256,512]{1,0:T(8,128)(2,1)S(1)}, bf16[256,512]{1,0:T(8,128)(2,1)S(1)}, u32[]{:S(2)}, u32[]{:S(2)}) collective-permute-start(bf16[256,512]{1,0:T(8,128)(2,1)S(1)} %fusion.23.refs_0_), channel_id=1, source_target_pairs={{0,16},{16,0},{32,48},{48,32},{64,80},{80,64},{96,112},{112,96},{1... | collective-permute-start | bytes 786440 | tf_op jit(solution)/shard_map/head_proj_grads/ppermute | solution.py:21
  225.5 14.0 %collective-permute-start.23 = (bf16[256,512]{1,0:T(8,128)(2,1)S(1)}, bf16[256,512]{1,0:T(8,128)(2,1)S(1)}, u32[]{:S(2)}, u32[]{:S(2)}) collective-permute-start(bf16[256,512]{1,0:T(8,128)(2,1)S(1)} %collective-permute-done.19.refs_6_), channel_id=1, source_target_pairs={{0,16},{16,0},{32,48},{48,32},{64,80},{80,64},{96,112},{112,96},{1... | collective-permute-start | bytes 786440 | tf_op jit(solution)/shard_map/head_proj_grads/ppermute | solution.py:21
  226.0 13.5 %collective-permute-start.18 = (bf16[256,512]{1,0:T(8,128)(2,1)S(1)}, bf16[256,512]{1,0:T(8,128)(2,1)S(1)}, u32[]{:S(2)}, u32[]{:S(2)}) collective-permute-start(bf16[256,512]{1,0:T(8,128)(2,1)S(1)} %collective-permute-done.17.refs_2_), channel_id=1, source_target_pairs={{0,16},{16,0},{32,48},{48,32},{64,80},{80,64},{96,112},{112,96},{1... | collective-permute-start | bytes 786440 | tf_op jit(solution)/shard_map/head_proj_grads/ppermute | solution.py:21
  230.4 9.1 %collective-permute-start.22 = (bf16[256,512]{1,0:T(8,128)(2,1)S(1)}, bf16[256,512]{1,0:T(8,128)(2,1)S(1)}, u32[]{:S(2)}, u32[]{:S(2)}) collective-permute-start(bf16[256,512]{1,0:T(8,128)(2,1)S(1)} %constant_dynamic-update-slice_fusion.4.refs_4_), channel_id=1, source_target_pairs={{0,16},{16,0},{32,48},{48,32},{64,80},{80,64},{96,112},{112,96},{1... | collective-permute-start | bytes 786440 | tf_op jit(solution)/shard_map/head_proj_grads/ppermute | solution.py:21
  230.5 6.9 %collective-permute-start.27 = (bf16[144,256]{1,0:T(8,128)(2,1)S(1)}, bf16[144,256]{1,0:T(8,128)(2,1)S(1)}, u32[]{:S(2)}, u32[]{:S(2)}) collective-permute-start(bf16[144,256]{1,0:T(8,128)(2,1)S(1)} %reduce_sum.182.refs_0_), channel_id=1, source_target_pairs={{0,96},{16,112},{32,64},{48,80},{64,32},{80,48},{96,0},{112,16},{1... | collective-permute-start | bytes 221192 | tf_op jit(solution)/shard_map/head_proj_grads/ppermute | solution.py:21
  237.4 4.4 %collective-permute-start.25 = (bf16[144,256]{1,0:T(8,128)(2,1)S(1)}, bf16[144,256]{1,0:T(8,128)(2,1)S(1)}, u32[]{:S(2)}, u32[]{:S(2)}) collective-permute-start(bf16[144,256]{1,0:T(8,128)(2,1)S(1)} %reduce_sum.182.refs_0_), channel_id=1, source_target_pairs={{0,32},{16,48},{32,0},{48,16},{64,96},{80,112},{96,64},{112,80},{1... | collective-permute-start | bytes 221192 | tf_op jit(solution)/shard_map/head_proj_grads/ppermute | solution.py:21
  237.4 9.6 %copy-start.4 = (bf16[16,8,16,896]{3,2,0,1:T(8,128)(2,1)S(1)}, bf16[16,8,16,896]{3,2,0,1:T(8,128)(2,1)}, u32[]{:S(2)}) copy-start(bf16[16,8,16,896]{3,2,0,1:T(8,128)(2,1)} %copy.42) | copy-start | bytes 11010052
  237.4 7.2 %collective-permute-start.28 = (bf16[64,256]{1,0:T(8,128)(2,1)S(1)}, bf16[64,256]{1,0:T(8,128)(2,1)S(1)}, u32[]{:S(2)}, u32[]{:S(2)}) collective-permute-start(bf16[64,256]{1,0:T(8,128)(2,1)S(1)} %slice.86), channel_id=1, source_target_pairs={{0,32},{16,48},{32,0},{48,16},{64,96},{80,112},{96,64},{112,80},{1... | collective-permute-start | bytes 98312 | tf_op jit(solution)/shard_map/head_proj_grads/ppermute | solution.py:21
  239.8 10.2 %collective-permute-start.24 = (bf16[144,256]{1,0:T(8,128)(2,1)S(1)}, bf16[144,256]{1,0:T(8,128)(2,1)S(1)}, u32[]{:S(2)}, u32[]{:S(2)}) collective-permute-start(bf16[144,256]{1,0:T(8,128)(2,1)S(1)} %reduce_sum.182.refs_0_), channel_id=1, source_target_pairs={{0,16},{16,0},{32,48},{48,32},{64,80},{80,64},{96,112},{112,96},{1... | collective-permute-start | bytes 221192 | tf_op jit(solution)/shard_map/head_proj_grads/ppermute | solution.py:21
  241.8 5.2 %collective-permute-start.29 = (bf16[80,256]{1,0:T(8,128)(2,1)S(1)}, bf16[80,256]{1,0:T(8,128)(2,1)S(1)}, u32[]{:S(2)}, u32[]{:S(2)}) collective-permute-start(bf16[80,256]{1,0:T(8,128)(2,1)S(1)} %slice.87), channel_id=1, source_target_pairs={{0,96},{16,112},{32,64},{48,80},{64,32},{80,48},{96,0},{112,16},{1... | collective-permute-start | bytes 122888 | tf_op jit(solution)/shard_map/head_proj_grads/ppermute | solution.py:21
  244.1 5.9 %collective-permute-start.31 = (bf16[144,256]{1,0:T(8,128)(2,1)S(1)}, bf16[144,256]{1,0:T(8,128)(2,1)S(1)}, u32[]{:S(2)}, u32[]{:S(2)}) collective-permute-start(bf16[144,256]{1,0:T(8,128)(2,1)S(1)} %collective-permute-done.27.refs_6_), channel_id=1, source_target_pairs={{0,16},{16,0},{32,48},{48,32},{64,80},{80,64},{96,112},{112,96},{1... | collective-permute-start | bytes 221192 | tf_op jit(solution)/shard_map/head_proj_grads/ppermute | solution.py:21
  244.1 5.9 %collective-permute-start.26 = (bf16[144,256]{1,0:T(8,128)(2,1)S(1)}, bf16[144,256]{1,0:T(8,128)(2,1)S(1)}, u32[]{:S(2)}, u32[]{:S(2)}) collective-permute-start(bf16[144,256]{1,0:T(8,128)(2,1)S(1)} %collective-permute-done.25.refs_2_), channel_id=1, source_target_pairs={{0,16},{16,0},{32,48},{48,32},{64,80},{80,64},{96,112},{112,96},{1... | collective-permute-start | bytes 221192 | tf_op jit(solution)/shard_map/head_proj_grads/ppermute | solution.py:21
  247.0 3.0 %collective-permute-start.30 = (bf16[144,256]{1,0:T(8,128)(2,1)S(1)}, bf16[144,256]{1,0:T(8,128)(2,1)S(1)}, u32[]{:S(2)}, u32[]{:S(2)}) collective-permute-start(bf16[144,256]{1,0:T(8,128)(2,1)S(1)} %constant_dynamic-update-slice_fusion.6.refs_4_), channel_id=1, source_target_pairs={{0,16},{16,0},{32,48},{48,32},{64,80},{80,64},{96,112},{112,96},{1... | collective-permute-start | bytes 221192 | tf_op jit(solution)/shard_map/head_proj_grads/ppermute | solution.py:21
  251.0 11.0 %copy-start.1 = (s32[65536]{0:T(1024)S(1)}, s32[65536]{0:T(1024)}, u32[]{:S(2)}) copy-start(s32[65536]{0:T(1024)} %param.21) | copy-start | bytes 786436
  (5 other events, 6.6 us)
Sparse Core Ops, SparseCore 0:
  9.7 28.2 all-gather.4
  39.7 52.1 all-gather.2
  158.5 32.0 reduce-scatter.4
  193.5 46.0 reduce-scatter.2
where the time goes:
time: 270 us; the launch traced here: 269 us
  waiting for transfers between devices  112 us (41%)
  starting transfers between devices  47.9 us (18%)
  matrix products  34.1 us (13%)
  local copies, waits for them, and re-layouts  24 us (9%)
  other arithmetic  18.3 us (7%)
  between operations  14.5 us (5%)
  blocking collectives  12.9 us (5%)
  Pallas kernels  5.09 us (2%)
    ppermute x32, waiting for transfers between devices, swap(): lax.ppermute(block, 'dp', [(i, i ^ flip) for i in range(lax.axis_size('dp...  63 us
    dot_general x12, matrix products, dot(): lax.dot_general(left, right, (((left_dim,), (right_dim,)), ((), ())), pre...  34.1 us
    ppermute x32, starting transfers between devices, swap(): lax.ppermute(block, 'dp', [(i, i ^ flip) for i in range(lax.axis_size('dp...  21.5 us
    all_to_all x2, waiting for transfers between devices, spread_vocab(): lax.all_to_all(jnp.broadcast_to(block[None], (size,) + block.shape), 'voc...  19.5 us
    all_to_all x1, waiting for transfers between devices, per_device(): dz = lax.all_to_all(dz, 'vocab', 0, 0)  18.5 us
    all_to_all x2, starting transfers between devices, spread_vocab(): lax.all_to_all(jnp.broadcast_to(block[None], (size,) + block.shape), 'voc...  13.6 us
    all_to_all x1, blocking collectives, spread_vocab(): lax.all_to_all(jnp.broadcast_to(block[None], (size,) + block.shape), 'voc...  12.9 us
    all_to_all x1, waiting for transfers between devices, per_device(): term = lax.all_to_all(term, 'vocab', 0, 0)  6.4 us
  transfers between devices with their start and end apart: 41, of which 18 were waited for; matrix products, arithmetic and copies ran while one was open for 21% of the time, Pallas kernels for 2%

commit v1 on v0

--- a/solution.py
+++ b/solution.py
@@ -17,25 +17,36 @@
     )
 
 
-def swap(block, flip):
-    return lax.ppermute(block, "dp", [(i, i ^ flip) for i in range(lax.axis_size("dp"))])
-
-
-def place_kernel(axis, me_ref, *refs):
+def swap(block, axis_name, flip):
+    pairs = [(i, i ^ flip) for i in range(lax.axis_size(axis_name))]
+    return lax.ppermute(block, axis_name, pairs)
+
+
+def ring_near(block, axis_name, step):
+    return swap(block, axis_name, step), swap(block, axis_name, 3 * step)
+
+
+def ring_far(near, other, axis_name, step, half):
+    return jnp.concatenate(
+        [swap(other[:half], axis_name, step), swap(near[half:], axis_name, 3 * step)], axis=0
+    )
+
+
+def place_kernel(axis, spots_ref, *refs):
     blocks, out, sems = refs[:-2], refs[-2], refs[-1]
     copies = []
-    for flip, block in enumerate(blocks):
+    for k, block in enumerate(blocks):
         size = block.shape[axis]
-        start = pl.multiple_of((me_ref[0] ^ flip) * size, size)
-        spot = out.at[pl.ds(start, size)] if axis == 0 else out.at[:, pl.ds(start, size)]
-        copies.append(pltpu.make_async_copy(block, spot, sems.at[flip]))
+        start = pl.multiple_of(spots_ref[k] * size, size)
+        spot = out.at[(slice(None),) * axis + (pl.ds(start, size),)]
+        copies.append(pltpu.make_async_copy(block, spot, sems.at[k]))
     for copy in copies:
         copy.start()
     for copy in copies:
         copy.wait()
 
 
-def place(blocks, axis):
+def place(blocks, spots, axis):
     shape = list(blocks[0].shape)
     shape[axis] *= len(blocks)
     moved = 2 * len(blocks) * blocks[0].size * blocks[0].dtype.itemsize
@@ -48,16 +59,62 @@
         scratch_shapes=[pltpu.SemaphoreType.DMA((len(blocks),))],
         compiler_params=pltpu.CompilerParams(vmem_limit_bytes=16 << 20),
         cost_estimate=pl.CostEstimate(flops=0, bytes_accessed=moved, transcendentals=0),
-    )(lax.axis_index("dp").astype(jnp.int32).reshape(1), *blocks)
+    )(jnp.stack(spots).astype(jnp.int32), *blocks)
+
+
+def half_rows(block):
+    return block.shape[0] // 32 * 16
+
+
+def both_cores(parts, axis):
+    blocks = [p for part in parts for p in (part, swap(part, "dp", 1))]
+    me = lax.axis_index("dp")
+    return place(blocks, [me ^ flip for flip in range(len(blocks))], axis)
 
 
 def gather_dp(block, axis):
-    half = block.shape[0] // 32 * 16
-    near = swap(block, 2)
-    other = swap(block, 6)
-    far = jnp.concatenate([swap(other[:half], 2), swap(near[half:], 6)], axis=0)
-    parts = [block, near, far, other]
-    return place([p for part in parts for p in (part, swap(part, 1))], axis)
+    near, other = ring_near(block, "dp", 2)
+    far = ring_far(near, other, "dp", 2, half_rows(block))
+    return both_cores([block, near, far, other], axis)
+
+
+def in_vmem(kernel, out_shape, *operands):
+    outs = out_shape if isinstance(out_shape, tuple) else (out_shape,)
+    size = sum(a.size * a.dtype.itemsize for a in operands + outs)
+    return pl.pallas_call(
+        kernel,
+        out_shape=out_shape,
+        compiler_params=pltpu.CompilerParams(vmem_limit_bytes=32 << 20),
+        cost_estimate=pl.CostEstimate(flops=2 * 10**9, bytes_accessed=size, transcendentals=0),
+    )(*operands)
+
+
+def columns(width_mid, width_tail, quarters):
+    spans = [(q * width_mid, width_mid) for q in range(quarters)]
+    return spans + [(quarters * width_mid, width_tail)]
+
+
+def logits_kernel(spans, z_ref, w_ref, mid_ref, tail_ref):
+    mid = None
+    for q, (start, size) in enumerate(spans):
+        part = dot(z_ref[q], w_ref[:, start : start + size], 0, 0)
+        if q == len(spans) - 1:
+            tail_ref[...] = part
+        else:
+            mid = part if mid is None else mid + part
+    mid_ref[...] = mid
+
+
+def code_grads_kernel(spans, w_ref, mid_ref, tail_ref, out_ref):
+    for q, (start, size) in enumerate(spans):
+        grad = tail_ref if q == len(spans) - 1 else mid_ref
+        out_ref[q] = dot(w_ref[:, start : start + size], grad[...], 1, 1).astype(BF16)
+
+
+def weight_grads_kernel(spans, z_ref, mid_ref, tail_ref, out_ref):
+    for q, (start, size) in enumerate(spans):
+        grad = tail_ref if q == len(spans) - 1 else mid_ref
+        out_ref[:, start : start + size] = dot(z_ref[q], grad[...], 1, 0).astype(BF16)
 
 
 def spread_vocab(block):
@@ -93,30 +150,53 @@
         )
         proj_full = gather_dp(proj_t, 1)
     with jax.named_scope("gather_mid_tail"):
-        mid_full = lax.all_gather(mid_weight, "dp", axis=0, tiled=True)
-        tail_full = lax.all_gather(tail_weight, "dp", axis=0, tiled=True)
-    with jax.named_scope("codes"):
-        codes = dot(proj_full, hidden, 1, 1).astype(BF16)
-    with jax.named_scope("spread_codes"):
-        codes_all = spread_vocab(codes)
-        z_mid = codes_all[:, :rank_mid].reshape(n_vocab * rank_mid, rows)
-        z_tail = codes_all[:, rank_mid:ranks].reshape(n_vocab * rank_tail, rows)
-    with jax.named_scope("gather_head"):
-        head_full = gather_dp(head_weight, 0)
+        depth_tail, quarters = tail_weight.shape[0], mid_weight.shape[0] // tail_weight.shape[0]
+        spans = columns(mid_weight.shape[1], tail_weight.shape[1], quarters)
+        packed_weight = jnp.concatenate(
+            [mid_weight[q * depth_tail : (q + 1) * depth_tail] for q in range(quarters)]
+            + [tail_weight],
+            axis=1,
+        )
+        packed_full = lax.all_gather(packed_weight, "dp", axis=0, tiled=True)
+    with jax.named_scope("gather_head_near"):
+        head_near, head_other = ring_near(head_weight, "dp", 2)
     with jax.named_scope("spread_hidden"):
         piece = rows // n_vocab
         mine = lax.dynamic_slice_in_dim(hidden, v * piece, piece, 0)
         mine = mine.reshape(piece, n_dp, depth).transpose(1, 0, 2)
         mine = lax.all_to_all(mine, "dp", 0, 0)
-        x_all = spread_vocab(mine)
-        x_all = x_all.transpose(1, 0, 2, 3).reshape(n_dp * rows, depth)
+        mine, packed_full = lax.optimization_barrier((mine, packed_full))
+        x_all = lax.all_gather(mine.reshape(n_dp * piece, depth), "vocab", axis=0)
+        x_all = x_all.reshape(n_vocab, n_dp, piece, depth).transpose(1, 0, 2, 3)
+        x_all = x_all.reshape(n_dp * rows, depth)
+    with jax.named_scope("codes"):
+        codes = dot(proj_full, hidden, 1, 1).astype(BF16)
+        codes, head_near, head_other = lax.optimization_barrier((codes, head_near, head_other))
+    with jax.named_scope("gather_head_far"):
+        head_far = ring_far(head_near, head_other, "dp", 2, half_rows(head_weight))
+    with jax.named_scope("spread_codes"):
+        codes_all = spread_vocab(codes)
+        by_dp = codes_all.reshape(n_dp, n_vocab // n_dp, ranks + pad, rows)
+        per = rank_mid // depth_tail
+        z = [
+            by_dp[:, q // per, (q % per) * depth_tail : (q % per + 1) * depth_tail]
+            for q in range(quarters)
+        ] + [by_dp[:, :, rank_mid:ranks].reshape(n_dp, depth_tail, rows)]
+        z = jnp.stack(z).reshape(quarters + 1, n_dp * depth_tail, rows)
+    with jax.named_scope("gather_head"):
+        head_full = both_cores([head_weight, head_near, head_far, head_other], 0)
 
     with jax.named_scope("logits"):
-        logits = (
-            dot(hidden, head_full, 1, 0),
-            dot(z_mid, mid_full, 0, 0),
-            dot(z_tail, tail_full, 0, 0),
-        )
+        mid_logits, tail_logits = in_vmem(
+            functools.partial(logits_kernel, spans),
+            (
+                jax.ShapeDtypeStruct((rows, mid_weight.shape[1]), F32),
+                jax.ShapeDtypeStruct((rows, tail_weight.shape[1]), F32),
+            ),
+            z,
+            packed_full,
+        )
+        logits = (dot(hidden, head_full, 1, 0), mid_logits, tail_logits)
     with jax.named_scope("statistics"):
         targets = (target_head.astype(F32), target_mid.astype(F32), target_tail.astype(F32))
         widths = (head_weight.shape[1], mid_weight.shape[1], tail_weight.shape[1])
@@ -143,7 +223,6 @@
         zero = jnp.zeros_like(picked)
         packed = jnp.stack([near_s, near_t, mass_s, mass_t, cross, picked, zero, zero])
     with jax.named_scope("spread_statistics"):
-        packed, x_all = lax.optimization_barrier((packed, x_all))
         packed = spread_vocab(packed)
         near_s, near_t, mass_s, mass_t, cross, picked = (packed[:, k] for k in range(6))
         top_s, top_t = jnp.max(near_s, axis=0), jnp.max(near_t, axis=0)
@@ -166,33 +245,48 @@
         )
 
     with jax.named_scope("code_grads"):
+        dz = in_vmem(
+            functools.partial(code_grads_kernel, spans),
+            jax.ShapeDtypeStruct(z.shape, BF16),
+            packed_full,
+            g_mid,
+            g_tail,
+        ).reshape(quarters + 1, n_dp, depth_tail, rows)
         dz = jnp.concatenate(
             [
-                dot(mid_full, g_mid, 1, 1).astype(BF16).reshape(n_vocab, rank_mid, rows),
-                dot(tail_full, g_tail, 1, 1).astype(BF16).reshape(n_vocab, rank_tail, rows),
+                dz[:quarters].transpose(1, 0, 2, 3).reshape(n_vocab, rank_mid, rows),
+                dz[quarters].reshape(n_vocab, rank_tail, rows),
                 jnp.zeros((n_vocab, pad, rows), BF16),
             ],
             axis=1,
         )
+        dz, g_mid = lax.optimization_barrier((dz, g_mid))
         dz = lax.all_to_all(dz, "vocab", 0, 0)
         dz = jnp.sum(dz.astype(F32), axis=0).astype(BF16)
     with jax.named_scope("mid_tail_grads"):
-        mid_grad = lax.psum_scatter(
-            dot(z_mid, g_mid, 1, 0).astype(BF16), "dp", scatter_dimension=0, tiled=True
-        )
-        tail_grad = lax.psum_scatter(
-            dot(z_tail, g_tail, 1, 0).astype(BF16), "dp", scatter_dimension=0, tiled=True
-        )
+        packed_grad = in_vmem(
+            functools.partial(weight_grads_kernel, spans),
+            jax.ShapeDtypeStruct(packed_full.shape, BF16),
+            z,
+            g_mid,
+            g_tail,
+        )
+        packed_grad = lax.psum_scatter(packed_grad, "dp", scatter_dimension=0, tiled=True)
+        pieces = [packed_grad[:, start : start + size] for start, size in spans]
+        mid_grad = jnp.concatenate(pieces[:quarters], axis=0)
+        tail_grad = pieces[quarters]
     with jax.named_scope("hidden_grad"):
         term = dot(head_full, g_head, 1, 1) + dot(proj_full, dz, 0, 0)
         term = term.astype(BF16).reshape(n_vocab, width // n_vocab, rows)
         term = lax.all_to_all(term, "vocab", 0, 0)
-        hidden_grad = jnp.sum(term.astype(F32), axis=0).astype(BF16).T
     with jax.named_scope("head_proj_grads"):
         g_all = gather_dp(g_head, 0)
         head_grad = dot(x_all, g_all, 0, 0).astype(BF16)
         dz_all = gather_dp(dz, 1)
         proj_grad = dot(x_all, dz_all, 0, 1).astype(BF16)
+    with jax.named_scope("hidden_grad_sum"):
+        term, head_grad, proj_grad = lax.optimization_barrier((term, head_grad, proj_grad))
+        hidden_grad = jnp.sum(term.astype(F32), axis=0).astype(BF16).T
     return (
         head_grad,
         proj_grad[:, :rank_mid],

time: 270 us -> 272 us (level)
  waiting for transfers between devices: 112 us -> 87.8 us
  local copies, waits for them, and re-layouts: 24 us -> 44.8 us
  matrix products: 34.1 us -> 22.6 us
  Pallas kernels: 5.09 us -> 13.6 us
  other arithmetic: 18.3 us -> 24.9 us
    all_to_all x2 -> x1, waiting for transfers between devices: 19.5 us -> 0.01 us  [spread_vocab(): lax.all_to_all(jnp.broadcast_to(block[None], (size,) + block.shape), 'voc...]
    unnamed x59 -> x95, local copies, waits for them, and re-layouts: 6.07 us -> 22.4 us
    dot_general x12 -> x6, matrix products: 34.1 us -> 22.6 us  [dot(): lax.dot_general(left, right, (((left_dim,), (right_dim,)), ((), ())), pre...]
    all_to_all x1, waiting for transfers between devices: 18.5 us -> 9.69 us  [per_device(): dz = lax.all_to_all(dz, 'vocab', 0, 0)]
    slice x11 -> x15, local copies, waits for them, and re-layouts: 2.28 us -> 9.24 us  [the longest x2 2.82 us: per_device(): pieces = [packed_grad[:, start:start + size] for start, size in spans]]
    pallas_call x0 -> x3, Pallas kernels: none -> 6 us  [in_vmem(): pl.pallas_call(kernel, out_shape=out_shape, compiler_params=pltpu.Compile...]
    ppermute x32, waiting for transfers between devices: 63 us -> 69 us  [swap(): return lax.ppermute(block, axis_name, pairs)]
    all_to_all x2 -> x1, starting transfers between devices: 13.6 us -> 8.11 us  [spread_vocab(): lax.all_to_all(jnp.broadcast_to(block[None], (size,) + block.shape), 'voc...]
  transfers between devices with their start and end apart: 41 -> 39, of which waited for: 18 -> 16; matrix products, arithmetic and copies ran while one was open for 21% -> 25% of each run, Pallas kernels for 2% -> 5%
where the time goes in v1:
time: 272 us; the launch traced here: 269 us
  waiting for transfers between devices  87.8 us (32%)
  starting transfers between devices  45.6 us (17%)
  local copies, waits for them, and re-layouts  44.8 us (16%)
  other arithmetic  24.9 us (9%)
  matrix products  22.6 us (8%)
  blocking collectives  14.8 us (5%)
  between operations  14.5 us (5%)
  Pallas kernels  13.6 us (5%)
    ppermute x32, waiting for transfers between devices, swap(): return lax.ppermute(block, axis_name, pairs)  69 us
    ppermute x32, starting transfers between devices, swap(): return lax.ppermute(block, axis_name, pairs)  24.3 us
    dot_general x6, matrix products, dot(): lax.dot_general(left, right, (((left_dim,), (right_dim,)), ((), ())), pre...  22.6 us
    unnamed x95, local copies, waits for them, and re-layouts  22.4 us
    all_to_all x1, blocking collectives, spread_vocab(): lax.all_to_all(jnp.broadcast_to(block[None], (size,) + block.shape), 'voc...  14.8 us
    all_to_all x1, waiting for transfers between devices, per_device(): dz = lax.all_to_all(dz, 'vocab', 0, 0)  9.69 us
    all_to_all x1, starting transfers between devices, spread_vocab(): lax.all_to_all(jnp.broadcast_to(block[None], (size,) + block.shape), 'voc...  8.11 us
    pallas_call x4, Pallas kernels, place(): pl.pallas_call(functools.partial(place_kernel, axis), out_shape=jax.Shape...  7.63 us
  transfers between devices with their start and end apart: 39, of which 16 were waited for; matrix products, arithmetic and copies ran while one was open for 25% of the time, Pallas kernels for 5%

profile of v1, /device:TPU:0, one launch (start us, length us, event | category | flops | bytes accessed | tf_op | source)
XLA Modules:
  0.0 268.7 jit_solution(14389555960540849339)
XLA Ops:
  13.1 2.9 %collective-permute-start.4 = (bf16[144,896]{1,0:T(8,128)(2,1)S(1)}, bf16[144,896]{1,0:T(8,128)(2,1)S(1)}, u32[]{:S(2)}, u32[]{:S(2)}) collective-permute-start(bf16[144,896]{1,0:T(8,128)(2,1)S(1)} %maximum_maximum_fusion.1.refs_0_), channel_id=1, source_target_pairs={{0,96},{16,112},{32,64},{48,80},{64,32},{80,48},{96,0},{112,16},{1... | collective-permute-start | bytes 774152 | tf_op jit(solution)/shard_map/gather_proj/ppermute | solution.py:22
  16.3 6.0 %collective-permute-done.4.refs_6_ = bf16[144,896]{1,0:T(8,128)(2,1)S(1)} collective-permute-done((bf16[144,896]{1,0:T(8,128)(2,1)S(1)}, bf16[144,896]{1,0:T(8,128)(2,1)S(1)}, u32[]{:S(2)}, u32[]{:S(2)}) %collective-permute-start.4) | collective-permute-done | bytes 258080 | tf_op jit(solution)/shard_map/gather_proj/ppermute | solution.py:22
  24.4 1.6 collective-permute-start.6
  26.0 1.4 collective-permute-start.9
  29.7 5.0 %collective-permute-done.6 = bf16[80,896]{1,0:T(8,128)(2,1)S(1)} collective-permute-done((bf16[80,896]{1,0:T(8,128)(2,1)}, bf16[80,896]{1,0:T(8,128)(2,1)S(1)}, u32[]{:S(2)}, u32[]{:S(2)}) %collective-permute-start.6) | collective-permute-done | bytes 143392 | tf_op jit(solution)/shard_map/gather_proj/ppermute | solution.py:22
  37.0 4.0 %all-to-all-start.1 = ((bf16[8,16,896]{2,1,0:T(8,128)(2,1)}), bf16[8,16,896]{2,1,0:T(8,128)(2,1)}, u32[]{:S(2)}, u32[]{:S(2)}) async-start(bf16[8,16,896]{2,1,0:T(8,128)(2,1)} %copy.53), calls=%async_computation.1 | async-start | bytes 458752 | tf_op jit(solution)/shard_map/spread_hidden/all_to_all | solution.py:167
  41.6 1.8 gather_proj.1
  43.5 1.4 convolution_convert_fusion.2
  44.9 23.8 %collective-permute-done.9.refs_2_ = bf16[896,512]{1,0:T(8,128)(2,1)S(1)} collective-permute-done((bf16[896,512]{1,0:T(8,128)(2,1)}, bf16[896,512]{1,0:T(8,128)(2,1)S(1)}, u32[]{:S(2)}, u32[]{:S(2)}) %collective-permute-start.9) | collective-permute-done | bytes 917536 | tf_op jit(solution)/shard_map/gather_head_near/ppermute | solution.py:22
  68.7 6.4 %collective-permute-done.10.refs_6_ = bf16[896,512]{1,0:T(8,128)(2,1)S(1)} collective-permute-done((bf16[896,512]{1,0:T(8,128)(2,1)}, bf16[896,512]{1,0:T(8,128)(2,1)S(1)}, u32[]{:S(2)}, u32[]{:S(2)}) %collective-permute-start.10) | collective-permute-done | bytes 917536 | tf_op jit(solution)/shard_map/gather_head_near/ppermute | solution.py:22
  75.1 1.9 all-to-all-done.1
  77.0 1.1 broadcast_in_dim.43
  78.1 8.1 %all-to-all-start = ((bf16[16,144,256]{2,1,0:T(8,128)(2,1)}), bf16[16,144,256]{2,1,0:T(8,128)(2,1)}, u32[]{:S(2)}, u32[]{:S(2)}) async-start(bf16[16,144,256]{2,1,0:T(8,128)(2,1)} %broadcast_in_dim.43), calls=%async_computation | async-start | bytes 2359296 | tf_op jit(solution)/shard_map/spread_codes/all_to_all | solution.py:122
  86.3 1.7 gather_fusion
  89.6 1.3 reduce_max.167
  91.9 3.2 %collective-permute-start.13 = (bf16[448,512]{1,0:T(8,128)(2,1)}, bf16[448,512]{1,0:T(8,128)(2,1)}, u32[]{:S(2)}, u32[]{:S(2)}) collective-permute-start(bf16[448,512]{1,0:T(8,128)(2,1)} %slice.103), channel_id=1, source_target_pairs={{0,96},{16,112},{32,64},{48,80},{64,32},{80,48},{96,0},{112,16},{1... | collective-permute-start | bytes 1376264 | tf_op jit(solution)/shard_map/gather_head_far/ppermute | solution.py:22
  96.9 3.5 %collective-permute-done.12 = bf16[448,512]{1,0:T(8,128)(2,1)} collective-permute-done((bf16[448,512]{1,0:T(8,128)(2,1)}, bf16[448,512]{1,0:T(8,128)(2,1)}, u32[]{:S(2)}, u32[]{:S(2)}) %collective-permute-start.12) | collective-permute-done | bytes 458784 | tf_op jit(solution)/shard_map/gather_head_far/ppermute | solution.py:22
  100.4 1.0 constant_dynamic-update-slice_fusion.3
  101.5 3.3 %collective-permute-done.13 = bf16[448,512]{1,0:T(8,128)(2,1)} collective-permute-done((bf16[448,512]{1,0:T(8,128)(2,1)}, bf16[448,512]{1,0:T(8,128)(2,1)}, u32[]{:S(2)}, u32[]{:S(2)}) %collective-permute-start.13) | collective-permute-done | bytes 458784 | tf_op jit(solution)/shard_map/gather_head_far/ppermute | solution.py:22
  104.8 1.1 constant_dynamic-update-slice_fusion.2.refs_4_
  108.4 1.4 fusion.41
  109.9 1.0 copy-done.11
  111.0 4.3 %gather_head.1 = bf16[7168,512]{1,0:T(8,128)(2,1)S(1)} custom-call(s32[8]{0:T(128)S(1)} %stack.42.spots_ref, bf16[896,512]{1,0:T(8,128)(2,1)} %refs_0_.1, bf16[896,512]{1,0:T(8,128)(2,1)} %collective-permute-done.refs_1_, bf16[896,512]{1,0:T(8,128)(2,1)S(1)} %collective-permute-done.9.refs_2_, bf16[896,512]{1,0:T(8,128)(2,1)} %collective-permute-done.11.refs_3_, ...), custom_call_target="tpu_custom_call" | custom-call | bytes 14680064 | tf_op jit(solution)/shard_map/gather_head/pallas_call | solution.py:53
  115.3 2.1 fusion.44
  119.3 2.9 %copy-done.3 = bf16[448,7424]{1,0:T(8,128)(2,1)S(1)} copy-done((bf16[448,7424]{1,0:T(8,128)(2,1)S(1)}, bf16[448,7424]{1,0:T(8,128)(2,1)}, u32[]{:S(2)}) %copy-start.3) | copy-done | bytes 6651928
  122.1 1.3 copy-done.12
  123.4 2.2 logits.1
  125.6 1.0 copy-done.8
  126.7 1.5 reduce_max.160
  128.4 1.6 fusion.19
  130.0 2.2 fusion.10
  132.2 1.5 fusion.1
  133.8 14.8 %all_to_all.25 = f32[16,8,256]{2,1,0:T(8,128)S(1)} all-to-all(f32[16,8,256]{2,1,0:T(8,128)S(1)} %broadcast_in_dim.51), channel_id=1, replica_groups=mesh['dp'=8,'vocab'=16] {'vocab'}, dimensions={0} | all-to-all | bytes 262144 | tf_op jit(solution)/shard_map/spread_statistics/all_to_all | solution.py:122
  149.3 2.1 fusion.12.mid_ref
  151.4 2.4 fusion.3.tail_ref
  153.8 2.9 %copy-done.4 = bf16[448,7424]{1,0:T(8,128)(2,1)S(1)} copy-done((bf16[448,7424]{1,0:T(8,128)(2,1)S(1)}, bf16[448,7424]{1,0:T(8,128)(2,1)}, u32[]{:S(2)}) %copy-start.4) | copy-done | bytes 6651928
  156.7 1.9 code_grads.1
  160.5 1.0 squeeze.27
  161.5 2.7 %maximum_maximum_fusion = bf16[16,144,256]{2,1,0:T(8,128)(2,1)} fusion(bf16[16,28,256]{2,1,0:T(8,128)(2,1)S(1)} %squeeze.27, bf16[16,112,256]{2,1,0:T(8,128)(2,1)} %bitcast.98, bf16[144]{0:T(256)(128)(2,1)S(1)} %copy-done.40), kind=kLoop, calls=%fused_computation.35 | loop fusion | flops 3538944 | bytes 2326816 | tf_op jit(solution)/shard_map/code_grads/concatenate | solution.py:255
  164.2 1.9 mid_tail_grads.1
  166.1 2.7 %copy-done.5 = bf16[448,7424]{1,0:T(8,128)(2,1)} copy-done((bf16[448,7424]{1,0:T(8,128)(2,1)}, bf16[448,7424]{1,0:T(8,128)(2,1)S(1)}, u32[]{:S(2)}) %copy-start.5) | copy-done | bytes 6651928
  168.9 4.5 %all-to-all-start.3 = ((bf16[16,144,256]{2,1,0:T(8,128)(2,1)}), bf16[16,144,256]{2,1,0:T(8,128)(2,1)}, u32[]{:S(2)}, u32[]{:S(2)}) async-start(bf16[16,144,256]{2,1,0:T(8,128)(2,1)} %maximum_maximum_fusion), calls=%async_computation.3 | async-start | bytes 2359296 | tf_op jit(solution)/shard_map/code_grads/all_to_all | solution.py:264
  173.8 9.0 %fusion.45 = f32[7168,256]{1,0:T(8,128)} fusion(bf16[7168,512]{1,0:T(8,128)(2,1)} %copy-done.2, bf16[256,512]{1,0:T(8,128)(2,1)S(1)} %fusion.21.refs_0_), kind=kOutput, calls=%fused_computation.113 | convolution fusion | flops 1879048192 | bytes 14942208 | tf_op jit(solution)/shard_map/hidden_grad/dot_general | solution.py:15
  182.8 9.7 %all-to-all-done.3 = bf16[16,144,256]{2,1,0:T(8,128)(2,1)} async-done(((bf16[16,144,256]{2,1,0:T(8,128)(2,1)}), bf16[16,144,256]{2,1,0:T(8,128)(2,1)}, u32[]{:S(2)}, u32[]{:S(2)}) %all-to-all-start.3) | async-done | bytes 1179680 | tf_op jit(solution)/shard_map/code_grads/all_to_all | solution.py:264
  192.5 1.5 reduce_sum.182.refs_0_
  194.0 6.3 %fusion = bf16[7168,256]{1,0:T(8,128)(2,1)} fusion(f32[7168,256]{1,0:T(8,128)} %fusion.45, bf16[144,7168]{1,0:T(8,128)(2,1)S(1)} %copy-done.7, bf16[144,256]{1,0:T(8,128)(2,1)S(1)} %reduce_sum.182.refs_0_), kind=kOutput, calls=%fused_computation.2 | convolution fusion | flops 532152320 | bytes 13148160 | tf_op jit(solution)/shard_map/hidden_grad/dot_general | solution.py:15
  200.2 4.5 %all-to-all-start.4 = ((bf16[16,448,256]{2,1,0:T(8,128)(2,1)}), bf16[16,448,256]{2,1,0:T(8,128)(2,1)}, u32[]{:S(2)}, u32[]{:S(2)}) async-start(bf16[16,448,256]{2,1,0:T(8,128)(2,1)} %bitcast.97), calls=%async_computation.4 | async-start | bytes 7340032 | tf_op jit(solution)/shard_map/hidden_grad/all_to_all | solution.py:281
  204.8 2.6 collective-permute-start.19
  207.3 7.8 %collective-permute-done.19.refs_6_ = bf16[256,512]{1,0:T(8,128)(2,1)S(1)} collective-permute-done((bf16[256,512]{1,0:T(8,128)(2,1)S(1)}, bf16[256,512]{1,0:T(8,128)(2,1)S(1)}, u32[]{:S(2)}, u32[]{:S(2)}) %collective-permute-start.19) | collective-permute-done | bytes 262176 | tf_op jit(solution)/shard_map/head_proj_grads/ppermute | solution.py:22
  215.9 1.3 collective-permute-start.21
  217.7 2.5 collective-permute-done.20
  220.2 1.8 collective-permute-start.27
  222.1 3.7 %collective-permute-done.27.refs_6_ = bf16[144,256]{1,0:T(8,128)(2,1)S(1)} collective-permute-done((bf16[144,256]{1,0:T(8,128)(2,1)S(1)}, bf16[144,256]{1,0:T(8,128)(2,1)S(1)}, u32[]{:S(2)}, u32[]{:S(2)}) %collective-permute-start.27) | collective-permute-done | bytes 73760 | tf_op jit(solution)/shard_map/head_proj_grads/ppermute | solution.py:22
  225.8 2.0 collective-permute-start.28
  227.8 2.3 collective-permute-done.25.refs_2_
  230.5 1.8 collective-permute-start.29
  232.3 3.4 %collective-permute-done.29 = bf16[80,256]{1,0:T(8,128)(2,1)S(1)} collective-permute-done((bf16[80,256]{1,0:T(8,128)(2,1)S(1)}, bf16[80,256]{1,0:T(8,128)(2,1)S(1)}, u32[]{:S(2)}, u32[]{:S(2)}) %collective-permute-start.29) | collective-permute-done | bytes 40992 | tf_op jit(solution)/shard_map/head_proj_grads/ppermute | solution.py:22
  237.6 1.4 copy-done.14
  239.7 2.3 copy.58
  243.7 3.0 %convolution_convert_fusion = bf16[896,512]{1,0:T(8,128)(2,1)} fusion(bf16[2048,896]{1,0:T(8,128)(2,1)S(1)} %bitcast.96, bf16[2048,512]{1,0:T(8,128)(2,1)S(1)} %copy-done.15), kind=kOutput, calls=%fused_computation.23 | convolution fusion | flops 1879506944 | bytes 6684672 | tf_op jit(solution)/shard_map/head_proj_grads/dot_general | solution.py:15
  246.7 7.1 %all-to-all-done.4 = bf16[16,448,256]{2,1,0:T(8,128)(2,1)} async-done(((bf16[16,448,256]{2,1,0:T(8,128)(2,1)}), bf16[16,448,256]{2,1,0:T(8,128)(2,1)}, u32[]{:S(2)}, u32[]{:S(2)}) %all-to-all-start.4) | async-done | bytes 3670048 | tf_op jit(solution)/shard_map/hidden_grad/all_to_all | solution.py:281
  255.1 3.3 %reduce_sum.183 = bf16[448,256]{1,0:T(8,128)(2,1)} reduce(bf16[16,448,256]{2,1,0:T(8,128)(2,1)} %all-to-all-done.4, bf16[]{:T(256)} %constant.16.clone.1), dimensions={0}, to_apply=%region_24.25 | reduce | flops 1720320 | bytes 3899394 | tf_op jit(solution)/shard_map/hidden_grad_sum/reduce_sum | solution.py:289
  258.5 1.2 fusion.42
  260.5 1.7 slice.156
  (193 shorter events, 33.5 us)
Async XLA Ops:
  7.2 79.1 %copy-start = (s32[65536]{0:T(1024)S(1)}, s32[65536]{0:T(1024)}, u32[]{:S(2)}) copy-start(s32[65536]{0:T(1024)} %param.21) | copy-start | bytes 786436
  7.2 5.8 %copy-start.28 = (bf16[896,28]{0,1:T(8,128)(2,1)S(1)}, bf16[896,28]{0,1:T(8,128)(2,1)}, u32[]{:S(2)}) copy-start(bf16[896,28]{0,1:T(8,128)(2,1)} %param.14) | copy-start | bytes 150532
  7.2 5.8 %copy-start.25 = (bf16[896,112]{0,1:T(8,128)(2,1)S(1)}, bf16[896,112]{0,1:T(8,128)(2,1)}, u32[]{:S(2)}) copy-start(bf16[896,112]{0,1:T(8,128)(2,1)} %param.13) | copy-start | bytes 602116
  7.2 88.5 %all-gather.3.cloned.1.call-start = ((), (), s32[]{:S(2)}) async-start(), calls=%async_computation.6 | async-start | bytes 7483392 | tf_op jit(solution)/shard_map/gather_mid_tail/all_gather | solution.py:160
  12.0 29.1 %copy-start.38 = (s32[256]{0:T(256)S(1)}, s32[256]{0:T(256)}, u32[]{:S(2)}) copy-start(s32[256]{0:T(256)} %param.20) | copy-start | bytes 3076
  13.0 13.0 %copy-start.39 = (bf16[144]{0:T(256)(128)(2,1)}, bf16[144]{0:T(256)(128)(2,1)S(1)}, u32[]{:S(2)}) copy-start(bf16[144]{0:T(256)(128)(2,1)S(1)} %pad.9.clone) | copy-start | bytes 868
  13.1 9.1 %collective-permute-start.4 = (bf16[144,896]{1,0:T(8,128)(2,1)S(1)}, bf16[144,896]{1,0:T(8,128)(2,1)S(1)}, u32[]{:S(2)}, u32[]{:S(2)}) collective-permute-start(bf16[144,896]{1,0:T(8,128)(2,1)S(1)} %maximum_maximum_fusion.1.refs_0_), channel_id=1, source_target_pairs={{0,96},{16,112},{32,64},{48,80},{64,32},{80,48},{96,0},{112,16},{1... | collective-permute-start | bytes 774152 | tf_op jit(solution)/shard_map/gather_proj/ppermute | solution.py:22
  16.1 7.7 %collective-permute-start.2 = (bf16[144,896]{1,0:T(8,128)(2,1)S(1)}, bf16[144,896]{1,0:T(8,128)(2,1)S(1)}, u32[]{:S(2)}, u32[]{:S(2)}) collective-permute-start(bf16[144,896]{1,0:T(8,128)(2,1)S(1)} %maximum_maximum_fusion.1.refs_0_), channel_id=1, source_target_pairs={{0,32},{16,48},{32,0},{48,16},{64,96},{80,112},{96,64},{112,80},{1... | collective-permute-start | bytes 774152 | tf_op jit(solution)/shard_map/gather_proj/ppermute | solution.py:22
  22.3 5.8 %collective-permute-start.5 = (bf16[64,896]{1,0:T(8,128)(2,1)S(1)}, bf16[64,896]{1,0:T(8,128)(2,1)S(1)}, u32[]{:S(2)}, u32[]{:S(2)}) collective-permute-start(bf16[64,896]{1,0:T(8,128)(2,1)S(1)} %slice.135), channel_id=1, source_target_pairs={{0,32},{16,48},{32,0},{48,16},{64,96},{80,112},{96,64},{112,80},{1... | collective-permute-start | bytes 344072 | tf_op jit(solution)/shard_map/gather_proj/ppermute | solution.py:22
  24.4 10.2 %collective-permute-start.6 = (bf16[80,896]{1,0:T(8,128)(2,1)}, bf16[80,896]{1,0:T(8,128)(2,1)S(1)}, u32[]{:S(2)}, u32[]{:S(2)}) collective-permute-start(bf16[80,896]{1,0:T(8,128)(2,1)} %slice.136), channel_id=1, source_target_pairs={{0,96},{16,112},{32,64},{48,80},{64,32},{80,48},{96,0},{112,16},{1... | collective-permute-start | bytes 430088 | tf_op jit(solution)/shard_map/gather_proj/ppermute | solution.py:22
  26.0 8.7 %collective-permute-start.1 = (bf16[144,896]{1,0:T(8,128)(2,1)S(1)}, bf16[144,896]{1,0:T(8,128)(2,1)S(1)}, u32[]{:S(2)}, u32[]{:S(2)}) collective-permute-start(bf16[144,896]{1,0:T(8,128)(2,1)S(1)} %maximum_maximum_fusion.1.refs_0_), channel_id=1, source_target_pairs={{0,16},{16,0},{32,48},{48,32},{64,80},{80,64},{96,112},{112,96},{1... | collective-permute-start | bytes 774152 | tf_op jit(solution)/shard_map/gather_proj/ppermute | solution.py:22
  26.0 42.7 %collective-permute-start.9 = (bf16[896,512]{1,0:T(8,128)(2,1)}, bf16[896,512]{1,0:T(8,128)(2,1)S(1)}, u32[]{:S(2)}, u32[]{:S(2)}) collective-permute-start(bf16[896,512]{1,0:T(8,128)(2,1)} %refs_0_.1), channel_id=1, source_target_pairs={{0,32},{16,48},{32,0},{48,16},{64,96},{80,112},{96,64},{112,80},{1... | collective-permute-start | bytes 2752520 | tf_op jit(solution)/shard_map/gather_head_near/ppermute | solution.py:22
  27.4 47.6 %collective-permute-start.10 = (bf16[896,512]{1,0:T(8,128)(2,1)}, bf16[896,512]{1,0:T(8,128)(2,1)S(1)}, u32[]{:S(2)}, u32[]{:S(2)}) collective-permute-start(bf16[896,512]{1,0:T(8,128)(2,1)} %refs_0_.1), channel_id=1, source_target_pairs={{0,96},{16,112},{32,64},{48,80},{64,32},{80,48},{96,0},{112,16},{1... | collective-permute-start | bytes 2752520 | tf_op jit(solution)/shard_map/gather_head_near/ppermute | solution.py:22
  28.8 12.4 %collective-permute-start.8 = (bf16[144,896]{1,0:T(8,128)(2,1)S(1)}, bf16[144,896]{1,0:T(8,128)(2,1)}, u32[]{:S(2)}, u32[]{:S(2)}) collective-permute-start(bf16[144,896]{1,0:T(8,128)(2,1)S(1)} %collective-permute-done.4.refs_6_), channel_id=1, source_target_pairs={{0,16},{16,0},{32,48},{48,32},{64,80},{80,64},{96,112},{112,96},{1... | collective-permute-start | bytes 774152 | tf_op jit(solution)/shard_map/gather_proj/ppermute | solution.py:22
  34.6 6.9 %collective-permute-start.3 = (bf16[144,896]{1,0:T(8,128)(2,1)S(1)}, bf16[144,896]{1,0:T(8,128)(2,1)}, u32[]{:S(2)}, u32[]{:S(2)}) collective-permute-start(bf16[144,896]{1,0:T(8,128)(2,1)S(1)} %collective-permute-done.2.refs_2_), channel_id=1, source_target_pairs={{0,16},{16,0},{32,48},{48,32},{64,80},{80,64},{96,112},{112,96},{1... | collective-permute-start | bytes 774152 | tf_op jit(solution)/shard_map/gather_proj/ppermute | solution.py:22
  34.7 6.9 %collective-permute-start.7 = (bf16[144,896]{1,0:T(8,128)(2,1)S(1)}, bf16[144,896]{1,0:T(8,128)(2,1)}, u32[]{:S(2)}, u32[]{:S(2)}) collective-permute-start(bf16[144,896]{1,0:T(8,128)(2,1)S(1)} %constant_dynamic-update-slice_fusion.refs_4_), channel_id=1, source_target_pairs={{0,16},{16,0},{32,48},{48,32},{64,80},{80,64},{96,112},{112,96},{1... | collective-permute-start | bytes 774152 | tf_op jit(solution)/shard_map/gather_proj/ppermute | solution.py:22
  37.0 40.0 %all-to-all-start.1 = ((bf16[8,16,896]{2,1,0:T(8,128)(2,1)}), bf16[8,16,896]{2,1,0:T(8,128)(2,1)}, u32[]{:S(2)}, u32[]{:S(2)}) async-start(bf16[8,16,896]{2,1,0:T(8,128)(2,1)} %copy.53), calls=%async_computation.1 | async-start | bytes 458752 | tf_op jit(solution)/shard_map/spread_hidden/all_to_all | solution.py:167
  41.1 69.8 %collective-permute-start = (bf16[896,512]{1,0:T(8,128)(2,1)}, bf16[896,512]{1,0:T(8,128)(2,1)}, u32[]{:S(2)}, u32[]{:S(2)}) collective-permute-start(bf16[896,512]{1,0:T(8,128)(2,1)} %refs_0_.1), channel_id=1, source_target_pairs={{0,16},{16,0},{32,48},{48,32},{64,80},{80,64},{96,112},{112,96},{1... | collective-permute-start | bytes 2752520 | tf_op jit(solution)/shard_map/gather_head/ppermute | solution.py:22
  78.1 11.4 %copy-start.22 = (bf16[256,512]{1,0:T(8,128)(2,1)S(1)}, bf16[256,512]{1,0:T(8,128)(2,1)}, u32[]{:S(2)}) copy-start(bf16[256,512]{1,0:T(8,128)(2,1)} %param.17) | copy-start | bytes 786436
  78.1 12.8 %copy-start.16 = (bf16[256,2304]{1,0:T(8,128)(2,1)S(1)}, bf16[256,2304]{1,0:T(8,128)(2,1)}, u32[]{:S(2)}) copy-start(bf16[256,2304]{1,0:T(8,128)(2,1)} %param.19) | copy-start | bytes 3538948
  78.1 28.6 %all-to-all-start = ((bf16[16,144,256]{2,1,0:T(8,128)(2,1)}), bf16[16,144,256]{2,1,0:T(8,128)(2,1)}, u32[]{:S(2)}, u32[]{:S(2)}) async-start(bf16[16,144,256]{2,1,0:T(8,128)(2,1)} %broadcast_in_dim.43), calls=%async_computation | async-start | bytes 2359296 | tf_op jit(solution)/shard_map/spread_codes/all_to_all | solution.py:122
  86.2 153.5 %all-gather.5.cloned.1.call-start = ((), (), s32[]{:S(2)}) async-start(), calls=%async_computation.7 | async-start | bytes 3899392 | tf_op jit(solution)/shard_map/spread_hidden/all_gather | solution.py:169
  88.8 11.6 %collective-permute-start.12 = (bf16[448,512]{1,0:T(8,128)(2,1)}, bf16[448,512]{1,0:T(8,128)(2,1)}, u32[]{:S(2)}, u32[]{:S(2)}) collective-permute-start(bf16[448,512]{1,0:T(8,128)(2,1)} %slice.102), channel_id=1, source_target_pairs={{0,32},{16,48},{32,0},{48,16},{64,96},{80,112},{96,64},{112,80},{1... | collective-permute-start | bytes 1376264 | tf_op jit(solution)/shard_map/gather_head_far/ppermute | solution.py:22
  91.9 12.8 %collective-permute-start.13 = (bf16[448,512]{1,0:T(8,128)(2,1)}, bf16[448,512]{1,0:T(8,128)(2,1)}, u32[]{:S(2)}, u32[]{:S(2)}) collective-permute-start(bf16[448,512]{1,0:T(8,128)(2,1)} %slice.103), channel_id=1, source_target_pairs={{0,96},{16,112},{32,64},{48,80},{64,32},{80,48},{96,0},{112,16},{1... | collective-permute-start | bytes 1376264 | tf_op jit(solution)/shard_map/gather_head_far/ppermute | solution.py:22
  95.7 162.7 %reduce-scatter.2.cloned.1.call-start = ((), (), s32[]{:S(2)}) async-start(), calls=%async_computation.8 | async-start | bytes 7483392 | tf_op jit(solution)/shard_map/mid_tail_grads/reduce_scatter | solution.py:274
  96.4 14.6 %collective-permute-start.11 = (bf16[896,512]{1,0:T(8,128)(2,1)S(1)}, bf16[896,512]{1,0:T(8,128)(2,1)}, u32[]{:S(2)}, u32[]{:S(2)}) collective-permute-start(bf16[896,512]{1,0:T(8,128)(2,1)S(1)} %collective-permute-done.9.refs_2_), channel_id=1, source_target_pairs={{0,16},{16,0},{32,48},{48,32},{64,80},{80,64},{96,112},{112,96},{1... | collective-permute-start | bytes 2752520 | tf_op jit(solution)/shard_map/gather_head/ppermute | solution.py:22
  96.4 14.6 %collective-permute-start.15 = (bf16[896,512]{1,0:T(8,128)(2,1)S(1)}, bf16[896,512]{1,0:T(8,128)(2,1)}, u32[]{:S(2)}, u32[]{:S(2)}) collective-permute-start(bf16[896,512]{1,0:T(8,128)(2,1)S(1)} %collective-permute-done.10.refs_6_), channel_id=1, source_target_pairs={{0,16},{16,0},{32,48},{48,32},{64,80},{80,64},{96,112},{112,96},{1... | collective-permute-start | bytes 2752520 | tf_op jit(solution)/shard_map/gather_head/ppermute | solution.py:22
  105.8 5.1 %collective-permute-start.14 = (bf16[896,512]{1,0:T(8,128)(2,1)S(1)}, bf16[896,512]{1,0:T(8,128)(2,1)}, u32[]{:S(2)}, u32[]{:S(2)}) collective-permute-start(bf16[896,512]{1,0:T(8,128)(2,1)S(1)} %constant_dynamic-update-slice_fusion.2.refs_4_), channel_id=1, source_target_pairs={{0,16},{16,0},{32,48},{48,32},{64,80},{80,64},{96,112},{112,96},{1... | collective-permute-start | bytes 2752520 | tf_op jit(solution)/shard_map/gather_head/ppermute | solution.py:22
  110.9 4.4 %copy-start.21 = (bf16[256,7168]{1,0:T(8,128)(2,1)S(1)}, bf16[256,7168]{1,0:T(8,128)(2,1)}, u32[]{:S(2)}) copy-start(bf16[256,7168]{1,0:T(8,128)(2,1)} %param.11) | copy-start | bytes 11010052
  115.3 3.0 %copy-start.2 = (bf16[7168,512]{1,0:T(8,128)(2,1)}, bf16[7168,512]{1,0:T(8,128)(2,1)S(1)}, u32[]{:S(2)}) copy-start(bf16[7168,512]{1,0:T(8,128)(2,1)S(1)} %gather_head.1) | copy-start | bytes 22020100
  119.3 2.9 %copy-start.3 = (bf16[448,7424]{1,0:T(8,128)(2,1)S(1)}, bf16[448,7424]{1,0:T(8,128)(2,1)}, u32[]{:S(2)}) copy-start(bf16[448,7424]{1,0:T(8,128)(2,1)} %all-gather.3.cloned.1.call-done.w_ref) | copy-start | bytes 19955716
  126.6 3.4 %copy-start.18 = (bf16[256,1280]{1,0:T(8,128)(2,1)S(1)}, bf16[256,1280]{1,0:T(8,128)(2,1)}, u32[]{:S(2)}) copy-start(bf16[256,1280]{1,0:T(8,128)(2,1)} %param.18) | copy-start | bytes 1966084
  126.6 3.4 %copy-start.27 = (s32[1280]{0:T(1024)S(1)}, s32[1280]{0:T(1024)}, u32[]{:S(2)}) copy-start(s32[1280]{0:T(1024)} %iota_add_fusion.1) | copy-start | bytes 15364
  128.4 3.8 %copy-start.17 = (bf16[256,2304]{1,0:T(8,128)(2,1)S(1)}, bf16[256,2304]{1,0:T(8,128)(2,1)}, u32[]{:S(2)}) copy-start(bf16[256,2304]{1,0:T(8,128)(2,1)} %param.19) | copy-start | bytes 3538948
  149.3 4.5 %copy-start.34 = (f32[256]{0:T(256)}, f32[256]{0:T(256)S(1)}, u32[]{:S(2)}) copy-start(f32[256]{0:T(256)S(1)} %get-tuple-element.49) | copy-start | bytes 3076
  149.3 4.5 %copy-start.36 = (f32[256]{0:T(256)}, f32[256]{0:T(256)S(1)}, u32[]{:S(2)}) copy-start(f32[256]{0:T(256)S(1)} %get-tuple-element.66) | copy-start | bytes 3076
  153.8 2.9 %copy-start.4 = (bf16[448,7424]{1,0:T(8,128)(2,1)S(1)}, bf16[448,7424]{1,0:T(8,128)(2,1)}, u32[]{:S(2)}) copy-start(bf16[448,7424]{1,0:T(8,128)(2,1)} %all-gather.3.cloned.1.call-done.w_ref) | copy-start | bytes 19955716
  159.4 4.8 %copy-start.10 = (bf16[256,2304]{1,0:T(8,128)(2,1)S(1)}, bf16[256,2304]{1,0:T(8,128)(2,1)}, u32[]{:S(2)}) copy-start(bf16[256,2304]{1,0:T(8,128)(2,1)} %copy-done.9) | copy-start | bytes 3538948
  159.4 4.8 %copy-start.13 = (bf16[5,448,256]{2,1,0:T(8,128)(2,1)S(1)}, bf16[5,448,256]{2,1,0:T(8,128)(2,1)}, u32[]{:S(2)}) copy-start(bf16[5,448,256]{2,1,0:T(8,128)(2,1)} %copy-done.11) | copy-start | bytes 3440644
  168.8 4.6 %copy-start.19 = (f32[512,256]{0,1:T(8,128)S(1)}, f32[512,256]{0,1:T(8,128)}, u32[]{:S(2)}) copy-start(f32[512,256]{0,1:T(8,128)} %copy.52) | copy-start | bytes 1572868
  168.9 4.6 %copy-start.30 = (s32[256]{0:T(256)S(1)}, s32[256]{0:T(256)}, u32[]{:S(2)}) copy-start(s32[256]{0:T(256)} %and_select_fusion) | copy-start | bytes 3076
  168.9 4.6 %copy-start.33 = (s32[512]{0:T(512)S(1)}, s32[512]{0:T(512)}, u32[]{:S(2)}) copy-start(s32[512]{0:T(512)} %iota_add_fusion.2) | copy-start | bytes 6148
  168.9 4.6 %copy-start.35 = (f32[256]{0:T(256)S(1)}, f32[256]{0:T(256)}, u32[]{:S(2)}) copy-start(f32[256]{0:T(256)} %copy-done.34) | copy-start | bytes 3076
  168.9 4.6 %copy-start.37 = (f32[256]{0:T(256)S(1)}, f32[256]{0:T(256)}, u32[]{:S(2)}) copy-start(f32[256]{0:T(256)} %copy-done.36) | copy-start | bytes 3076
  168.9 23.6 %all-to-all-start.3 = ((bf16[16,144,256]{2,1,0:T(8,128)(2,1)}), bf16[16,144,256]{2,1,0:T(8,128)(2,1)}, u32[]{:S(2)}, u32[]{:S(2)}) async-start(bf16[16,144,256]{2,1,0:T(8,128)(2,1)} %maximum_maximum_fusion), calls=%async_computation.3 | async-start | bytes 2359296 | tf_op jit(solution)/shard_map/code_grads/all_to_all | solution.py:264
  173.8 20.2 %copy-start.7 = (bf16[144,7168]{1,0:T(8,128)(2,1)S(1)}, bf16[144,7168]{1,0:T(8,128)(2,1)}, u32[]{:S(2)}) copy-start(bf16[144,7168]{1,0:T(8,128)(2,1)} %copy-done.6) | copy-start | bytes 6193156
  200.2 53.6 %all-to-all-start.4 = ((bf16[16,448,256]{2,1,0:T(8,128)(2,1)}), bf16[16,448,256]{2,1,0:T(8,128)(2,1)}, u32[]{:S(2)}, u32[]{:S(2)}) async-start(bf16[16,448,256]{2,1,0:T(8,128)(2,1)} %bitcast.97), calls=%async_computation.4 | async-start | bytes 7340032 | tf_op jit(solution)/shard_map/hidden_grad/all_to_all | solution.py:281
  204.8 10.4 %collective-permute-start.19 = (bf16[256,512]{1,0:T(8,128)(2,1)S(1)}, bf16[256,512]{1,0:T(8,128)(2,1)S(1)}, u32[]{:S(2)}, u32[]{:S(2)}) collective-permute-start(bf16[256,512]{1,0:T(8,128)(2,1)S(1)} %fusion.21.refs_0_), channel_id=1, source_target_pairs={{0,96},{16,112},{32,64},{48,80},{64,32},{80,48},{96,0},{112,16},{1... | collective-permute-start | bytes 786440 | tf_op jit(solution)/shard_map/head_proj_grads/ppermute | solution.py:22
  207.3 8.6 %collective-permute-start.17 = (bf16[256,512]{1,0:T(8,128)(2,1)S(1)}, bf16[256,512]{1,0:T(8,128)(2,1)S(1)}, u32[]{:S(2)}, u32[]{:S(2)}) collective-permute-start(bf16[256,512]{1,0:T(8,128)(2,1)S(1)} %fusion.21.refs_0_), channel_id=1, source_target_pairs={{0,32},{16,48},{32,0},{48,16},{64,96},{80,112},{96,64},{112,80},{1... | collective-permute-start | bytes 786440 | tf_op jit(solution)/shard_map/head_proj_grads/ppermute | solution.py:22
  215.2 5.0 %collective-permute-start.20 = (bf16[128,512]{1,0:T(8,128)(2,1)S(1)}, bf16[128,512]{1,0:T(8,128)(2,1)S(1)}, u32[]{:S(2)}, u32[]{:S(2)}) collective-permute-start(bf16[128,512]{1,0:T(8,128)(2,1)S(1)} %slice.148), channel_id=1, source_target_pairs={{0,32},{16,48},{32,0},{48,16},{64,96},{80,112},{96,64},{112,80},{1... | collective-permute-start | bytes 393224 | tf_op jit(solution)/shard_map/head_proj_grads/ppermute | solution.py:22
  215.9 9.9 %collective-permute-start.21 = (bf16[128,512]{1,0:T(8,128)(2,1)S(1)}, bf16[128,512]{1,0:T(8,128)(2,1)S(1)}, u32[]{:S(2)}, u32[]{:S(2)}) collective-permute-start(bf16[128,512]{1,0:T(8,128)(2,1)S(1)} %slice.149), channel_id=1, source_target_pairs={{0,96},{16,112},{32,64},{48,80},{64,32},{80,48},{96,0},{112,16},{1... | collective-permute-start | bytes 393224 | tf_op jit(solution)/shard_map/head_proj_grads/ppermute | solution.py:22
  217.2 18.5 %collective-permute-start.16 = (bf16[256,512]{1,0:T(8,128)(2,1)S(1)}, bf16[256,512]{1,0:T(8,128)(2,1)S(1)}, u32[]{:S(2)}, u32[]{:S(2)}) collective-permute-start(bf16[256,512]{1,0:T(8,128)(2,1)S(1)} %fusion.21.refs_0_), channel_id=1, source_target_pairs={{0,16},{16,0},{32,48},{48,32},{64,80},{80,64},{96,112},{112,96},{1... | collective-permute-start | bytes 786440 | tf_op jit(solution)/shard_map/head_proj_grads/ppermute | solution.py:22
  217.2 19.0 %collective-permute-start.23 = (bf16[256,512]{1,0:T(8,128)(2,1)S(1)}, bf16[256,512]{1,0:T(8,128)(2,1)S(1)}, u32[]{:S(2)}, u32[]{:S(2)}) collective-permute-start(bf16[256,512]{1,0:T(8,128)(2,1)S(1)} %collective-permute-done.19.refs_6_), channel_id=1, source_target_pairs={{0,16},{16,0},{32,48},{48,32},{64,80},{80,64},{96,112},{112,96},{1... | collective-permute-start | bytes 786440 | tf_op jit(solution)/shard_map/head_proj_grads/ppermute | solution.py:22
  217.7 18.6 %collective-permute-start.18 = (bf16[256,512]{1,0:T(8,128)(2,1)S(1)}, bf16[256,512]{1,0:T(8,128)(2,1)S(1)}, u32[]{:S(2)}, u32[]{:S(2)}) collective-permute-start(bf16[256,512]{1,0:T(8,128)(2,1)S(1)} %collective-permute-done.17.refs_2_), channel_id=1, source_target_pairs={{0,16},{16,0},{32,48},{48,32},{64,80},{80,64},{96,112},{112,96},{1... | collective-permute-start | bytes 786440 | tf_op jit(solution)/shard_map/head_proj_grads/ppermute | solution.py:22
  220.2 5.6 %collective-permute-start.27 = (bf16[144,256]{1,0:T(8,128)(2,1)S(1)}, bf16[144,256]{1,0:T(8,128)(2,1)S(1)}, u32[]{:S(2)}, u32[]{:S(2)}) collective-permute-start(bf16[144,256]{1,0:T(8,128)(2,1)S(1)} %reduce_sum.182.refs_0_), channel_id=1, source_target_pairs={{0,96},{16,112},{32,64},{48,80},{64,32},{80,48},{96,0},{112,16},{1... | collective-permute-start | bytes 221192 | tf_op jit(solution)/shard_map/head_proj_grads/ppermute | solution.py:22
  225.8 4.4 %collective-permute-start.25 = (bf16[144,256]{1,0:T(8,128)(2,1)S(1)}, bf16[144,256]{1,0:T(8,128)(2,1)S(1)}, u32[]{:S(2)}, u32[]{:S(2)}) collective-permute-start(bf16[144,256]{1,0:T(8,128)(2,1)S(1)} %reduce_sum.182.refs_0_), channel_id=1, source_target_pairs={{0,32},{16,48},{32,0},{48,16},{64,96},{80,112},{96,64},{112,80},{1... | collective-permute-start | bytes 221192 | tf_op jit(solution)/shard_map/head_proj_grads/ppermute | solution.py:22
  225.8 4.7 %collective-permute-start.28 = (bf16[64,256]{1,0:T(8,128)(2,1)S(1)}, bf16[64,256]{1,0:T(8,128)(2,1)S(1)}, u32[]{:S(2)}, u32[]{:S(2)}) collective-permute-start(bf16[64,256]{1,0:T(8,128)(2,1)S(1)} %slice.150), channel_id=1, source_target_pairs={{0,32},{16,48},{32,0},{48,16},{64,96},{80,112},{96,64},{112,80},{1... | collective-permute-start | bytes 98312 | tf_op jit(solution)/shard_map/head_proj_grads/ppermute | solution.py:22
  230.1 6.6 %collective-permute-start.22 = (bf16[256,512]{1,0:T(8,128)(2,1)S(1)}, bf16[256,512]{1,0:T(8,128)(2,1)S(1)}, u32[]{:S(2)}, u32[]{:S(2)}) collective-permute-start(bf16[256,512]{1,0:T(8,128)(2,1)S(1)} %constant_dynamic-update-slice_fusion.10.refs_4_), channel_id=1, source_target_pairs={{0,16},{16,0},{32,48},{48,32},{64,80},{80,64},{96,112},{112,96},{1... | collective-permute-start | bytes 786440 | tf_op jit(solution)/shard_map/head_proj_grads/ppermute | solution.py:22
  230.5 5.2 %collective-permute-start.29 = (bf16[80,256]{1,0:T(8,128)(2,1)S(1)}, bf16[80,256]{1,0:T(8,128)(2,1)S(1)}, u32[]{:S(2)}, u32[]{:S(2)}) collective-permute-start(bf16[80,256]{1,0:T(8,128)(2,1)S(1)} %slice.151), channel_id=1, source_target_pairs={{0,96},{16,112},{32,64},{48,80},{64,32},{80,48},{96,0},{112,16},{1... | collective-permute-start | bytes 122888 | tf_op jit(solution)/shard_map/head_proj_grads/ppermute | solution.py:22
  235.7 3.2 %collective-permute-start.24 = (bf16[144,256]{1,0:T(8,128)(2,1)S(1)}, bf16[144,256]{1,0:T(8,128)(2,1)S(1)}, u32[]{:S(2)}, u32[]{:S(2)}) collective-permute-start(bf16[144,256]{1,0:T(8,128)(2,1)S(1)} %reduce_sum.182.refs_0_), channel_id=1, source_target_pairs={{0,16},{16,0},{32,48},{48,32},{64,80},{80,64},{96,112},{112,96},{1... | collective-permute-start | bytes 221192 | tf_op jit(solution)/shard_map/head_proj_grads/ppermute | solution.py:22
  235.7 3.2 %collective-permute-start.31 = (bf16[144,256]{1,0:T(8,128)(2,1)S(1)}, bf16[144,256]{1,0:T(8,128)(2,1)S(1)}, u32[]{:S(2)}, u32[]{:S(2)}) collective-permute-start(bf16[144,256]{1,0:T(8,128)(2,1)S(1)} %collective-permute-done.27.refs_6_), channel_id=1, source_target_pairs={{0,16},{16,0},{32,48},{48,32},{64,80},{80,64},{96,112},{112,96},{1... | collective-permute-start | bytes 221192 | tf_op jit(solution)/shard_map/head_proj_grads/ppermute | solution.py:22
  236.2 2.7 %collective-permute-start.26 = (bf16[144,256]{1,0:T(8,128)(2,1)S(1)}, bf16[144,256]{1,0:T(8,128)(2,1)S(1)}, u32[]{:S(2)}, u32[]{:S(2)}) collective-permute-start(bf16[144,256]{1,0:T(8,128)(2,1)S(1)} %collective-permute-done.25.refs_2_), channel_id=1, source_target_pairs={{0,16},{16,0},{32,48},{48,32},{64,80},{80,64},{96,112},{112,96},{1... | collective-permute-start | bytes 221192 | tf_op jit(solution)/shard_map/head_proj_grads/ppermute | solution.py:22
  236.3 2.6 collective-permute-start.30
  255.1 7.0 %copy-start.1 = (s32[65536]{0:T(1024)S(1)}, s32[65536]{0:T(1024)}, u32[]{:S(2)}) copy-start(s32[65536]{0:T(1024)} %param.21) | copy-start | bytes 786436
  (16 other events, 25.2 us)
Sparse Core Ops, SparseCore 0:
  13.0 68.4 all-gather.2
  95.8 49.0 all-gather.4
  169.0 46.1 reduce-scatter.1

commit v2 on v1

v2 whole, which is shorter than its diff:
```python
import functools

import jax
import jax.numpy as jnp
from jax import lax
from jax.experimental import pallas as pl
from jax.experimental.pallas import tpu as pltpu
from jax.sharding import PartitionSpec as P

BF16 = jnp.bfloat16
F32 = jnp.float32


def dot(left, right, left_dim, right_dim):
    return lax.dot_general(
        left, right, (((left_dim,), (right_dim,)), ((), ())), preferred_element_type=F32
    )


def swap(block, axis_name, flip):
    pairs = [(i, i ^ flip) for i in range(lax.axis_size(axis_name))]
    return lax.ppermute(block, axis_name, pairs)


def ring_near(block, axis_name, step):
    return swap(block, axis_name, step), swap(block, axis_name, 3 * step)


def ring_far(near, other, axis_name, step, half):
    return jnp.concatenate(
        [swap(other[:half], axis_name, step), swap(near[half:], axis_name, 3 * step)], axis=0
    )


def place_kernel(axis, spots_ref, *refs):
    blocks, out, sems = refs[:-2], refs[-2], refs[-1]
    copies = []
    for k, block in enumerate(blocks):
        size = block.shape[axis]
        start = pl.multiple_of(spots_ref[k] * size, size)
        spot = out.at[(slice(None),) * axis + (pl.ds(start, size),)]
        copies.append(pltpu.make_async_copy(block, spot, sems.at[k]))
    for copy in copies:
        copy.start()
    for copy in copies:
        copy.wait()


def place(blocks, spots, axis, hidden_flops=0):
    shape = list(blocks[0].shape)
    shape[axis] *= len(blocks)
    moved = 2 * len(blocks) * blocks[0].size * blocks[0].dtype.itemsize
    return pl.pallas_call(
        functools.partial(place_kernel, axis),
        out_shape=jax.ShapeDtypeStruct(tuple(shape), blocks[0].dtype),
        in_specs=[pl.BlockSpec(memory_space=pltpu.SMEM)]
        + [pl.BlockSpec(memory_space=pltpu.VMEM)] * len(blocks),
        out_specs=pl.BlockSpec(memory_space=pl.ANY),
        scratch_shapes=[pltpu.SemaphoreType.DMA((len(blocks),))],
        compiler_params=pltpu.CompilerParams(vmem_limit_bytes=16 << 20),
        cost_estimate=pl.CostEstimate(flops=hidden_flops, bytes_accessed=moved, transcendentals=0),
    )(jnp.stack(spots).astype(jnp.int32), *blocks)


def half_rows(block):
    return block.shape[0] // 32 * 16


def both_cores(parts, axis, hidden_flops=0):
    blocks = [p for part in parts for p in (part, swap(part, "dp", 1))]
    me = lax.axis_index("dp")
    return place(blocks, [me ^ flip for flip in range(len(blocks))], axis, hidden_flops)


def gather_dp(block, axis, hidden_flops=0):
    near, other = ring_near(block, "dp", 2)
    far = ring_far(near, other, "dp", 2, half_rows(block))
    return both_cores([block, near, far, other], axis, hidden_flops)


def in_vmem(kernel, out_shape, *operands, in_specs=None, scratch_shapes=()):
    outs = out_shape if isinstance(out_shape, tuple) else (out_shape,)
    size = sum(a.size * a.dtype.itemsize for a in operands + outs)
    specs = in_specs or [pl.BlockSpec(memory_space=pltpu.VMEM)] * len(operands)
    return pl.pallas_call(
        kernel,
        out_shape=out_shape,
        in_specs=specs,
        scratch_shapes=scratch_shapes,
        compiler_params=pltpu.CompilerParams(vmem_limit_bytes=48 << 20),
        cost_estimate=pl.CostEstimate(flops=2 * 10**9, bytes_accessed=size, transcendentals=0),
    )(*operands)


def fetch(source, held, sems, spans, base=0):
    copies = [
        pltpu.make_async_copy(
            source.at[:, pl.ds(start, size)], held.at[:, pl.ds(start - base, size)], sems.at[k]
        )
        for k, (start, size) in enumerate(spans)
    ]
    for copy in copies:
        copy.start()
    return copies


def column_spans(groups, widths):
    spans, start = [], 0
    for count, width in zip(groups, widths):
        for _ in range(count):
            spans.append((start, width))
            start += width
    return spans


def pack_kernel(spans, quarters, mid_ref, tail_ref, head_ref, out_ref):
    depth = tail_ref.shape[0]
    mid, head = mid_ref[...].astype(F32), head_ref[...].astype(F32)
    for k, (start, size) in enumerate(spans):
        if k < quarters:
            piece = mid[k * depth : (k + 1) * depth].astype(BF16)
        elif k == quarters:
            piece = tail_ref[...]
        else:
            row = (k - quarters - 1) * depth
            piece = head[row : row + depth].astype(BF16)
        out_ref[:, start : start + size] = piece


def unpack_kernel(spans, packed_ref, mid_ref, tail_ref):
    quarters = [packed_ref[:, a : a + size].astype(F32) for a, size in spans[:-1]]
    mid_ref[...] = jnp.concatenate(quarters, axis=0).astype(BF16)
    start, size = spans[-1]
    tail_ref[...] = packed_ref[:, start : start + size]


ROWS = 16


def row_blocks(rows, body):
    def step(k, carry):
        body(pl.ds(pl.multiple_of(k * ROWS, ROWS), ROWS))
        return carry

    lax.fori_loop(0, rows // ROWS, step, 0)


def hits_of(base, position, shape):
    return position - base == lax.broadcasted_iota(jnp.int32, shape, 1)


def forward_kernel(
    spans, quarters, ranks, bases_ref, w_any, codes_ref, hidden_ref, position_ref,
    target_head, target_mid, target_tail,
    z_ref, head_ref, mid_ref, tail_ref, stats_ref, w_ref, sems,
):
    copies = fetch(w_any, w_ref, sems, spans)
    rank_mid, rank_tail = ranks
    n_dp, per = 2 * codes_ref.shape[0] // quarters, quarters // 2
    depth = rank_mid // per
    codes = [codes_ref[k].astype(F32) for k in range(codes_ref.shape[0])]
    for q in range(quarters):
        first = q % per * depth
        z_ref[q] = jnp.concatenate(
            [codes[2 * j + q // per][first : first + depth] for j in range(n_dp)], axis=0
        ).astype(BF16)
    z_ref[quarters] = jnp.concatenate(
        [code[rank_mid : rank_mid + rank_tail] for code in codes], axis=0
    ).astype(BF16)
    for k, (start, size) in enumerate(spans):
        copies[k].wait()
        weight = w_ref[:, start : start + size]
        if k < quarters:
            part = dot(z_ref[k], weight, 0, 0)
            mid_ref[...] = part if k == 0 else mid_ref[...] + part
        elif k == quarters:
            tail_ref[...] = dot(z_ref[k], weight, 0, 0)
        else:
            part = dot(hidden_ref[k - quarters - 1], weight, 0, 0)
            head_ref[...] = part if k == quarters + 1 else head_ref[...] + part

    tiers = ((head_ref, target_head), (mid_ref, target_mid), (tail_ref, target_tail))

    def body(block):
        pairs = [(s[block, :], t[block, :].astype(F32)) for s, t in tiers]
        position = position_ref[block, :]
        top_s = top_t = None
        for s, t in pairs:
            here_s, here_t = (jnp.max(a, axis=1, keepdims=True) for a in (s, t))
            top_s = here_s if top_s is None else jnp.maximum(top_s, here_s)
            top_t = here_t if top_t is None else jnp.maximum(top_t, here_t)
        mass_s = mass_t = cross = picked = jnp.zeros_like(top_s)
        for k, (s, t) in enumerate(pairs):
            hit = hits_of(bases_ref[k], position, s.shape)
            weight = jnp.exp(t - top_t)
            mass_s += jnp.sum(jnp.exp(s - top_s), axis=1, keepdims=True)
            mass_t += jnp.sum(weight, axis=1, keepdims=True)
            cross += jnp.sum(weight * (t - s), axis=1, keepdims=True)
            picked += jnp.sum(jnp.where(hit, s, 0.0), axis=1, keepdims=True)
        lane = lax.broadcasted_iota(jnp.int32, (ROWS, stats_ref.shape[1]), 1)
        out = jnp.zeros(lane.shape, F32)
        for k, value in enumerate((top_s, top_t, mass_s, mass_t, cross, picked)):
            out = jnp.where(lane == k, value, out)
        stats_ref[block, :] = out

    row_blocks(head_ref.shape[0], body)


def backward_kernel(
    spans, ranks, bases_ref, w_any, lse_ref, position_ref, s_head, s_mid, s_tail,
    target_head, target_mid, target_tail,
    g_head, g_mid, g_tail, dz_ref, w_ref, sems,
):
    copies = fetch(w_any, w_ref, sems, spans)
    tiers = (
        (s_head, target_head, g_head), (s_mid, target_mid, g_mid), (s_tail, target_tail, g_tail)
    )

    def body(block):
        position, lse = position_ref[block, :], lse_ref[block, :]
        lse_s, lse_t = lse[:, 0:1], lse[:, 1:2]
        for k, (s_ref, t_ref, g_ref) in enumerate(tiers):
            s, t = s_ref[block, :], t_ref[block, :].astype(F32)
            hit = hits_of(bases_ref[k], position, s.shape)
            g = 2.0 * jnp.exp(s - lse_s) - jnp.exp(t - lse_t) - jnp.where(hit, 1.0, 0.0)
            g_ref[block, :] = g.astype(BF16)

    row_blocks(s_head.shape[0], body)
    rank_mid, rank_tail = ranks
    quarters = len(spans) - 1
    n_vocab, padded, rows = dz_ref.shape
    per = quarters // 2
    depth = rank_mid // per
    parts = []
    for q, (start, size) in enumerate(spans):
        copies[q].wait()
        grad = g_tail if q == quarters else g_mid
        parts.append(dot(w_ref[:, start : start + size], grad[...], 1, 1))
    zeros = jnp.zeros((padded - rank_mid - rank_tail, rows), F32)
    for k in range(n_vocab):
        first = k // 2 * depth
        pieces = [parts[k % 2 * per + q][first : first + depth] for q in range(per)]
        pieces += [parts[quarters][k * rank_tail : (k + 1) * rank_tail], zeros]
        dz_ref[k] = jnp.concatenate(pieces, axis=0).astype(BF16)


def weight_grads_kernel(spans, z_ref, mid_ref, tail_ref, out_ref):
    for q, (start, size) in enumerate(spans):
        grad = tail_ref if q == len(spans) - 1 else mid_ref
        out_ref[:, start : start + size] = dot(z_ref[q], grad[...], 1, 0).astype(BF16)


def hidden_kernel(spans, depth, w_any, g_ref, proj_ref, dz_ref, out_ref, w_ref, sems):
    copies = fetch(w_any, w_ref, sems, spans, spans[0][0])
    n_out, height, _ = out_ref.shape
    n_dp = w_ref.shape[0] // depth
    per = height // depth
    for half in range(n_out // n_dp):
        parts = []
        for q in range(half * per, (half + 1) * per):
            copies[q].wait()
            start = spans[q][0] - spans[0][0]
            parts.append(dot(w_ref[:, start : start + spans[q][1]], g_ref[...], 1, 1))
        for j in range(n_dp):
            k = j * (n_out // n_dp) + half
            rows = slice(j * depth, (j + 1) * depth)
            head = jnp.concatenate([part[rows] for part in parts], axis=0)
            out_ref[k] = (head + dot(proj_ref[k], dz_ref[...], 1, 0)).astype(BF16)


def spread_vocab(block):
    size = lax.axis_size("vocab")
    return lax.all_to_all(jnp.broadcast_to(block[None], (size,) + block.shape), "vocab", 0, 0)


def per_device(
    hidden,
    head_weight,
    proj_mid,
    proj_tail,
    mid_weight,
    tail_weight,
    target_head,
    target_mid,
    target_tail,
    top_ids,
    tier_of,
):
    n_vocab = lax.axis_size("vocab")
    n_dp = lax.axis_size("dp")
    v = lax.axis_index("vocab")
    rows, width = hidden.shape
    depth = head_weight.shape[0]
    rank_mid, rank_tail = proj_mid.shape[1], proj_tail.shape[1]
    ranks = rank_mid + rank_tail

    depth_tail = tail_weight.shape[0]
    quarters, groups = mid_weight.shape[0] // depth_tail, depth // depth_tail
    widths = (head_weight.shape[1], mid_weight.shape[1], tail_weight.shape[1])
    spans = column_spans((quarters, 1, groups), (widths[1], widths[2], widths[0]))
    low, head_spans = spans[: quarters + 1], spans[quarters + 1 :]
    packed_width = spans[-1][0] + spans[-1][1]
    low_width = head_spans[0][0]
    height = n_dp * depth_tail
    vmem, smem, anywhere = (
        pl.BlockSpec(memory_space=space) for space in (pltpu.VMEM, pltpu.SMEM, pl.ANY)
    )

    def shaped(*shape, dtype=BF16):
        return jax.ShapeDtypeStruct(shape, dtype)

    with jax.named_scope("gather_weights"):
        packed = in_vmem(
            functools.partial(pack_kernel, spans, quarters),
            shaped(depth_tail, packed_width),
            mid_weight,
            tail_weight,
            head_weight,
        )
        weights = lax.all_gather(packed, "dp", axis=0, tiled=True)
    with jax.named_scope("gather_proj"):
        packed, proj_mid, proj_tail = lax.optimization_barrier((packed, proj_mid, proj_tail))
        pad = -ranks % 16
        proj_t = jnp.concatenate(
            [proj_mid.T, proj_tail.T, jnp.zeros((pad, depth), BF16)], axis=0
        )
        proj_full = gather_dp(proj_t, 1)
    with jax.named_scope("codes"):
        codes = dot(proj_full, hidden, 1, 1).astype(BF16)
    with jax.named_scope("spread_codes"):
        codes_all = spread_vocab(codes)
    with jax.named_scope("spread_hidden"):
        piece = rows // n_vocab
        mine = lax.dynamic_slice_in_dim(hidden, v * piece, piece, 0)
        mine = mine.reshape(piece, n_dp, depth).transpose(1, 0, 2)
        mine = lax.all_to_all(mine, "dp", 0, 0)
        mine, weights = lax.optimization_barrier((mine, weights))
        x_all = lax.all_gather(mine.reshape(n_dp * piece, depth), "vocab", axis=0)
        x_all = x_all.reshape(n_vocab, n_dp, piece, depth).transpose(1, 0, 2, 3)
        x_all = x_all.reshape(n_dp * rows, depth)
    with jax.named_scope("arrange"):
        hidden_t = hidden.T.reshape(n_dp, groups, depth_tail, rows).transpose(1, 0, 2, 3)
        hidden_t = hidden_t.reshape(groups, height, rows)
        proj_rows = proj_full.T.reshape(n_vocab, width // n_vocab, ranks + pad)
        starts = (0, widths[0] * n_vocab, (widths[0] + widths[1]) * n_vocab)
        bases = jnp.stack([start + v * w for start, w in zip(starts, widths)]).astype(jnp.int32)
        positions = jnp.take(tier_of, top_ids).astype(jnp.int32)[:, None]
        codes_all, hidden_t, proj_rows, positions = lax.optimization_barrier(
            (codes_all, hidden_t, proj_rows, positions)
        )

    with jax.named_scope("logits"):
        z, s_head, s_mid, s_tail, stats = in_vmem(
            functools.partial(forward_kernel, spans, quarters, (rank_mid, rank_tail)),
            (
                shaped(quarters + 1, height, rows),
                shaped(rows, widths[0], dtype=F32),
                shaped(rows, widths[1], dtype=F32),
                shaped(rows, widths[2], dtype=F32),
                shaped(rows, 128, dtype=F32),
            ),
            bases,
            weights,
            codes_all,
            hidden_t,
            positions,
            target_head,
            target_mid,
            target_tail,
            in_specs=[smem, anywhere] + [vmem] * 6,
            scratch_shapes=[
                pltpu.VMEM((height, packed_width), BF16),
                pltpu.SemaphoreType.DMA((len(spans),)),
            ],
        )
    with jax.named_scope("spread_statistics"):
        stats = spread_vocab(stats[:, :8].T)
        near_s, near_t, mass_s, mass_t, cross, picked = (stats[:, k] for k in range(6))
        top_s, top_t = jnp.max(near_s, axis=0), jnp.max(near_t, axis=0)
        scale_s, scale_t = jnp.exp(near_s - top_s[None]), jnp.exp(near_t - top_t[None])
        mass_s = jnp.sum(mass_s * scale_s, axis=0)
        mass_t = jnp.sum(mass_t * scale_t, axis=0)
        cross = jnp.sum(cross * scale_t, axis=0)
        picked = jnp.sum(picked, axis=0)
        lse_s = top_s + jnp.log(mass_s)
        lse_t = top_t + jnp.log(mass_t)
        row_loss = cross / mass_t - lse_t + 2.0 * lse_s - picked
        lse = jnp.stack([lse_s, lse_t], axis=1)
    with jax.named_scope("grad_logits"):
        g_head, g_mid, g_tail, dz = in_vmem(
            functools.partial(backward_kernel, low, (rank_mid, rank_tail)),
            (
                shaped(rows, widths[0]),
                shaped(rows, widths[1]),
                shaped(rows, widths[2]),
                shaped(n_vocab, ranks + pad, rows),
            ),
            bases,
            weights,
            lse,
            positions,
            s_head,
            s_mid,
            s_tail,
            target_head,
            target_mid,
            target_tail,
            in_specs=[smem, anywhere] + [vmem] * 8,
            scratch_shapes=[
                pltpu.VMEM((height, low_width), BF16),
                pltpu.SemaphoreType.DMA((len(low),)),
            ],
        )
    with jax.named_scope("code_grads"):
        dz = lax.all_to_all(dz, "vocab", 0, 0)
        dz = jnp.sum(dz.astype(F32), axis=0).astype(BF16)
    with jax.named_scope("mid_tail_grads"):
        packed_grad = in_vmem(
            functools.partial(weight_grads_kernel, low),
            shaped(height, low_width),
            z,
            g_mid,
            g_tail,
        )
        packed_grad = lax.psum_scatter(packed_grad, "dp", scatter_dimension=0, tiled=True)
        mid_grad, tail_grad = in_vmem(
            functools.partial(unpack_kernel, low),
            (shaped(*mid_weight.shape), shaped(*tail_weight.shape)),
            packed_grad,
        )
    with jax.named_scope("hidden_grad"):
        term = in_vmem(
            functools.partial(hidden_kernel, head_spans, depth_tail),
            shaped(n_vocab, width // n_vocab, rows),
            weights,
            g_head,
            proj_rows,
            dz,
            in_specs=[anywhere] + [vmem] * 3,
            scratch_shapes=[
                pltpu.VMEM((height, packed_width - low_width), BF16),
                pltpu.SemaphoreType.DMA((len(head_spans),)),
            ],
        )
        term = lax.all_to_all(term, "vocab", 0, 0)
    with jax.named_scope("head_proj_grads"):
        g_all = gather_dp(g_head, 0)
        head_grad = dot(x_all, g_all, 0, 0).astype(BF16)
        dz_all = gather_dp(dz, 1)
        proj_grad = dot(x_all, dz_all, 0, 1).astype(BF16)
    with jax.named_scope("hidden_grad_sum"):
        term, head_grad, proj_grad, mid_grad, tail_grad = lax.optimization_barrier(
            (term, head_grad, proj_grad, mid_grad, tail_grad)
        )
        hidden_grad = jnp.sum(term.astype(F32), axis=0).astype(BF16).T
    return (
        head_grad,
        proj_grad[:, :rank_mid],
        proj_grad[:, rank_mid:ranks],
        mid_grad,
        tail_grad,
        hidden_grad,
        row_loss,
    )


def solution(mesh):
    split = P("dp", "vocab")
    in_specs = (P("dp", None),) + (split,) * 8 + (P("dp"), P())
    out_specs = (split,) * 6 + (P("dp"),)
    return jax.shard_map(
        per_device, mesh=mesh, in_specs=in_specs, out_specs=out_specs, check_vma=False
    )
```

time: 272 us -> 302 us (1.11)
  Pallas kernels: 13.6 us -> 47.1 us
  waiting for transfers between devices: 87.8 us -> 120 us
  blocking collectives: 14.8 us -> 44.8 us
  other arithmetic: 24.9 us -> 4.37 us
  starting transfers between devices: 45.6 us -> 25.5 us
  matrix products: 22.6 us -> 5.2 us
  local copies, waits for them, and re-layouts: 44.8 us -> 40.5 us
    all_gather x1, waiting for transfers between devices: 0.01 us -> 63.2 us  [per_device(): weights = lax.all_gather(packed, 'dp', axis=0, tiled=True)]
    pallas_call x3 -> x6, Pallas kernels: 6 us -> 44.7 us  [in_vmem(): pl.pallas_call(kernel, out_shape=out_shape, in_specs=specs, scratch_shape...]
    ppermute x32 -> x24, waiting for transfers between devices: 69 us -> 31.6 us  [swap(): return lax.ppermute(block, axis_name, pairs)]
    all_to_all x0 -> x2, blocking collectives: none -> 32.4 us  [the longest x1 20.9 us: per_device(): dz = lax.all_to_all(dz, 'vocab', 0, 0)]
    dot_general x6 -> x3, matrix products: 22.6 us -> 5.2 us  [dot(): lax.dot_general(left, right, (((left_dim,), (right_dim,)), ((), ())), pre...]
    all_to_all x1, waiting for transfers between devices: 0.01 us -> 14.8 us  [spread_vocab(): lax.all_to_all(jnp.broadcast_to(block[None], (size,) + block.shape), 'voc...]
    all_to_all x2 -> x0, waiting for transfers between devices: 11.6 us -> none  [the longest x1 9.69 us: per_device(): dz = lax.all_to_all(dz, 'vocab', 0, 0)]
    ppermute x32 -> x24, starting transfers between devices: 24.3 us -> 13.9 us  [swap(): return lax.ppermute(block, axis_name, pairs)]
  transfers between devices with their start and end apart: 39 -> 29, of which waited for: 16 -> 14; matrix products, arithmetic and copies ran while one was open for 25% -> 9% of each run, Pallas kernels for 5% -> 15%
where the time goes in v2:
time: 302 us; the launch traced here: 301 us
  waiting for transfers between devices  120 us (40%)
  Pallas kernels  47.1 us (16%)
  blocking collectives  44.8 us (15%)
  local copies, waits for them, and re-layouts  40.5 us (13%)
  starting transfers between devices  25.5 us (8%)
  between operations  14.2 us (5%)
  matrix products  5.2 us (2%)
  other arithmetic  4.37 us (1%)
    all_gather x1, waiting for transfers between devices, per_device(): weights = lax.all_gather(packed, 'dp', axis=0, tiled=True)  63.2 us
    pallas_call x6, Pallas kernels, in_vmem(): pl.pallas_call(kernel, out_shape=out_shape, in_specs=specs, scratch_shape...  44.7 us
    ppermute x24, waiting for transfers between devices, swap(): return lax.ppermute(block, axis_name, pairs)  31.6 us
    unnamed x65, local copies, waits for them, and re-layouts  24.5 us
    all_to_all x1, blocking collectives, per_device(): dz = lax.all_to_all(dz, 'vocab', 0, 0)  20.9 us
    all_to_all x1, waiting for transfers between devices, spread_vocab(): lax.all_to_all(jnp.broadcast_to(block[None], (size,) + block.shape), 'voc...  14.8 us
    ppermute x24, starting transfers between devices, swap(): return lax.ppermute(block, axis_name, pairs)  13.9 us
    all_to_all x1, blocking collectives, spread_vocab(): lax.all_to_all(jnp.broadcast_to(block[None], (size,) + block.shape), 'voc...  12.4 us
  transfers between devices with their start and end apart: 29, of which 14 were waited for; matrix products, arithmetic and copies ran while one was open for 9% of the time, Pallas kernels for 15%

profile of v2, /device:TPU:0, one launch (start us, length us, event | category | flops | bytes accessed | tf_op | source)
XLA Modules:
  0.0 301.3 jit_solution(13268621982790871054)
XLA Ops:
  7.2 1.2 copy-done.22
  8.4 1.1 copy-done.24
  9.5 0.9 copy-done.25
  10.5 1.4 gather_weights.1
  11.9 1.0 constant_dynamic-slice_fusion
  13.0 11.5 %all_to_all.25 = bf16[8,16,896]{2,1,0:T(8,128)(2,1)} all-to-all(bf16[8,16,896]{2,1,0:T(8,128)(2,1)S(1)} %copy.81), channel_id=1, replica_groups=mesh['dp'=8,'vocab'=16] {'dp'}, dimensions={0} | all-to-all | bytes 458752 | tf_op jit(solution)/shard_map/spread_hidden/all_to_all | solution.py:336
  24.4 63.2 %all-gather.3.cloned.1.call-done.w_any = bf16[448,15616]{1,0:T(8,128)(2,1)} async-done(((bf16[56,15616]{1,0:T(8,128)(2,1)}), bf16[448,15616]{1,0:T(8,128)(2,1)}) %all-gather.3.cloned.1.call-update) | async-done | bytes 13991952 | tf_op jit(solution)/shard_map/gather_weights/all_gather | solution.py:320
  87.9 1.1 collective-permute-start.3
  89.0 1.1 collective-permute-start.1
  90.1 7.4 %collective-permute-done.3.refs_6_ = bf16[144,896]{1,0:T(8,128)(2,1)S(1)} collective-permute-done((bf16[144,896]{1,0:T(8,128)(2,1)S(1)}, bf16[144,896]{1,0:T(8,128)(2,1)S(1)}, u32[]{:S(2)}, u32[]{:S(2)}) %collective-permute-start.3) | collective-permute-done | bytes 258080 | tf_op jit(solution)/shard_map/gather_proj/ppermute | solution.py:22
  97.7 1.7 collective-permute-start.5
  100.0 2.5 collective-permute-done.4
  102.5 1.6 collective-permute-done.5
  105.1 0.7 copy-done.16
  105.8 0.7 copy-done.18
  106.5 0.7 copy-done.20
  107.2 0.9 copy-done.15
  108.1 0.9 copy-done.17
  109.1 0.9 copy-done.19
  110.0 0.9 copy-done.21
  111.0 0.9 gather_proj.1
  111.9 1.1 copy-done.26
  113.0 1.4 convolution_convert_fusion.2
  114.4 1.1 broadcast_in_dim.15
  115.4 7.0 %all-to-all-start.1 = ((bf16[16,144,256]{2,1,0:T(8,128)(2,1)}), bf16[16,144,256]{2,1,0:T(8,128)(2,1)}, u32[]{:S(2)}, u32[]{:S(2)}) async-start(bf16[16,144,256]{2,1,0:T(8,128)(2,1)} %broadcast_in_dim.15), calls=%async_computation.1 | async-start | bytes 2359296 | tf_op jit(solution)/shard_map/spread_codes/all_to_all | solution.py:273
  122.5 5.9 %copy.82 = bf16[256,7168]{0,1:T(8,128)(2,1)} copy(bf16[256,7168]{1,0:T(8,128)(2,1)} %param.11) | data formatting | bytes 7340032 | tf_op args[0]
  128.5 4.3 %copy.83 = bf16[16,8,56,256]{3,2,1,0:T(8,128)(2,1)} copy(bf16[16,8,56,256]{3,2,0,1:T(8,128)(2,1)} %bitcast.76) | data formatting | bytes 7340032 | tf_op jit(solution)/shard_map/arrange/transpose | solution.py:342
  132.8 1.7 gather_fusion
  134.6 2.9 copy.84
  137.6 14.8 %all-to-all-done.1.codes_ref = bf16[16,144,256]{2,1,0:T(8,128)(2,1)} async-done(((bf16[16,144,256]{2,1,0:T(8,128)(2,1)}), bf16[16,144,256]{2,1,0:T(8,128)(2,1)}, u32[]{:S(2)}, u32[]{:S(2)}) %all-to-all-start.1) | async-done | bytes 1179680 | tf_op jit(solution)/shard_map/spread_codes/all_to_all | solution.py:273
  152.6 1.1 copy-done.4
  153.7 17.5 %logits.1 = (bf16[5,448,256]{2,1,0:T(8,128)(2,1)S(1)}, f32[256,512]{1,0:T(8,128)S(1)}, f32[256,1280]{1,0:T(8,128)}, f32[256,2304]{1,0:T(8,128)}, f32[256,128]{1,0:T(8,128)S(1)}) custom-call(s32[3]{0:T(128)S(1)} %pad_add_fusion.bases_ref, bf16[448,15616]{1,0:T(8,128)(2,1)} %all-gather.3.cloned.1.call-done.w_any, ...), custom_call_target="tpu_custom_call" | custom-call | flops 2000000000 | bytes 26412044 | tf_op jit(solution)/shard_map/logits/pallas_call | solution.py:85
  171.2 0.8 copy-done.12
  172.1 12.4 %all_to_all.26 = f32[16,8,256]{2,1,0:T(8,128)S(1)} all-to-all(f32[16,8,256]{2,1,0:T(8,128)S(1)} %broadcast_in_dim.30), channel_id=1, replica_groups=mesh['dp'=8,'vocab'=16] {'vocab'}, dimensions={0} | all-to-all | bytes 262144 | tf_op jit(solution)/shard_map/spread_statistics/all_to_all | solution.py:273
  185.2 0.8 copy.90.lse_ref
  186.0 0.9 copy-done.11
  186.9 1.0 copy-done.13
  188.0 9.4 %grad_logits.1 = (bf16[256,512]{1,0:T(8,128)(2,1)S(1)}, bf16[256,1280]{1,0:T(8,128)(2,1)S(1)}, bf16[256,2304]{1,0:T(8,128)(2,1)S(1)}, bf16[16,144,256]{2,1,0:T(8,128)(2,1)S(1)}) custom-call(s32[3]{0:T(128)S(1)} %pad_add_fusion.bases_ref, bf16[448,15616]{1,0:T(8,128)(2,1)} %all-gather.3.cloned.1.call-done.w_any, f32[256,2]{1,0:T(8,128)S(1)} %copy-done.11, ...), custom_call_target="tpu_custom_call" | custom-call | flops 2000000000 | bytes 23563276 | tf_op jit(solution)/shard_map/grad_logits/pallas_call | solution.py:85
  197.4 0.7 copy-done.9
  198.1 4.7 %mid_tail_grads.2 = bf16[448,7424]{1,0:T(8,128)(2,1)} custom-call(bf16[5,448,256]{2,1,0:T(8,128)(2,1)S(1)} %copy-done.7, bf16[256,1280]{1,0:T(8,128)(2,1)S(1)} %get-tuple-element.46.mid_ref, bf16[256,2304]{1,0:T(8,128)(2,1)S(1)} %get-tuple-element.47.tail_ref), custom_call_target="tpu_custom_call" | custom-call | flops 2000000000 | bytes 9633792 | tf_op jit(solution)/shard_map/mid_tail_grads/pallas_call | solution.py:85
  202.8 20.9 %all_to_all.27 = bf16[16,144,256]{2,1,0:T(8,128)(2,1)S(1)} all-to-all(bf16[16,144,256]{2,1,0:T(8,128)(2,1)S(1)} %get-tuple-element.43), channel_id=1, replica_groups=mesh['dp'=8,'vocab'=16] {'vocab'}, dimensions={0} | all-to-all | bytes 2359296 | tf_op jit(solution)/shard_map/code_grads/all_to_all | solution.py:415
  223.8 10.9 %hidden_grad.1 = bf16[16,448,256]{2,1,0:T(8,128)(2,1)S(1)} custom-call(bf16[448,15616]{1,0:T(8,128)(2,1)} %all-gather.3.cloned.1.call-done.w_any, bf16[256,512]{1,0:T(8,128)(2,1)S(1)} %copy-done.10, bf16[16,448,144]{2,1,0:T(8,128)(2,1)} %bitcast.75, bf16[144,256]{1,0:T(8,128)(2,1)S(1)} %reduce_sum.62.dz_ref.refs_0_), custom_call_target="tpu_custom_call" | custom-call | flops 2000000000 | bytes 20062208 | tf_op jit(solution)/shard_map/hidden_grad/pallas_call | solution.py:85
  234.7 1.9 copy-done.2
  236.6 4.5 %all-to-all-start.4 = ((bf16[16,448,256]{2,1,0:T(8,128)(2,1)}), bf16[16,448,256]{2,1,0:T(8,128)(2,1)}, u32[]{:S(2)}, u32[]{:S(2)}) async-start(bf16[16,448,256]{2,1,0:T(8,128)(2,1)} %copy-done.2), calls=%async_computation.4 | async-start | bytes 7340032 | tf_op jit(solution)/shard_map/hidden_grad/all_to_all | solution.py:445
  241.1 1.1 collective-permute-start.11
  242.2 6.6 %collective-permute-done.11.refs_6_ = bf16[256,512]{1,0:T(8,128)(2,1)S(1)} collective-permute-done((bf16[256,512]{1,0:T(8,128)(2,1)S(1)}, bf16[256,512]{1,0:T(8,128)(2,1)S(1)}, u32[]{:S(2)}, u32[]{:S(2)}) %collective-permute-start.11) | collective-permute-done | bytes 262176 | tf_op jit(solution)/shard_map/head_proj_grads/ppermute | solution.py:22
  249.3 2.4 collective-permute-start.13
  252.2 1.6 collective-permute-done.12
  253.8 1.1 collective-permute-start.19
  254.9 4.5 %collective-permute-done.19.refs_6_ = bf16[144,256]{1,0:T(8,128)(2,1)S(1)} collective-permute-done((bf16[144,256]{1,0:T(8,128)(2,1)S(1)}, bf16[144,256]{1,0:T(8,128)(2,1)S(1)}, u32[]{:S(2)}, u32[]{:S(2)}) %collective-permute-start.19) | collective-permute-done | bytes 73760 | tf_op jit(solution)/shard_map/head_proj_grads/ppermute | solution.py:22
  259.4 2.0 collective-permute-start.20
  261.4 2.3 collective-permute-done.17.refs_2_
  264.1 1.1 collective-permute-start.21
  265.2 4.1 %collective-permute-done.21 = bf16[80,256]{1,0:T(8,128)(2,1)S(1)} collective-permute-done((bf16[80,256]{1,0:T(8,128)(2,1)S(1)}, bf16[80,256]{1,0:T(8,128)(2,1)S(1)}, u32[]{:S(2)}, u32[]{:S(2)}) %collective-permute-start.21) | collective-permute-done | bytes 40992 | tf_op jit(solution)/shard_map/head_proj_grads/ppermute | solution.py:22
  270.4 0.8 head_proj_grads.2
  271.3 0.7 head_proj_grads.3
  272.0 2.3 copy.92
  274.3 0.8 convolution_convert_fusion.1
  275.2 3.0 %convolution_convert_fusion = bf16[896,512]{1,0:T(8,128)(2,1)} fusion(bf16[2048,896]{1,0:T(8,128)(2,1)S(1)} %bitcast.78, bf16[2048,512]{1,0:T(8,128)(2,1)S(1)} %head_proj_grads.2), kind=kOutput, calls=%fused_computation.1 | convolution fusion | flops 1879506944 | bytes 6684672 | tf_op jit(solution)/shard_map/head_proj_grads/dot_general | solution.py:15
  278.2 1.1 copy-done.23
  279.4 0.9 mid_tail_grads.3
  280.3 9.8 %all-to-all-done.4 = bf16[16,448,256]{2,1,0:T(8,128)(2,1)} async-done(((bf16[16,448,256]{2,1,0:T(8,128)(2,1)}), bf16[16,448,256]{2,1,0:T(8,128)(2,1)}, u32[]{:S(2)}, u32[]{:S(2)}) %all-to-all-start.4) | async-done | bytes 3670048 | tf_op jit(solution)/shard_map/hidden_grad/all_to_all | solution.py:445
  290.1 0.7 slice.56
  291.4 3.3 %reduce_sum.63 = bf16[448,256]{1,0:T(8,128)(2,1)} reduce(bf16[16,448,256]{2,1,0:T(8,128)(2,1)} %all-to-all-done.4, bf16[]{:T(256)} %constant.57.clone.1), dimensions={0}, to_apply=%region_6.7 | reduce | flops 1720320 | bytes 3899394 | tf_op jit(solution)/shard_map/hidden_grad_sum/reduce_sum | solution.py:455
  (114 shorter events, 6.4 us)
Async XLA Ops:
  7.2 125.6 %copy-start = (s32[65536]{0:T(1024)S(1)}, s32[65536]{0:T(1024)}, u32[]{:S(2)}) copy-start(s32[65536]{0:T(1024)} %param.21) | copy-start | bytes 786436
  7.2 80.5 %all-gather.3.cloned.1.call-start = ((), (), s32[]{:S(2)}) async-start(), calls=%async_computation.6 | async-start | bytes 15740928 | tf_op jit(solution)/shard_map/gather_weights/all_gather | solution.py:320
  7.2 1.2 copy-start.22
  8.4 1.1 copy-start.24
  9.5 0.9 copy-start.25
  11.8 76.0 %copy-start.27 = (bf16[896,112]{0,1:T(8,128)(2,1)S(1)}, bf16[896,112]{0,1:T(8,128)(2,1)}, u32[]{:S(2)}) copy-start(bf16[896,112]{0,1:T(8,128)(2,1)} %param.13) | copy-start | bytes 602116
  11.8 76.0 %copy-start.28 = (bf16[896,28]{0,1:T(8,128)(2,1)S(1)}, bf16[896,28]{0,1:T(8,128)(2,1)}, u32[]{:S(2)}) copy-start(bf16[896,28]{0,1:T(8,128)(2,1)} %param.14) | copy-start | bytes 150532
  11.8 260.1 %all-gather.5.cloned.1.call-start = ((), (), s32[]{:S(2)}) async-start(), calls=%async_computation.7 | async-start | bytes 3899392 | tf_op jit(solution)/shard_map/spread_hidden/all_gather | solution.py:338
  87.9 9.7 %collective-permute-start.3 = (bf16[144,896]{1,0:T(8,128)(2,1)S(1)}, bf16[144,896]{1,0:T(8,128)(2,1)S(1)}, u32[]{:S(2)}, u32[]{:S(2)}) collective-permute-start(bf16[144,896]{1,0:T(8,128)(2,1)S(1)} %maximum_maximum_fusion.refs_0_), channel_id=1, source_target_pairs={{0,96},{16,112},{32,64},{48,80},{64,32},{80,48},{96,0},{112,16},{1... | collective-permute-start | bytes 774152 | tf_op jit(solution)/shard_map/gather_proj/ppermute | solution.py:22
  89.0 8.7 %collective-permute-start.1 = (bf16[144,896]{1,0:T(8,128)(2,1)S(1)}, bf16[144,896]{1,0:T(8,128)(2,1)S(1)}, u32[]{:S(2)}, u32[]{:S(2)}) collective-permute-start(bf16[144,896]{1,0:T(8,128)(2,1)S(1)} %maximum_maximum_fusion.refs_0_), channel_id=1, source_target_pairs={{0,32},{16,48},{32,0},{48,16},{64,96},{80,112},{96,64},{112,80},{1... | collective-permute-start | bytes 774152 | tf_op jit(solution)/shard_map/gather_proj/ppermute | solution.py:22
  97.6 4.9 %collective-permute-start.4 = (bf16[64,896]{1,0:T(8,128)(2,1)S(1)}, bf16[64,896]{1,0:T(8,128)(2,1)S(1)}, u32[]{:S(2)}, u32[]{:S(2)}) collective-permute-start(bf16[64,896]{1,0:T(8,128)(2,1)S(1)} %slice.62), channel_id=1, source_target_pairs={{0,32},{16,48},{32,0},{48,16},{64,96},{80,112},{96,64},{112,80},{1... | collective-permute-start | bytes 344072 | tf_op jit(solution)/shard_map/gather_proj/ppermute | solution.py:22
  97.7 6.4 %collective-permute-start.5 = (bf16[80,896]{1,0:T(8,128)(2,1)S(1)}, bf16[80,896]{1,0:T(8,128)(2,1)S(1)}, u32[]{:S(2)}, u32[]{:S(2)}) collective-permute-start(bf16[80,896]{1,0:T(8,128)(2,1)S(1)} %slice.63), channel_id=1, source_target_pairs={{0,96},{16,112},{32,64},{48,80},{64,32},{80,48},{96,0},{112,16},{1... | collective-permute-start | bytes 430088 | tf_op jit(solution)/shard_map/gather_proj/ppermute | solution.py:22
  99.4 4.9 %collective-permute-start = (bf16[144,896]{1,0:T(8,128)(2,1)S(1)}, bf16[144,896]{1,0:T(8,128)(2,1)S(1)}, u32[]{:S(2)}, u32[]{:S(2)}) collective-permute-start(bf16[144,896]{1,0:T(8,128)(2,1)S(1)} %maximum_maximum_fusion.refs_0_), channel_id=1, source_target_pairs={{0,16},{16,0},{32,48},{48,32},{64,80},{80,64},{96,112},{112,96},{1... | collective-permute-start | bytes 774152 | tf_op jit(solution)/shard_map/gather_proj/ppermute | solution.py:22
  99.4 5.6 %collective-permute-start.2 = (bf16[144,896]{1,0:T(8,128)(2,1)S(1)}, bf16[144,896]{1,0:T(8,128)(2,1)S(1)}, u32[]{:S(2)}, u32[]{:S(2)}) collective-permute-start(bf16[144,896]{1,0:T(8,128)(2,1)S(1)} %collective-permute-done.1.refs_2_), channel_id=1, source_target_pairs={{0,16},{16,0},{32,48},{48,32},{64,80},{80,64},{96,112},{112,96},{1... | collective-permute-start | bytes 774152 | tf_op jit(solution)/shard_map/gather_proj/ppermute | solution.py:22
  99.9 5.8 %collective-permute-start.7 = (bf16[144,896]{1,0:T(8,128)(2,1)S(1)}, bf16[144,896]{1,0:T(8,128)(2,1)S(1)}, u32[]{:S(2)}, u32[]{:S(2)}) collective-permute-start(bf16[144,896]{1,0:T(8,128)(2,1)S(1)} %collective-permute-done.3.refs_6_), channel_id=1, source_target_pairs={{0,16},{16,0},{32,48},{48,32},{64,80},{80,64},{96,112},{112,96},{1... | collective-permute-start | bytes 774152 | tf_op jit(solution)/shard_map/gather_proj/ppermute | solution.py:22
  104.2 2.3 collective-permute-start.6
  104.3 0.7 copy-start.14
  105.1 0.7 copy-start.16
  105.8 0.7 copy-start.18
  106.5 0.7 copy-start.20
  107.2 0.9 copy-start.15
  108.1 0.9 copy-start.17
  109.0 0.9 copy-start.19
  110.0 0.9 copy-start.21
  110.9 2.0 copy-start.26
  115.4 37.0 %all-to-all-start.1 = ((bf16[16,144,256]{2,1,0:T(8,128)(2,1)}), bf16[16,144,256]{2,1,0:T(8,128)(2,1)}, u32[]{:S(2)}, u32[]{:S(2)}) async-start(bf16[16,144,256]{2,1,0:T(8,128)(2,1)} %broadcast_in_dim.15), calls=%async_computation.1 | async-start | bytes 2359296 | tf_op jit(solution)/shard_map/spread_codes/all_to_all | solution.py:273
  122.5 155.7 %reduce-scatter.2.cloned.1.call-start = ((), (), s32[]{:S(2)}) async-start(), calls=%async_computation.8 | async-start | bytes 7483392 | tf_op jit(solution)/shard_map/mid_tail_grads/reduce_scatter | solution.py:425
  128.5 4.3 %copy-start.29 = (s32[256]{0:T(256)S(1)}, s32[256]{0:T(256)}, u32[]{:S(2)}) copy-start(s32[256]{0:T(256)} %param.20) | copy-start | bytes 3076
  132.8 19.8 %copy-start.3 = (bf16[256,2304]{1,0:T(8,128)(2,1)S(1)}, bf16[256,2304]{1,0:T(8,128)(2,1)}, u32[]{:S(2)}) copy-start(bf16[256,2304]{1,0:T(8,128)(2,1)} %target_tail.3) | copy-start | bytes 3538948
  134.5 18.0 %copy-start.8 = (bf16[256,512]{1,0:T(8,128)(2,1)S(1)}, bf16[256,512]{1,0:T(8,128)(2,1)}, u32[]{:S(2)}) copy-start(bf16[256,512]{1,0:T(8,128)(2,1)} %target_head.3) | copy-start | bytes 786436
  152.6 1.1 copy-start.4
  153.7 32.3 %copy-start.5 = (bf16[256,1280]{1,0:T(8,128)(2,1)S(1)}, bf16[256,1280]{1,0:T(8,128)(2,1)}, u32[]{:S(2)}) copy-start(bf16[256,1280]{1,0:T(8,128)(2,1)} %target_mid.3) | copy-start | bytes 1966084
  171.2 0.8 copy-start.12
  172.0 14.0 %copy-start.6 = (bf16[5,448,256]{2,1,0:T(8,128)(2,1)}, bf16[5,448,256]{2,1,0:T(8,128)(2,1)S(1)}, u32[]{:S(2)}) copy-start(bf16[5,448,256]{2,1,0:T(8,128)(2,1)S(1)} %get-tuple-element.45.z_ref) | copy-start | bytes 3440644
  186.0 0.9 copy-start.11
  186.9 1.0 copy-start.13
  188.0 10.1 %copy-start.7 = (bf16[5,448,256]{2,1,0:T(8,128)(2,1)S(1)}, bf16[5,448,256]{2,1,0:T(8,128)(2,1)}, u32[]{:S(2)}) copy-start(bf16[5,448,256]{2,1,0:T(8,128)(2,1)} %copy-done.6) | copy-start | bytes 3440644
  197.4 0.7 copy-start.9
  202.7 21.1 %copy-start.10 = (bf16[256,512]{1,0:T(8,128)(2,1)S(1)}, bf16[256,512]{1,0:T(8,128)(2,1)}, u32[]{:S(2)}) copy-start(bf16[256,512]{1,0:T(8,128)(2,1)} %copy-done.9) | copy-start | bytes 786436
  234.7 1.9 copy-start.2
  236.6 53.5 %all-to-all-start.4 = ((bf16[16,448,256]{2,1,0:T(8,128)(2,1)}), bf16[16,448,256]{2,1,0:T(8,128)(2,1)}, u32[]{:S(2)}, u32[]{:S(2)}) async-start(bf16[16,448,256]{2,1,0:T(8,128)(2,1)} %copy-done.2), calls=%async_computation.4 | async-start | bytes 7340032 | tf_op jit(solution)/shard_map/hidden_grad/all_to_all | solution.py:445
  241.1 7.7 %collective-permute-start.11 = (bf16[256,512]{1,0:T(8,128)(2,1)S(1)}, bf16[256,512]{1,0:T(8,128)(2,1)S(1)}, u32[]{:S(2)}, u32[]{:S(2)}) collective-permute-start(bf16[256,512]{1,0:T(8,128)(2,1)S(1)} %copy-done.10), channel_id=1, source_target_pairs={{0,96},{16,112},{32,64},{48,80},{64,32},{80,48},{96,0},{112,16},{1... | collective-permute-start | bytes 786440 | tf_op jit(solution)/shard_map/head_proj_grads/ppermute | solution.py:22
  242.2 7.1 %collective-permute-start.9 = (bf16[256,512]{1,0:T(8,128)(2,1)S(1)}, bf16[256,512]{1,0:T(8,128)(2,1)S(1)}, u32[]{:S(2)}, u32[]{:S(2)}) collective-permute-start(bf16[256,512]{1,0:T(8,128)(2,1)S(1)} %copy-done.10), channel_id=1, source_target_pairs={{0,32},{16,48},{32,0},{48,16},{64,96},{80,112},{96,64},{112,80},{1... | collective-permute-start | bytes 786440 | tf_op jit(solution)/shard_map/head_proj_grads/ppermute | solution.py:22
  248.8 5.0 %collective-permute-start.12 = (bf16[128,512]{1,0:T(8,128)(2,1)S(1)}, bf16[128,512]{1,0:T(8,128)(2,1)S(1)}, u32[]{:S(2)}, u32[]{:S(2)}) collective-permute-start(bf16[128,512]{1,0:T(8,128)(2,1)S(1)} %slice.68), channel_id=1, source_target_pairs={{0,32},{16,48},{32,0},{48,16},{64,96},{80,112},{96,64},{112,80},{1... | collective-permute-start | bytes 393224 | tf_op jit(solution)/shard_map/head_proj_grads/ppermute | solution.py:22
  249.3 10.1 %collective-permute-start.13 = (bf16[128,512]{1,0:T(8,128)(2,1)S(1)}, bf16[128,512]{1,0:T(8,128)(2,1)S(1)}, u32[]{:S(2)}, u32[]{:S(2)}) collective-permute-start(bf16[128,512]{1,0:T(8,128)(2,1)S(1)} %slice.69), channel_id=1, source_target_pairs={{0,96},{16,112},{32,64},{48,80},{64,32},{80,48},{96,0},{112,16},{1... | collective-permute-start | bytes 393224 | tf_op jit(solution)/shard_map/head_proj_grads/ppermute | solution.py:22
  251.7 17.6 %collective-permute-start.8 = (bf16[256,512]{1,0:T(8,128)(2,1)S(1)}, bf16[256,512]{1,0:T(8,128)(2,1)S(1)}, u32[]{:S(2)}, u32[]{:S(2)}) collective-permute-start(bf16[256,512]{1,0:T(8,128)(2,1)S(1)} %copy-done.10), channel_id=1, source_target_pairs={{0,16},{16,0},{32,48},{48,32},{64,80},{80,64},{96,112},{112,96},{1... | collective-permute-start | bytes 786440 | tf_op jit(solution)/shard_map/head_proj_grads/ppermute | solution.py:22
  251.7 18.2 %collective-permute-start.10 = (bf16[256,512]{1,0:T(8,128)(2,1)S(1)}, bf16[256,512]{1,0:T(8,128)(2,1)S(1)}, u32[]{:S(2)}, u32[]{:S(2)}) collective-permute-start(bf16[256,512]{1,0:T(8,128)(2,1)S(1)} %collective-permute-done.9.refs_2_), channel_id=1, source_target_pairs={{0,16},{16,0},{32,48},{48,32},{64,80},{80,64},{96,112},{112,96},{1... | collective-permute-start | bytes 786440 | tf_op jit(solution)/shard_map/head_proj_grads/ppermute | solution.py:22
  252.2 17.7 %collective-permute-start.15 = (bf16[256,512]{1,0:T(8,128)(2,1)S(1)}, bf16[256,512]{1,0:T(8,128)(2,1)S(1)}, u32[]{:S(2)}, u32[]{:S(2)}) collective-permute-start(bf16[256,512]{1,0:T(8,128)(2,1)S(1)} %collective-permute-done.11.refs_6_), channel_id=1, source_target_pairs={{0,16},{16,0},{32,48},{48,32},{64,80},{80,64},{96,112},{112,96},{1... | collective-permute-start | bytes 786440 | tf_op jit(solution)/shard_map/head_proj_grads/ppermute | solution.py:22
  253.8 5.6 %collective-permute-start.19 = (bf16[144,256]{1,0:T(8,128)(2,1)S(1)}, bf16[144,256]{1,0:T(8,128)(2,1)S(1)}, u32[]{:S(2)}, u32[]{:S(2)}) collective-permute-start(bf16[144,256]{1,0:T(8,128)(2,1)S(1)} %reduce_sum.62.dz_ref.refs_0_), channel_id=1, source_target_pairs={{0,96},{16,112},{32,64},{48,80},{64,32},{80,48},{96,0},{112,16},{1... | collective-permute-start | bytes 221192 | tf_op jit(solution)/shard_map/head_proj_grads/ppermute | solution.py:22
  259.4 4.4 %collective-permute-start.17 = (bf16[144,256]{1,0:T(8,128)(2,1)S(1)}, bf16[144,256]{1,0:T(8,128)(2,1)S(1)}, u32[]{:S(2)}, u32[]{:S(2)}) collective-permute-start(bf16[144,256]{1,0:T(8,128)(2,1)S(1)} %reduce_sum.62.dz_ref.refs_0_), channel_id=1, source_target_pairs={{0,32},{16,48},{32,0},{48,16},{64,96},{80,112},{96,64},{112,80},{1... | collective-permute-start | bytes 221192 | tf_op jit(solution)/shard_map/head_proj_grads/ppermute | solution.py:22
  259.4 4.7 %collective-permute-start.20 = (bf16[64,256]{1,0:T(8,128)(2,1)S(1)}, bf16[64,256]{1,0:T(8,128)(2,1)S(1)}, u32[]{:S(2)}, u32[]{:S(2)}) collective-permute-start(bf16[64,256]{1,0:T(8,128)(2,1)S(1)} %slice.70), channel_id=1, source_target_pairs={{0,32},{16,48},{32,0},{48,16},{64,96},{80,112},{96,64},{112,80},{1... | collective-permute-start | bytes 98312 | tf_op jit(solution)/shard_map/head_proj_grads/ppermute | solution.py:22
  263.7 6.6 %collective-permute-start.14 = (bf16[256,512]{1,0:T(8,128)(2,1)S(1)}, bf16[256,512]{1,0:T(8,128)(2,1)S(1)}, u32[]{:S(2)}, u32[]{:S(2)}) collective-permute-start(bf16[256,512]{1,0:T(8,128)(2,1)S(1)} %constant_dynamic-update-slice_fusion.2.refs_4_), channel_id=1, source_target_pairs={{0,16},{16,0},{32,48},{48,32},{64,80},{80,64},{96,112},{112,96},{1... | collective-permute-start | bytes 786440 | tf_op jit(solution)/shard_map/head_proj_grads/ppermute | solution.py:22
  264.1 5.2 %collective-permute-start.21 = (bf16[80,256]{1,0:T(8,128)(2,1)S(1)}, bf16[80,256]{1,0:T(8,128)(2,1)S(1)}, u32[]{:S(2)}, u32[]{:S(2)}) collective-permute-start(bf16[80,256]{1,0:T(8,128)(2,1)S(1)} %slice.71), channel_id=1, source_target_pairs={{0,96},{16,112},{32,64},{48,80},{64,32},{80,48},{96,0},{112,16},{1... | collective-permute-start | bytes 122888 | tf_op jit(solution)/shard_map/head_proj_grads/ppermute | solution.py:22
  269.3 1.8 collective-permute-start.16
  269.3 1.8 collective-permute-start.18
  269.8 1.3 collective-permute-start.23
  269.9 1.3 collective-permute-start.22
  278.2 1.1 copy-start.23
  279.4 15.4 %copy-start.1 = (s32[65536]{0:T(1024)S(1)}, s32[65536]{0:T(1024)}, u32[]{:S(2)}) copy-start(s32[65536]{0:T(1024)} %param.21) | copy-start | bytes 786436
Sparse Core Ops, SparseCore 0:
  12.0 75.6 all-gather.2
  89.8 62.9 all-gather.4
  202.9 40.7 reduce-scatter.1

commit v3 on v2

--- a/solution.py
+++ b/solution.py
@@ -46,7 +46,7 @@
         copy.wait()
 
 
-def place(blocks, spots, axis, hidden_flops=0):
+def place(blocks, spots, axis):
     shape = list(blocks[0].shape)
     shape[axis] *= len(blocks)
     moved = 2 * len(blocks) * blocks[0].size * blocks[0].dtype.itemsize
@@ -58,27 +58,23 @@
         out_specs=pl.BlockSpec(memory_space=pl.ANY),
         scratch_shapes=[pltpu.SemaphoreType.DMA((len(blocks),))],
         compiler_params=pltpu.CompilerParams(vmem_limit_bytes=16 << 20),
-        cost_estimate=pl.CostEstimate(flops=hidden_flops, bytes_accessed=moved, transcendentals=0),
+        cost_estimate=pl.CostEstimate(flops=0, bytes_accessed=moved, transcendentals=0),
     )(jnp.stack(spots).astype(jnp.int32), *blocks)
 
 
-def half_rows(block):
-    return block.shape[0] // 32 * 16
-
-
-def both_cores(parts, axis, hidden_flops=0):
+def both_cores(parts, axis):
     blocks = [p for part in parts for p in (part, swap(part, "dp", 1))]
     me = lax.axis_index("dp")
-    return place(blocks, [me ^ flip for flip in range(len(blocks))], axis, hidden_flops)
-
-
-def gather_dp(block, axis, hidden_flops=0):
+    return place(blocks, [me ^ flip for flip in range(len(blocks))], axis)
+
+
+def gather_dp(block, axis, half):
     near, other = ring_near(block, "dp", 2)
-    far = ring_far(near, other, "dp", 2, half_rows(block))
-    return both_cores([block, near, far, other], axis, hidden_flops)
-
-
-def in_vmem(kernel, out_shape, *operands, in_specs=None, scratch_shapes=()):
+    far = ring_far(near, other, "dp", 2, half)
+    return both_cores([block, near, far, other], axis)
+
+
+def in_vmem(kernel, out_shape, *operands, in_specs=None, scratch_shapes=(), flops=2 * 10**9):
     outs = out_shape if isinstance(out_shape, tuple) else (out_shape,)
     size = sum(a.size * a.dtype.itemsize for a in operands + outs)
     specs = in_specs or [pl.BlockSpec(memory_space=pltpu.VMEM)] * len(operands)
@@ -88,7 +84,7 @@
         in_specs=specs,
         scratch_shapes=scratch_shapes,
         compiler_params=pltpu.CompilerParams(vmem_limit_bytes=48 << 20),
-        cost_estimate=pl.CostEstimate(flops=2 * 10**9, bytes_accessed=size, transcendentals=0),
+        cost_estimate=pl.CostEstimate(flops=flops, bytes_accessed=size, transcendentals=0),
     )(*operands)
 
 
@@ -250,7 +246,10 @@
         out_ref[:, start : start + size] = dot(z_ref[q], grad[...], 1, 0).astype(BF16)
 
 
-def hidden_kernel(spans, depth, w_any, g_ref, proj_ref, dz_ref, out_ref, w_ref, sems):
+def hidden_kernel(
+    spans, depth, me_ref, w_any, g_ref, proj_ref, dz_ref,
+    a_own, a_near, a_lo, a_hi, a_other, b_own, b_near, b_lo, b_hi, b_other, out_ref, w_ref, sems,
+):
     copies = fetch(w_any, w_ref, sems, spans, spans[0][0])
     n_out, height, _ = out_ref.shape
     n_dp = w_ref.shape[0] // depth
@@ -265,7 +264,81 @@
             k = j * (n_out // n_dp) + half
             rows = slice(j * depth, (j + 1) * depth)
             head = jnp.concatenate([part[rows] for part in parts], axis=0)
-            out_ref[k] = (head + dot(proj_ref[k], dz_ref[...], 1, 0)).astype(BF16)
+            out_ref[me_ref[0] ^ k] = (head + dot(proj_ref[k], dz_ref[...], 1, 0)).astype(BF16)
+    cut = height // 2
+    for k in range(4):
+        a_own[k], a_near[k], a_other[k] = (out_ref[4 * z + k, :cut] for z in (0, 1, 3))
+        b_own[k], b_near[k], b_other[k] = (out_ref[4 * k + y, cut:] for y in (0, 1, 3))
+    for k in range(2):
+        a_lo[k], a_hi[k] = out_ref[8 + k, :cut], out_ref[10 + k, :cut]
+        b_lo[k], b_hi[k] = out_ref[4 * k + 2, cut:], out_ref[4 * k + 10, cut:]
+
+
+def fold_kernel(*refs):
+    n = len(refs) // 6
+    for k in range(n):
+        near, hi, other, lo = refs[4 * k : 4 * k + 4]
+        near_out, other_out = refs[4 * n + 2 * k : 4 * n + 2 * k + 2]
+        cut = lo.shape[0]
+        near_out[:cut] = near[:cut]
+        near_out[cut:] = (near[cut:].astype(F32) + hi[...].astype(F32)).astype(BF16)
+        other_out[:cut] = (other[:cut].astype(F32) + lo[...].astype(F32)).astype(BF16)
+        other_out[cut:] = other[cut:]
+
+
+def total_of(refs):
+    return sum(ref[...].astype(F32) for ref in refs)
+
+
+def turn_kernel(*refs):
+    for k in range(2):
+        total = total_of(refs[3 * k : 3 * k + 3]).astype(BF16)
+        for flip in range(4):
+            refs[6 + 4 * k + flip][...] = total[flip]
+
+
+def end_kernel(*refs):
+    total = jnp.concatenate([total_of(refs[:4]), total_of(refs[4:8])], axis=0)
+    refs[8][...] = total.T.astype(BF16)
+
+
+def fold(*rings, beside):
+    operands = []
+    for near, lo, hi, other, step in rings:
+        lo, hi = swap(lo, "vocab", step), swap(hi, "vocab", 3 * step)
+        operands += [near, hi, other, lo]
+    operands[1], beside = lax.optimization_barrier((operands[1], beside))
+    out = in_vmem(
+        fold_kernel,
+        tuple(
+            jax.ShapeDtypeStruct(ring[k].shape, BF16) for ring in rings for k in (0, 3)
+        ),
+        *operands,
+    )
+    return [
+        (swap(out[2 * k], "vocab", ring[4]), swap(out[2 * k + 1], "vocab", 3 * ring[4]))
+        for k, ring in enumerate(rings)
+    ] + [beside]
+
+
+def ring_sums(a, b, early, late):
+    (a_near, a_other), (b_near, b_other), early = fold((*a[1:], 4), (*b[1:], 1), beside=early)
+    chunk = a[0].shape[1:]
+    out = in_vmem(
+        turn_kernel,
+        (jax.ShapeDtypeStruct(chunk, BF16),) * 8,
+        a[0], a_near, a_other, b[0], b_near, b_other,
+    )
+    moved = [
+        part if flip == 0 else swap(part, "vocab", flip * step)
+        for step, parts in ((1, out[:4]), (4, out[4:]))
+        for flip, part in enumerate(parts)
+    ]
+    moved[0], late = lax.optimization_barrier((moved[0], late))
+    total = in_vmem(
+        end_kernel, jax.ShapeDtypeStruct((chunk[1], 2 * chunk[0]), BF16), *moved
+    )
+    return total, early, late
 
 
 def spread_vocab(block):
@@ -324,7 +397,7 @@
         proj_t = jnp.concatenate(
             [proj_mid.T, proj_tail.T, jnp.zeros((pad, depth), BF16)], axis=0
         )
-        proj_full = gather_dp(proj_t, 1)
+        proj_full = gather_dp(proj_t, 1, (ranks + pad) // 32 * 16)
     with jax.named_scope("codes"):
         codes = dot(proj_full, hidden, 1, 1).astype(BF16)
     with jax.named_scope("spread_codes"):
@@ -334,10 +407,8 @@
         mine = lax.dynamic_slice_in_dim(hidden, v * piece, piece, 0)
         mine = mine.reshape(piece, n_dp, depth).transpose(1, 0, 2)
         mine = lax.all_to_all(mine, "dp", 0, 0)
-        mine, weights = lax.optimization_barrier((mine, weights))
+        mine, codes_all = lax.optimization_barrier((mine, codes_all))
         x_all = lax.all_gather(mine.reshape(n_dp * piece, depth), "vocab", axis=0)
-        x_all = x_all.reshape(n_vocab, n_dp, piece, depth).transpose(1, 0, 2, 3)
-        x_all = x_all.reshape(n_dp * rows, depth)
     with jax.named_scope("arrange"):
         hidden_t = hidden.T.reshape(n_dp, groups, depth_tail, rows).transpose(1, 0, 2, 3)
         hidden_t = hidden_t.reshape(groups, height, rows)
@@ -411,9 +482,14 @@
                 pltpu.SemaphoreType.DMA((len(low),)),
             ],
         )
+        x_all = x_all.reshape(n_dp * rows, depth)
+    with jax.named_scope("head_grad"):
+        g_all = gather_dp(g_head.reshape(n_vocab, piece, -1), 1, n_vocab // 2)
+        g_all = g_all.reshape(n_dp * rows, -1)
     with jax.named_scope("code_grads"):
         dz = lax.all_to_all(dz, "vocab", 0, 0)
         dz = jnp.sum(dz.astype(F32), axis=0).astype(BF16)
+        dz, g_all, x_all = lax.optimization_barrier((dz, g_all, x_all))
     with jax.named_scope("mid_tail_grads"):
         packed_grad = in_vmem(
             functools.partial(weight_grads_kernel, low),
@@ -429,30 +505,34 @@
             packed_grad,
         )
     with jax.named_scope("hidden_grad"):
-        term = in_vmem(
+        cut = width // n_vocab // 2
+        chunks = [shaped(4, cut, rows)] * 2 + [shaped(2, cut, rows)] * 2 + [shaped(4, cut, rows)]
+        pieces = in_vmem(
             functools.partial(hidden_kernel, head_spans, depth_tail),
-            shaped(n_vocab, width // n_vocab, rows),
+            tuple(chunks * 2),
+            v.astype(jnp.int32).reshape(1),
             weights,
             g_head,
             proj_rows,
             dz,
-            in_specs=[anywhere] + [vmem] * 3,
+            in_specs=[smem, anywhere] + [vmem] * 3,
             scratch_shapes=[
+                pltpu.VMEM((n_vocab, 2 * cut, rows), BF16),
                 pltpu.VMEM((height, packed_width - low_width), BF16),
                 pltpu.SemaphoreType.DMA((len(head_spans),)),
             ],
         )
-        term = lax.all_to_all(term, "vocab", 0, 0)
     with jax.named_scope("head_proj_grads"):
-        g_all = gather_dp(g_head, 0)
         head_grad = dot(x_all, g_all, 0, 0).astype(BF16)
-        dz_all = gather_dp(dz, 1)
-        proj_grad = dot(x_all, dz_all, 0, 1).astype(BF16)
+        dz_all = jnp.broadcast_to(dz.T[None], (n_dp, rows, ranks + pad))
+        dz_all = lax.all_to_all(dz_all, "dp", 0, 0).reshape(n_dp, n_vocab, piece, -1)
+        dz_all = dz_all.transpose(1, 0, 2, 3).reshape(n_dp * rows, -1)
+        proj_grad = dot(x_all, dz_all, 0, 0).astype(BF16)
     with jax.named_scope("hidden_grad_sum"):
-        term, head_grad, proj_grad, mid_grad, tail_grad = lax.optimization_barrier(
-            (term, head_grad, proj_grad, mid_grad, tail_grad)
-        )
-        hidden_grad = jnp.sum(term.astype(F32), axis=0).astype(BF16).T
+        hidden_grad, head_grad, late = ring_sums(
+            pieces[:5], pieces[5:], head_grad, (proj_grad, mid_grad, tail_grad)
+        )
+        proj_grad, mid_grad, tail_grad = late
     return (
         head_grad,
         proj_grad[:, :rank_mid],

time: 302 us -> 242 us (0.80)
  waiting for transfers between devices: 120 us -> 38.4 us
  starting transfers between devices: 25.5 us -> 43.7 us
    all_gather x1, waiting for transfers between devices: 63.2 us -> 0.02 us  [per_device(): weights = lax.all_gather(packed, 'dp', axis=0, tiled=True)]
    all_to_all x2 -> x0, blocking collectives: 32.4 us -> none  [the longest x1 20.9 us: per_device(): dz = lax.all_to_all(dz, 'vocab', 0, 0)]
    all_to_all x1 -> x2, blocking collectives: 12.4 us -> 43.2 us  [spread_vocab(): lax.all_to_all(jnp.broadcast_to(block[None], (size,) + block.shape), 'voc...]
    all_to_all x2 -> x3, waiting for transfers between devices: 24.7 us -> 0.01 us  [the longest x1 0.01 us: per_device(): dz = lax.all_to_all(dz, 'vocab', 0, 0)]
    ppermute x24 -> x30, starting transfers between devices: 13.9 us -> 30.2 us  [swap(): return lax.ppermute(block, axis_name, pairs)]
    ppermute x24 -> x30, waiting for transfers between devices: 31.6 us -> 38.3 us  [swap(): return lax.ppermute(block, axis_name, pairs)]
    pallas_call x6 -> x9, Pallas kernels: 44.7 us -> 48.4 us  [in_vmem(): pl.pallas_call(kernel, out_shape=out_shape, in_specs=specs, scratch_shape...]
    reduce_sum x1 -> x0, other arithmetic: 3.29 us -> none  [per_device(): hidden_grad = jnp.sum(term.astype(F32), axis=0).astype(BF16).T]
  transfers between devices with their start and end apart: 29 -> 36, of which waited for: 14 -> 17; matrix products, arithmetic and copies ran while one was open for 9% -> 13% of each run, Pallas kernels for 15% -> 20%
where the time goes in v3:
time: 242 us; the launch traced here: 241 us
  Pallas kernels  50.1 us (21%)
  starting transfers between devices  43.7 us (18%)
  blocking collectives  43.2 us (18%)
  local copies, waits for them, and re-layouts  42.9 us (18%)
  waiting for transfers between devices  38.4 us (16%)
  between operations  14.2 us (6%)
  matrix products  5.85 us (2%)
    pallas_call x9, Pallas kernels, in_vmem(): pl.pallas_call(kernel, out_shape=out_shape, in_specs=specs, scratch_shape...  48.4 us
    all_to_all x2, blocking collectives, spread_vocab(): lax.all_to_all(jnp.broadcast_to(block[None], (size,) + block.shape), 'voc...  43.2 us
    ppermute x30, waiting for transfers between devices, swap(): return lax.ppermute(block, axis_name, pairs)  38.3 us
    ppermute x30, starting transfers between devices, swap(): return lax.ppermute(block, axis_name, pairs)  30.2 us
    unnamed x65, local copies, waits for them, and re-layouts  25 us
    dot_general x3, matrix products, dot(): lax.dot_general(left, right, (((left_dim,), (right_dim,)), ((), ())), pre...  5.85 us
  transfers between devices with their start and end apart: 36, of which 17 were waited for; matrix products, arithmetic and copies ran while one was open for 13% of the time, Pallas kernels for 20%

profile of v3, /device:TPU:0, one launch (start us, length us, event | category | flops | bytes accessed | tf_op | source)
XLA Modules:
  0.0 240.7 jit_solution(16562051449008550941)
XLA Ops:
  7.2 1.2 copy-done.20
  8.4 1.1 copy-done.22
  9.5 0.9 copy-done.23
  10.5 1.3 gather_weights.1
  12.0 2.9 %collective-permute-start.3 = (bf16[144,896]{1,0:T(8,128)(2,1)S(1)}, bf16[144,896]{1,0:T(8,128)(2,1)S(1)}, u32[]{:S(2)}, u32[]{:S(2)}) collective-permute-start(bf16[144,896]{1,0:T(8,128)(2,1)S(1)} %maximum_maximum_fusion.refs_0_), channel_id=1, source_target_pairs={{0,96},{16,112},{32,64},{48,80},{64,32},{80,48},{96,0},{112,16},{1... | collective-permute-start | bytes 774152 | tf_op jit(solution)/shard_map/gather_proj/ppermute | solution.py:22
  15.2 6.0 %collective-permute-done.3.refs_6_ = bf16[144,896]{1,0:T(8,128)(2,1)S(1)} collective-permute-done((bf16[144,896]{1,0:T(8,128)(2,1)S(1)}, bf16[144,896]{1,0:T(8,128)(2,1)S(1)}, u32[]{:S(2)}, u32[]{:S(2)}) %collective-permute-start.3) | collective-permute-done | bytes 258080 | tf_op jit(solution)/shard_map/gather_proj/ppermute | solution.py:22
  22.6 1.7 collective-permute-start.5
  24.8 1.2 collective-permute-done.4
  26.0 3.0 %collective-permute-done.5 = bf16[80,896]{1,0:T(8,128)(2,1)S(1)} collective-permute-done((bf16[80,896]{1,0:T(8,128)(2,1)S(1)}, bf16[80,896]{1,0:T(8,128)(2,1)S(1)}, u32[]{:S(2)}, u32[]{:S(2)}) %collective-permute-start.5) | collective-permute-done | bytes 143392 | tf_op jit(solution)/shard_map/gather_proj/ppermute | solution.py:22
  29.1 1.0 constant_dynamic-slice_fusion
  30.8 4.6 %all-to-all-start = ((bf16[8,16,896]{2,1,0:T(8,128)(2,1)}), bf16[8,16,896]{2,1,0:T(8,128)(2,1)}, u32[]{:S(2)}, u32[]{:S(2)}) async-start(bf16[8,16,896]{2,1,0:T(8,128)(2,1)} %copy.79), calls=%async_computation | async-start | bytes 458752 | tf_op jit(solution)/shard_map/spread_hidden/all_to_all | solution.py:409
  38.4 0.9 copy-done.13
  39.3 1.1 copy-done.15
  40.4 1.0 copy-done.17
  41.4 1.0 copy-done.19
  42.3 0.9 gather_proj.1
  43.2 1.1 copy-done.24
  44.4 2.0 convolution_convert_fusion.2
  46.4 1.0 broadcast_in_dim.17
  47.3 28.7 %all_to_all.25.codes_ref = bf16[16,144,256]{2,1,0:T(8,128)(2,1)} all-to-all(bf16[16,144,256]{2,1,0:T(8,128)(2,1)S(1)} %broadcast_in_dim.17), channel_id=1, replica_groups=mesh['dp'=8,'vocab'=16] {'vocab'}, dimensions={0} | all-to-all | bytes 2359296 | tf_op jit(solution)/shard_map/spread_codes/all_to_all | solution.py:346
  76.1 5.9 %copy.80 = bf16[256,7168]{0,1:T(8,128)(2,1)} copy(bf16[256,7168]{1,0:T(8,128)(2,1)} %param.11) | data formatting | bytes 7340032 | tf_op args[0]
  82.0 4.3 %copy.81 = bf16[16,8,56,256]{3,2,1,0:T(8,128)(2,1)} copy(bf16[16,8,56,256]{3,2,0,1:T(8,128)(2,1)} %bitcast.86) | data formatting | bytes 7340032 | tf_op jit(solution)/shard_map/arrange/transpose | solution.py:413
  86.3 1.7 gather_fusion
  88.1 3.0 %copy.82 = bf16[7168,144]{1,0:T(8,128)(2,1)} copy(bf16[7168,144]{0,1:T(8,128)(2,1)S(1)} %bitcast.78) | data formatting | bytes 4128768 | tf_op jit(solution)/shard_map/arrange/transpose | solution.py:415
  91.3 1.3 copy-done.3
  92.5 1.1 copy-done.4
  93.6 0.9 copy-done.6
  94.6 17.0 %logits.1 = (bf16[5,448,256]{2,1,0:T(8,128)(2,1)S(1)}, f32[256,512]{1,0:T(8,128)S(1)}, f32[256,1280]{1,0:T(8,128)}, f32[256,2304]{1,0:T(8,128)}, f32[256,128]{1,0:T(8,128)S(1)}) custom-call(s32[3]{0:T(128)S(1)} %pad_add_fusion.bases_ref, bf16[448,15616]{1,0:T(8,128)(2,1)} %all-gather.3.cloned.1.call-done.w_any, bf16[16,144,256]{2,1,0:T(8,128)(2,1)S(1)} %copy-done.3, ...), custom_call_target="tpu_custom_call" | custom-call | flops 2000000000 | bytes 26412044 | tf_op jit(solution)/shard_map/logits/pallas_call | solution.py:81
  112.5 14.4 %all_to_all.26 = f32[16,8,256]{2,1,0:T(8,128)S(1)} all-to-all(f32[16,8,256]{2,1,0:T(8,128)S(1)} %broadcast_in_dim.36), channel_id=1, replica_groups=mesh['dp'=8,'vocab'=16] {'vocab'}, dimensions={0} | all-to-all | bytes 262144 | tf_op jit(solution)/shard_map/spread_statistics/all_to_all | solution.py:346
  127.8 1.0 copy-done.11
  128.8 10.3 %grad_logits.1 = (bf16[256,512]{1,0:T(8,128)(2,1)S(1)}, bf16[256,1280]{1,0:T(8,128)(2,1)S(1)}, bf16[256,2304]{1,0:T(8,128)(2,1)S(1)}, bf16[16,144,256]{2,1,0:T(8,128)(2,1)}) custom-call(s32[3]{0:T(128)S(1)} %pad_add_fusion.bases_ref, bf16[448,15616]{1,0:T(8,128)(2,1)} %all-gather.3.cloned.1.call-done.w_any, f32[256,2]{1,0:T(8,128)S(1)} %copy.88.lse_ref, ...), custom_call_target="tpu_custom_call" | custom-call | flops 2000000000 | bytes 23563276 | tf_op jit(solution)/shard_map/grad_logits/pallas_call | solution.py:81
  139.9 4.6 %mid_tail_grads.2 = bf16[448,7424]{1,0:T(8,128)(2,1)} custom-call(bf16[5,448,256]{2,1,0:T(8,128)(2,1)S(1)} %get-tuple-element.91.z_ref, bf16[256,1280]{1,0:T(8,128)(2,1)S(1)} %get-tuple-element.92.mid_ref, bf16[256,2304]{1,0:T(8,128)(2,1)S(1)} %get-tuple-element.93.tail_ref), custom_call_target="tpu_custom_call" | custom-call | flops 2000000000 | bytes 9633792 | tf_op jit(solution)/shard_map/mid_tail_grads/pallas_call | solution.py:81
  144.5 4.5 %all-to-all-start.3 = ((bf16[16,144,256]{2,1,0:T(8,128)(2,1)}), bf16[16,144,256]{2,1,0:T(8,128)(2,1)}, u32[]{:S(2)}, u32[]{:S(2)}) async-start(bf16[16,144,256]{2,1,0:T(8,128)(2,1)} %get-tuple-element.69), calls=%async_computation.3 | async-start | bytes 2359296 | tf_op jit(solution)/shard_map/code_grads/all_to_all | solution.py:490
  149.1 1.3 collective-permute-start.11
  150.6 7.9 %collective-permute-done.11.refs_6_ = bf16[16,16,512]{2,1,0:T(8,128)(2,1)S(1)} collective-permute-done((bf16[16,16,512]{2,1,0:T(8,128)(2,1)S(1)}, bf16[16,16,512]{2,1,0:T(8,128)(2,1)S(1)}, u32[]{:S(2)}, u32[]{:S(2)}) %collective-permute-start.11) | collective-permute-done | bytes 262176 | tf_op jit(solution)/shard_map/head_grad/ppermute | solution.py:22
  158.7 1.0 collective-permute-done.9.refs_2_
  159.7 2.6 %collective-permute-start.13 = (bf16[8,16,512]{2,1,0:T(8,128)(2,1)S(1)}, bf16[8,16,512]{2,1,0:T(8,128)(2,1)S(1)}, u32[]{:S(2)}, u32[]{:S(2)}) collective-permute-start(bf16[8,16,512]{2,1,0:T(8,128)(2,1)S(1)} %slice.61), channel_id=1, source_target_pairs={{0,96},{16,112},{32,64},{48,80},{64,32},{80,48},{96,0},{112,16},{1... | collective-permute-start | bytes 393224 | tf_op jit(solution)/shard_map/head_grad/ppermute | solution.py:22
  162.9 2.1 collective-permute-done.12
  165.0 2.4 %collective-permute-done.13 = bf16[8,16,512]{2,1,0:T(8,128)(2,1)S(1)} collective-permute-done((bf16[8,16,512]{2,1,0:T(8,128)(2,1)S(1)}, bf16[8,16,512]{2,1,0:T(8,128)(2,1)S(1)}, u32[]{:S(2)}, u32[]{:S(2)}) %collective-permute-start.13) | collective-permute-done | bytes 131104 | tf_op jit(solution)/shard_map/head_grad/ppermute | solution.py:22
  167.6 1.5 collective-permute-done.14.refs_5_
  169.9 1.5 reduce_sum.50.dz_ref
  172.3 4.2 %all-to-all-start.4 = ((bf16[8,256,144]{1,2,0:T(8,128)(2,1)}), bf16[8,256,144]{1,2,0:T(8,128)(2,1)}, u32[]{:S(2)}, u32[]{:S(2)}) async-start(bf16[8,256,144]{1,2,0:T(8,128)(2,1)} %broadcast_in_dim.37), calls=%async_computation.4 | async-start | bytes 1179648 | tf_op jit(solution)/shard_map/head_proj_grads/all_to_all | solution.py:528
  176.5 11.4 %hidden_grad.1 = (bf16[4,224,256]{2,1,0:T(8,128)(2,1)S(1)}, bf16[4,224,256]{2,1,0:T(8,128)(2,1)S(1)}, bf16[2,224,256]{2,1,0:T(8,128)(2,1)S(1)}, bf16[2,224,256]{...) custom-call(s32[1]{0:T(128)} %bitcast.me_ref, ...), custom_call_target="tpu_custom_call" | custom-call | flops 2000000000 | bytes 20062212 | tf_op jit(solution)/shard_map/hidden_grad/pallas_call | solution.py:81
  188.0 2.7 %collective-permute-start.16 = (bf16[2,224,256]{2,1,0:T(8,128)(2,1)S(1)}, bf16[2,224,256]{2,1,0:T(8,128)(2,1)S(1)}, u32[]{:S(2)}, u32[]{:S(2)}) collective-permute-start(bf16[2,224,256]{2,1,0:T(8,128)(2,1)S(1)} %get-tuple-element.72), channel_id=1, source_target_pairs={{0,12},{1,13},{2,14},{3,15},{4,8},{5,9},{6,10},{7,11},{8,4},{9,5},... | collective-permute-start | bytes 688136 | tf_op jit(solution)/shard_map/hidden_grad_sum/ppermute | solution.py:22
  191.0 2.6 %collective-permute-start.18 = (bf16[2,224,256]{2,1,0:T(8,128)(2,1)S(1)}, bf16[2,224,256]{2,1,0:T(8,128)(2,1)S(1)}, u32[]{:S(2)}, u32[]{:S(2)}) collective-permute-start(bf16[2,224,256]{2,1,0:T(8,128)(2,1)S(1)} %get-tuple-element.82), channel_id=1, source_target_pairs={{0,3},{1,2},{2,1},{3,0},{4,7},{5,6},{6,5},{7,4},{8,11},{9,10},{10,... | collective-permute-start | bytes 688136 | tf_op jit(solution)/shard_map/hidden_grad_sum/ppermute | solution.py:22
  193.9 3.0 %convolution_convert_fusion = bf16[896,512]{1,0:T(8,128)(2,1)} fusion(bf16[2048,896]{1,0:T(8,128)(2,1)S(1)} %bitcast.97, bf16[2048,512]{1,0:T(8,128)(2,1)S(1)} %bitcast.79), kind=kOutput, calls=%fused_computation.1 | convolution fusion | flops 1879506944 | bytes 6684672 | tf_op jit(solution)/shard_map/head_proj_grads/dot_general | solution.py:15
  197.1 1.1 collective-permute-done.17.refs_3_
  198.3 1.3 collective-permute-done.18.refs_5_
  199.5 1.1 collective-permute-done.19.refs_7_
  200.7 1.1 hidden_grad_sum.3
  201.8 1.7 collective-permute-start.20
  204.6 1.2 collective-permute-start.23
  205.8 2.2 copy.90
  208.0 1.3 copy.91
  209.3 3.7 %collective-permute-done.20.refs_1_ = bf16[4,224,256]{2,1,0:T(8,128)(2,1)S(1)} collective-permute-done((bf16[4,224,256]{2,1,0:T(8,128)(2,1)}, bf16[4,224,256]{2,1,0:T(8,128)(2,1)S(1)}, u32[]{:S(2)}, u32[]{:S(2)}) %collective-permute-start.20) | collective-permute-done | bytes 458784 | tf_op jit(solution)/shard_map/hidden_grad_sum/ppermute | solution.py:22
  213.0 2.6 %collective-permute-done.21.refs_2_ = bf16[4,224,256]{2,1,0:T(8,128)(2,1)S(1)} collective-permute-done((bf16[4,224,256]{2,1,0:T(8,128)(2,1)}, bf16[4,224,256]{2,1,0:T(8,128)(2,1)S(1)}, u32[]{:S(2)}, u32[]{:S(2)}) %collective-permute-start.21) | collective-permute-done | bytes 458784 | tf_op jit(solution)/shard_map/hidden_grad_sum/ppermute | solution.py:22
  216.2 1.5 hidden_grad_sum.4
  219.2 2.7 %collective-permute-start.25 = (bf16[224,256]{1,0:T(8,128)(2,1)S(1)}, bf16[224,256]{1,0:T(8,128)(2,1)S(1)}, u32[]{:S(2)}, u32[]{:S(2)}) collective-permute-start(bf16[224,256]{1,0:T(8,128)(2,1)S(1)} %get-tuple-element.101), channel_id=1, source_target_pairs={{0,2},{1,3},{2,0},{3,1},{4,6},{5,7},{6,4},{7,5},{8,10},{9,11},{10,... | collective-permute-start | bytes 344072 | tf_op jit(solution)/shard_map/hidden_grad_sum/ppermute | solution.py:22
  221.9 1.4 collective-permute-start.26
  223.6 3.6 %collective-permute-start.28 = (bf16[224,256]{1,0:T(8,128)(2,1)S(1)}, bf16[224,256]{1,0:T(8,128)(2,1)S(1)}, u32[]{:S(2)}, u32[]{:S(2)}) collective-permute-start(bf16[224,256]{1,0:T(8,128)(2,1)S(1)} %get-tuple-element.105), channel_id=1, source_target_pairs={{0,8},{1,9},{2,10},{3,11},{4,12},{5,13},{6,14},{7,15},{8,0},{9,1},... | collective-permute-start | bytes 344072 | tf_op jit(solution)/shard_map/hidden_grad_sum/ppermute | solution.py:22
  227.2 0.9 collective-permute-start.29
  228.1 1.1 copy-done.21
  229.2 0.9 mid_tail_grads.3
  231.5 1.7 collective-permute-done.29.refs_7_
  (127 shorter events, 18.3 us)
Async XLA Ops:
  7.2 79.1 %copy-start = (s32[65536]{0:T(1024)S(1)}, s32[65536]{0:T(1024)}, u32[]{:S(2)}) copy-start(s32[65536]{0:T(1024)} %param.21) | copy-start | bytes 786436
  7.2 84.1 %all-gather.3.cloned.1.call-start = ((), (), s32[]{:S(2)}) async-start(), calls=%async_computation.6 | async-start | bytes 15740928 | tf_op jit(solution)/shard_map/gather_weights/all_gather | solution.py:393
  7.2 1.2 copy-start.20
  8.4 1.1 copy-start.22
  9.5 0.9 copy-start.23
  10.5 1.4 copy-start.25
  10.5 1.4 copy-start.26
  12.0 9.1 %collective-permute-start.3 = (bf16[144,896]{1,0:T(8,128)(2,1)S(1)}, bf16[144,896]{1,0:T(8,128)(2,1)S(1)}, u32[]{:S(2)}, u32[]{:S(2)}) collective-permute-start(bf16[144,896]{1,0:T(8,128)(2,1)S(1)} %maximum_maximum_fusion.refs_0_), channel_id=1, source_target_pairs={{0,96},{16,112},{32,64},{48,80},{64,32},{80,48},{96,0},{112,16},{1... | collective-permute-start | bytes 774152 | tf_op jit(solution)/shard_map/gather_proj/ppermute | solution.py:22
  14.9 7.7 %collective-permute-start.1 = (bf16[144,896]{1,0:T(8,128)(2,1)S(1)}, bf16[144,896]{1,0:T(8,128)(2,1)S(1)}, u32[]{:S(2)}, u32[]{:S(2)}) collective-permute-start(bf16[144,896]{1,0:T(8,128)(2,1)S(1)} %maximum_maximum_fusion.refs_0_), channel_id=1, source_target_pairs={{0,32},{16,48},{32,0},{48,16},{64,96},{80,112},{96,64},{112,80},{1... | collective-permute-start | bytes 774152 | tf_op jit(solution)/shard_map/gather_proj/ppermute | solution.py:22
  21.2 4.9 %collective-permute-start.4 = (bf16[64,896]{1,0:T(8,128)(2,1)S(1)}, bf16[64,896]{1,0:T(8,128)(2,1)S(1)}, u32[]{:S(2)}, u32[]{:S(2)}) collective-permute-start(bf16[64,896]{1,0:T(8,128)(2,1)S(1)} %slice.54), channel_id=1, source_target_pairs={{0,32},{16,48},{32,0},{48,16},{64,96},{80,112},{96,64},{112,80},{1... | collective-permute-start | bytes 344072 | tf_op jit(solution)/shard_map/gather_proj/ppermute | solution.py:22
  22.6 6.4 %collective-permute-start.5 = (bf16[80,896]{1,0:T(8,128)(2,1)S(1)}, bf16[80,896]{1,0:T(8,128)(2,1)S(1)}, u32[]{:S(2)}, u32[]{:S(2)}) collective-permute-start(bf16[80,896]{1,0:T(8,128)(2,1)S(1)} %slice.55), channel_id=1, source_target_pairs={{0,96},{16,112},{32,64},{48,80},{64,32},{80,48},{96,0},{112,16},{1... | collective-permute-start | bytes 430088 | tf_op jit(solution)/shard_map/gather_proj/ppermute | solution.py:22
  24.3 11.3 %collective-permute-start = (bf16[144,896]{1,0:T(8,128)(2,1)S(1)}, bf16[144,896]{1,0:T(8,128)(2,1)S(1)}, u32[]{:S(2)}, u32[]{:S(2)}) collective-permute-start(bf16[144,896]{1,0:T(8,128)(2,1)S(1)} %maximum_maximum_fusion.refs_0_), channel_id=1, source_target_pairs={{0,16},{16,0},{32,48},{48,32},{64,80},{80,64},{96,112},{112,96},{1... | collective-permute-start | bytes 774152 | tf_op jit(solution)/shard_map/gather_proj/ppermute | solution.py:22
  24.3 12.0 %collective-permute-start.2 = (bf16[144,896]{1,0:T(8,128)(2,1)S(1)}, bf16[144,896]{1,0:T(8,128)(2,1)S(1)}, u32[]{:S(2)}, u32[]{:S(2)}) collective-permute-start(bf16[144,896]{1,0:T(8,128)(2,1)S(1)} %collective-permute-done.1.refs_2_), channel_id=1, source_target_pairs={{0,16},{16,0},{32,48},{48,32},{64,80},{80,64},{96,112},{112,96},{1... | collective-permute-start | bytes 774152 | tf_op jit(solution)/shard_map/gather_proj/ppermute | solution.py:22
  24.8 12.1 %collective-permute-start.7 = (bf16[144,896]{1,0:T(8,128)(2,1)S(1)}, bf16[144,896]{1,0:T(8,128)(2,1)S(1)}, u32[]{:S(2)}, u32[]{:S(2)}) collective-permute-start(bf16[144,896]{1,0:T(8,128)(2,1)S(1)} %collective-permute-done.3.refs_6_), channel_id=1, source_target_pairs={{0,16},{16,0},{32,48},{48,32},{64,80},{80,64},{96,112},{112,96},{1... | collective-permute-start | bytes 774152 | tf_op jit(solution)/shard_map/gather_proj/ppermute | solution.py:22
  29.0 8.7 %collective-permute-start.6 = (bf16[144,896]{1,0:T(8,128)(2,1)S(1)}, bf16[144,896]{1,0:T(8,128)(2,1)S(1)}, u32[]{:S(2)}, u32[]{:S(2)}) collective-permute-start(bf16[144,896]{1,0:T(8,128)(2,1)S(1)} %constant_dynamic-update-slice_fusion.refs_4_), channel_id=1, source_target_pairs={{0,16},{16,0},{32,48},{48,32},{64,80},{80,64},{96,112},{112,96},{1... | collective-permute-start | bytes 774152 | tf_op jit(solution)/shard_map/gather_proj/ppermute | solution.py:22
  30.8 15.5 %all-to-all-start = ((bf16[8,16,896]{2,1,0:T(8,128)(2,1)}), bf16[8,16,896]{2,1,0:T(8,128)(2,1)}, u32[]{:S(2)}, u32[]{:S(2)}) async-start(bf16[8,16,896]{2,1,0:T(8,128)(2,1)} %copy.79), calls=%async_computation | async-start | bytes 458752 | tf_op jit(solution)/shard_map/spread_hidden/all_to_all | solution.py:409
  35.4 136.0 %all-gather.5.cloned.1.call-start = ((), (), s32[]{:S(2)}) async-start(), calls=%async_computation.7 | async-start | bytes 3899392 | tf_op jit(solution)/shard_map/spread_hidden/all_gather | solution.py:411
  35.6 0.7 copy-start.12
  37.0 0.7 copy-start.16
  38.4 0.9 copy-start.13
  39.3 1.1 copy-start.15
  40.4 1.0 copy-start.17
  41.4 1.0 copy-start.19
  42.3 2.0 copy-start.24
  76.1 152.0 %reduce-scatter.2.cloned.1.call-start = ((), (), s32[]{:S(2)}) async-start(), calls=%async_computation.8 | async-start | bytes 7483392 | tf_op jit(solution)/shard_map/mid_tail_grads/reduce_scatter | solution.py:501
  82.0 4.3 %copy-start.27 = (s32[256]{0:T(256)S(1)}, s32[256]{0:T(256)}, u32[]{:S(2)}) copy-start(s32[256]{0:T(256)} %param.20) | copy-start | bytes 3076
  88.1 3.2 %copy-start.2 = (bf16[256,2304]{1,0:T(8,128)(2,1)S(1)}, bf16[256,2304]{1,0:T(8,128)(2,1)}, u32[]{:S(2)}) copy-start(bf16[256,2304]{1,0:T(8,128)(2,1)} %target_tail.3) | copy-start | bytes 3538948
  91.3 1.3 copy-start.3
  92.5 1.1 copy-start.4
  93.6 0.9 copy-start.6
  94.6 33.2 %copy-start.5 = (bf16[256,1280]{1,0:T(8,128)(2,1)S(1)}, bf16[256,1280]{1,0:T(8,128)(2,1)}, u32[]{:S(2)}) copy-start(bf16[256,1280]{1,0:T(8,128)(2,1)} %target_mid.3) | copy-start | bytes 1966084
  94.6 33.2 %copy-start.7 = (bf16[256,512]{1,0:T(8,128)(2,1)S(1)}, bf16[256,512]{1,0:T(8,128)(2,1)}, u32[]{:S(2)}) copy-start(bf16[256,512]{1,0:T(8,128)(2,1)} %target_head.3) | copy-start | bytes 786436
  111.6 0.8 copy-start.10
  127.8 1.0 copy-start.11
  139.2 0.7 copy-start.8
  144.5 4.5 %copy-start.9 = (bf16[256,512]{1,0:T(8,128)(2,1)S(1)}, bf16[256,512]{1,0:T(8,128)(2,1)}, u32[]{:S(2)}) copy-start(bf16[256,512]{1,0:T(8,128)(2,1)} %copy-done.8) | copy-start | bytes 786436
  144.5 25.4 %all-to-all-start.3 = ((bf16[16,144,256]{2,1,0:T(8,128)(2,1)}), bf16[16,144,256]{2,1,0:T(8,128)(2,1)}, u32[]{:S(2)}, u32[]{:S(2)}) async-start(bf16[16,144,256]{2,1,0:T(8,128)(2,1)} %get-tuple-element.69), calls=%async_computation.3 | async-start | bytes 2359296 | tf_op jit(solution)/shard_map/code_grads/all_to_all | solution.py:490
  149.1 9.5 %collective-permute-start.11 = (bf16[16,16,512]{2,1,0:T(8,128)(2,1)S(1)}, bf16[16,16,512]{2,1,0:T(8,128)(2,1)S(1)}, u32[]{:S(2)}, u32[]{:S(2)}) collective-permute-start(bf16[16,16,512]{2,1,0:T(8,128)(2,1)S(1)} %bitcast.80), channel_id=1, source_target_pairs={{0,96},{16,112},{32,64},{48,80},{64,32},{80,48},{96,0},{112,16},{1... | collective-permute-start | bytes 786440 | tf_op jit(solution)/shard_map/head_grad/ppermute | solution.py:22
  150.4 9.4 %collective-permute-start.9 = (bf16[16,16,512]{2,1,0:T(8,128)(2,1)S(1)}, bf16[16,16,512]{2,1,0:T(8,128)(2,1)S(1)}, u32[]{:S(2)}, u32[]{:S(2)}) collective-permute-start(bf16[16,16,512]{2,1,0:T(8,128)(2,1)S(1)} %bitcast.81), channel_id=1, source_target_pairs={{0,32},{16,48},{32,0},{48,16},{64,96},{80,112},{96,64},{112,80},{1... | collective-permute-start | bytes 786440 | tf_op jit(solution)/shard_map/head_grad/ppermute | solution.py:22
  158.6 6.4 %collective-permute-start.12 = (bf16[8,16,512]{2,1,0:T(8,128)(2,1)S(1)}, bf16[8,16,512]{2,1,0:T(8,128)(2,1)S(1)}, u32[]{:S(2)}, u32[]{:S(2)}) collective-permute-start(bf16[8,16,512]{2,1,0:T(8,128)(2,1)S(1)} %slice.60), channel_id=1, source_target_pairs={{0,32},{16,48},{32,0},{48,16},{64,96},{80,112},{96,64},{112,80},{1... | collective-permute-start | bytes 393224 | tf_op jit(solution)/shard_map/head_grad/ppermute | solution.py:22
  159.7 7.7 %collective-permute-start.13 = (bf16[8,16,512]{2,1,0:T(8,128)(2,1)S(1)}, bf16[8,16,512]{2,1,0:T(8,128)(2,1)S(1)}, u32[]{:S(2)}, u32[]{:S(2)}) collective-permute-start(bf16[8,16,512]{2,1,0:T(8,128)(2,1)S(1)} %slice.61), channel_id=1, source_target_pairs={{0,96},{16,112},{32,64},{48,80},{64,32},{80,48},{96,0},{112,16},{1... | collective-permute-start | bytes 393224 | tf_op jit(solution)/shard_map/head_grad/ppermute | solution.py:22
  162.4 5.2 %collective-permute-start.8 = (bf16[16,16,512]{2,1,0:T(8,128)(2,1)S(1)}, bf16[16,16,512]{2,1,0:T(8,128)(2,1)S(1)}, u32[]{:S(2)}, u32[]{:S(2)}) collective-permute-start(bf16[16,16,512]{2,1,0:T(8,128)(2,1)S(1)} %bitcast.82), channel_id=1, source_target_pairs={{0,16},{16,0},{32,48},{48,32},{64,80},{80,64},{96,112},{112,96},{1... | collective-permute-start | bytes 786440 | tf_op jit(solution)/shard_map/head_grad/ppermute | solution.py:22
  162.4 5.2 %collective-permute-start.10 = (bf16[16,16,512]{2,1,0:T(8,128)(2,1)S(1)}, bf16[16,16,512]{2,1,0:T(8,128)(2,1)S(1)}, u32[]{:S(2)}, u32[]{:S(2)}) collective-permute-start(bf16[16,16,512]{2,1,0:T(8,128)(2,1)S(1)} %collective-permute-done.9.refs_2_), channel_id=1, source_target_pairs={{0,16},{16,0},{32,48},{48,32},{64,80},{80,64},{96,112},{112,96},{1... | collective-permute-start | bytes 786440 | tf_op jit(solution)/shard_map/head_grad/ppermute | solution.py:22
  162.9 4.7 %collective-permute-start.15 = (bf16[16,16,512]{2,1,0:T(8,128)(2,1)S(1)}, bf16[16,16,512]{2,1,0:T(8,128)(2,1)S(1)}, u32[]{:S(2)}, u32[]{:S(2)}) collective-permute-start(bf16[16,16,512]{2,1,0:T(8,128)(2,1)S(1)} %collective-permute-done.11.refs_6_), channel_id=1, source_target_pairs={{0,16},{16,0},{32,48},{48,32},{64,80},{80,64},{96,112},{112,96},{1... | collective-permute-start | bytes 786440 | tf_op jit(solution)/shard_map/head_grad/ppermute | solution.py:22
  167.5 1.6 collective-permute-start.14
  172.3 33.5 %all-to-all-start.4 = ((bf16[8,256,144]{1,2,0:T(8,128)(2,1)}), bf16[8,256,144]{1,2,0:T(8,128)(2,1)}, u32[]{:S(2)}, u32[]{:S(2)}) async-start(bf16[8,256,144]{1,2,0:T(8,128)(2,1)} %broadcast_in_dim.37), calls=%async_computation.4 | async-start | bytes 1179648 | tf_op jit(solution)/shard_map/head_proj_grads/all_to_all | solution.py:528
  176.5 17.4 %copy-start.28 = (bf16[16,128,896]{2,1,0:T(8,128)(2,1)S(1)}, bf16[16,128,896]{2,1,0:T(8,128)(2,1)}, u32[]{:S(2)}) copy-start(bf16[16,128,896]{2,1,0:T(8,128)(2,1)} %all-gather.5.cloned.1.call-done) | copy-start | bytes 11010052
  188.0 9.2 %collective-permute-start.16 = (bf16[2,224,256]{2,1,0:T(8,128)(2,1)S(1)}, bf16[2,224,256]{2,1,0:T(8,128)(2,1)S(1)}, u32[]{:S(2)}, u32[]{:S(2)}) collective-permute-start(bf16[2,224,256]{2,1,0:T(8,128)(2,1)S(1)} %get-tuple-element.72), channel_id=1, source_target_pairs={{0,12},{1,13},{2,14},{3,15},{4,8},{5,9},{6,10},{7,11},{8,4},{9,5},... | collective-permute-start | bytes 688136 | tf_op jit(solution)/shard_map/hidden_grad_sum/ppermute | solution.py:22
  190.7 7.6 %collective-permute-start.17 = (bf16[2,224,256]{2,1,0:T(8,128)(2,1)S(1)}, bf16[2,224,256]{2,1,0:T(8,128)(2,1)S(1)}, u32[]{:S(2)}, u32[]{:S(2)}) collective-permute-start(bf16[2,224,256]{2,1,0:T(8,128)(2,1)S(1)} %get-tuple-element.80), channel_id=1, source_target_pairs={{0,4},{1,5},{2,6},{3,7},{4,0},{5,1},{6,2},{7,3},{8,12},{9,13},{10,... | collective-permute-start | bytes 688136 | tf_op jit(solution)/shard_map/hidden_grad_sum/ppermute | solution.py:22
  191.0 8.5 %collective-permute-start.18 = (bf16[2,224,256]{2,1,0:T(8,128)(2,1)S(1)}, bf16[2,224,256]{2,1,0:T(8,128)(2,1)S(1)}, u32[]{:S(2)}, u32[]{:S(2)}) collective-permute-start(bf16[2,224,256]{2,1,0:T(8,128)(2,1)S(1)} %get-tuple-element.82), channel_id=1, source_target_pairs={{0,3},{1,2},{2,1},{3,0},{4,7},{5,6},{6,5},{7,4},{8,11},{9,10},{10,... | collective-permute-start | bytes 688136 | tf_op jit(solution)/shard_map/hidden_grad_sum/ppermute | solution.py:22
  193.6 7.0 %collective-permute-start.19 = (bf16[2,224,256]{2,1,0:T(8,128)(2,1)S(1)}, bf16[2,224,256]{2,1,0:T(8,128)(2,1)S(1)}, u32[]{:S(2)}, u32[]{:S(2)}) collective-permute-start(bf16[2,224,256]{2,1,0:T(8,128)(2,1)S(1)} %get-tuple-element.84), channel_id=1, source_target_pairs={{0,1},{1,0},{2,3},{3,2},{4,5},{5,4},{6,7},{7,6},{8,9},{9,8},{10,11... | collective-permute-start | bytes 688136 | tf_op jit(solution)/shard_map/hidden_grad_sum/ppermute | solution.py:22
  201.8 11.2 %collective-permute-start.20 = (bf16[4,224,256]{2,1,0:T(8,128)(2,1)}, bf16[4,224,256]{2,1,0:T(8,128)(2,1)S(1)}, u32[]{:S(2)}, u32[]{:S(2)}) collective-permute-start(bf16[4,224,256]{2,1,0:T(8,128)(2,1)} %get-tuple-element.85), channel_id=1, source_target_pairs={{0,4},{1,5},{2,6},{3,7},{4,0},{5,1},{6,2},{7,3},{8,12},{9,13},{10,... | collective-permute-start | bytes 1376264 | tf_op jit(solution)/shard_map/hidden_grad_sum/ppermute | solution.py:22
  203.5 12.2 %collective-permute-start.21 = (bf16[4,224,256]{2,1,0:T(8,128)(2,1)}, bf16[4,224,256]{2,1,0:T(8,128)(2,1)S(1)}, u32[]{:S(2)}, u32[]{:S(2)}) collective-permute-start(bf16[4,224,256]{2,1,0:T(8,128)(2,1)} %get-tuple-element.86), channel_id=1, source_target_pairs={{0,12},{1,13},{2,14},{3,15},{4,8},{5,9},{6,10},{7,11},{8,4},{9,5},... | collective-permute-start | bytes 1376264 | tf_op jit(solution)/shard_map/hidden_grad_sum/ppermute | solution.py:22
  204.3 11.4 %collective-permute-start.22 = (bf16[4,224,256]{2,1,0:T(8,128)(2,1)S(1)}, bf16[4,224,256]{2,1,0:T(8,128)(2,1)S(1)}, u32[]{:S(2)}, u32[]{:S(2)}) collective-permute-start(bf16[4,224,256]{2,1,0:T(8,128)(2,1)S(1)} %get-tuple-element.88), channel_id=1, source_target_pairs={{0,1},{1,0},{2,3},{3,2},{4,5},{5,4},{6,7},{7,6},{8,9},{9,8},{10,11... | collective-permute-start | bytes 1376264 | tf_op jit(solution)/shard_map/hidden_grad_sum/ppermute | solution.py:22
  204.6 11.6 %collective-permute-start.23 = (bf16[4,224,256]{2,1,0:T(8,128)(2,1)S(1)}, bf16[4,224,256]{2,1,0:T(8,128)(2,1)}, u32[]{:S(2)}, u32[]{:S(2)}) collective-permute-start(bf16[4,224,256]{2,1,0:T(8,128)(2,1)S(1)} %get-tuple-element.89), channel_id=1, source_target_pairs={{0,3},{1,2},{2,1},{3,0},{4,7},{5,6},{6,5},{7,4},{8,11},{9,10},{10,... | collective-permute-start | bytes 1376264 | tf_op jit(solution)/shard_map/hidden_grad_sum/ppermute | solution.py:22
  216.2 2.2 copy-start.29
  217.7 9.5 %collective-permute-start.24 = (bf16[224,256]{1,0:T(8,128)(2,1)S(1)}, bf16[224,256]{1,0:T(8,128)(2,1)S(1)}, u32[]{:S(2)}, u32[]{:S(2)}) collective-permute-start(bf16[224,256]{1,0:T(8,128)(2,1)S(1)} %get-tuple-element.100), channel_id=1, source_target_pairs={{0,1},{1,0},{2,3},{3,2},{4,5},{5,4},{6,7},{7,6},{8,9},{9,8},{10,11... | collective-permute-start | bytes 344072 | tf_op jit(solution)/shard_map/hidden_grad_sum/ppermute | solution.py:22
  219.2 12.3 %collective-permute-start.25 = (bf16[224,256]{1,0:T(8,128)(2,1)S(1)}, bf16[224,256]{1,0:T(8,128)(2,1)S(1)}, u32[]{:S(2)}, u32[]{:S(2)}) collective-permute-start(bf16[224,256]{1,0:T(8,128)(2,1)S(1)} %get-tuple-element.101), channel_id=1, source_target_pairs={{0,2},{1,3},{2,0},{3,1},{4,6},{5,7},{6,4},{7,5},{8,10},{9,11},{10,... | collective-permute-start | bytes 344072 | tf_op jit(solution)/shard_map/hidden_grad_sum/ppermute | solution.py:22
  221.9 9.6 %collective-permute-start.26 = (bf16[224,256]{1,0:T(8,128)(2,1)S(1)}, bf16[224,256]{1,0:T(8,128)(2,1)S(1)}, u32[]{:S(2)}, u32[]{:S(2)}) collective-permute-start(bf16[224,256]{1,0:T(8,128)(2,1)S(1)} %get-tuple-element.102), channel_id=1, source_target_pairs={{0,3},{1,2},{2,1},{3,0},{4,7},{5,6},{6,5},{7,4},{8,11},{9,10},{10,... | collective-permute-start | bytes 344072 | tf_op jit(solution)/shard_map/hidden_grad_sum/ppermute | solution.py:22
  223.4 8.1 %collective-permute-start.27 = (bf16[224,256]{1,0:T(8,128)(2,1)S(1)}, bf16[224,256]{1,0:T(8,128)(2,1)S(1)}, u32[]{:S(2)}, u32[]{:S(2)}) collective-permute-start(bf16[224,256]{1,0:T(8,128)(2,1)S(1)} %get-tuple-element.104), channel_id=1, source_target_pairs={{0,4},{1,5},{2,6},{3,7},{4,0},{5,1},{6,2},{7,3},{8,12},{9,13},{10,... | collective-permute-start | bytes 344072 | tf_op jit(solution)/shard_map/hidden_grad_sum/ppermute | solution.py:22
  223.6 7.9 %collective-permute-start.28 = (bf16[224,256]{1,0:T(8,128)(2,1)S(1)}, bf16[224,256]{1,0:T(8,128)(2,1)S(1)}, u32[]{:S(2)}, u32[]{:S(2)}) collective-permute-start(bf16[224,256]{1,0:T(8,128)(2,1)S(1)} %get-tuple-element.105), channel_id=1, source_target_pairs={{0,8},{1,9},{2,10},{3,11},{4,12},{5,13},{6,14},{7,15},{8,0},{9,1},... | collective-permute-start | bytes 344072 | tf_op jit(solution)/shard_map/hidden_grad_sum/ppermute | solution.py:22
  227.2 6.0 %collective-permute-start.29 = (bf16[224,256]{1,0:T(8,128)(2,1)S(1)}, bf16[224,256]{1,0:T(8,128)(2,1)S(1)}, u32[]{:S(2)}, u32[]{:S(2)}) collective-permute-start(bf16[224,256]{1,0:T(8,128)(2,1)S(1)} %get-tuple-element.106), channel_id=1, source_target_pairs={{0,12},{1,13},{2,14},{3,15},{4,8},{5,9},{6,10},{7,11},{8,4},{9,5},... | collective-permute-start | bytes 344072 | tf_op jit(solution)/shard_map/hidden_grad_sum/ppermute | solution.py:22
  228.1 1.1 copy-start.21
  233.2 1.0 copy-start.1
  (2 other events, 1.4 us)
Sparse Core Ops, SparseCore 0:
  11.9 78.1 all-gather.2
  92.2 50.5 all-gather.4
  145.2 53.7 reduce-scatter.1

commit v4 on v3

--- a/solution.py
+++ b/solution.py
@@ -74,7 +74,7 @@
     return both_cores([block, near, far, other], axis)
 
 
-def in_vmem(kernel, out_shape, *operands, in_specs=None, scratch_shapes=(), flops=2 * 10**9):
+def in_vmem(kernel, out_shape, *operands, in_specs=None, out_specs=None, scratch_shapes=(), mib=16):
     outs = out_shape if isinstance(out_shape, tuple) else (out_shape,)
     size = sum(a.size * a.dtype.itemsize for a in operands + outs)
     specs = in_specs or [pl.BlockSpec(memory_space=pltpu.VMEM)] * len(operands)
@@ -82,16 +82,17 @@
         kernel,
         out_shape=out_shape,
         in_specs=specs,
+        out_specs=out_specs or jax.tree.map(lambda _: pl.BlockSpec(memory_space=pltpu.VMEM), out_shape),
         scratch_shapes=scratch_shapes,
-        compiler_params=pltpu.CompilerParams(vmem_limit_bytes=48 << 20),
-        cost_estimate=pl.CostEstimate(flops=flops, bytes_accessed=size, transcendentals=0),
+        compiler_params=pltpu.CompilerParams(vmem_limit_bytes=mib << 20),
+        cost_estimate=pl.CostEstimate(flops=2 * 10**9, bytes_accessed=size, transcendentals=0),
     )(*operands)
 
 
-def fetch(source, held, sems, spans, base=0):
+def fetch(source, held, sems, spans, base=0, first=0):
     copies = [
         pltpu.make_async_copy(
-            source.at[:, pl.ds(start, size)], held.at[:, pl.ds(start - base, size)], sems.at[k]
+            source.at[:, pl.ds(start, size)], held.at[:, pl.ds(start - base, size)], sems.at[first + k]
         )
         for k, (start, size) in enumerate(spans)
     ]
@@ -130,7 +131,8 @@
     tail_ref[...] = packed_ref[:, start : start + size]
 
 
-ROWS = 16
+ROWS = 32
+UNROLL = 2
 
 
 def row_blocks(rows, body):
@@ -138,19 +140,54 @@
         body(pl.ds(pl.multiple_of(k * ROWS, ROWS), ROWS))
         return carry
 
-    lax.fori_loop(0, rows // ROWS, step, 0)
+    lax.fori_loop(0, rows // ROWS, step, 0, unroll=UNROLL)
 
 
 def hits_of(base, position, shape):
     return position - base == lax.broadcasted_iota(jnp.int32, shape, 1)
 
 
+def add_statistics(bases_ref, tiers, position_ref, stats_ref, block, first):
+    pairs = [(k, s[block, :], t[block, :].astype(F32)) for k, s, t in tiers]
+    position = position_ref[block, :]
+    old = stats_ref[block, :]
+    column = [old[:, k : k + 1] for k in range(6)]
+    top_s, top_t = (None, None) if first else column[:2]
+    for _, s, t in pairs:
+        here_s, here_t = (jnp.max(a, axis=1, keepdims=True) for a in (s, t))
+        top_s = here_s if top_s is None else jnp.maximum(top_s, here_s)
+        top_t = here_t if top_t is None else jnp.maximum(top_t, here_t)
+    if first:
+        mass_s = mass_t = cross = picked = jnp.zeros_like(top_s)
+    else:
+        scale_s, scale_t = jnp.exp(column[0] - top_s), jnp.exp(column[1] - top_t)
+        mass_s, mass_t, cross = column[2] * scale_s, column[3] * scale_t, column[4] * scale_t
+        picked = column[5]
+    for k, s, t in pairs:
+        hit = hits_of(bases_ref[k], position, s.shape)
+        weight = jnp.exp(t - top_t)
+        mass_s += jnp.sum(jnp.exp(s - top_s), axis=1, keepdims=True)
+        mass_t += jnp.sum(weight, axis=1, keepdims=True)
+        cross += jnp.sum(weight * (t - s), axis=1, keepdims=True)
+        picked += jnp.sum(jnp.where(hit, s, 0.0), axis=1, keepdims=True)
+    lane = lax.broadcasted_iota(jnp.int32, (ROWS, stats_ref.shape[1]), 1)
+    out = jnp.zeros(lane.shape, F32)
+    for k, value in enumerate((top_s, top_t, mass_s, mass_t, cross, picked)):
+        out = jnp.where(lane == k, value, out)
+    stats_ref[block, :] = out
+
+
 def forward_kernel(
-    spans, quarters, ranks, bases_ref, w_any, codes_ref, hidden_ref, position_ref,
+    spans, quarters, ranks, bases_ref, w_any, codes_ref, hidden_any, position_ref,
     target_head, target_mid, target_tail,
-    z_ref, head_ref, mid_ref, tail_ref, stats_ref, w_ref, sems,
+    z_ref, head_any, mid_any, tail_any, stats_ref,
+    w_ref, hidden_ref, head_ref, mid_ref, tail_ref, sems, out_sems,
 ):
-    copies = fetch(w_any, w_ref, sems, spans)
+    low = quarters + 1
+    copies = fetch(w_any, w_ref, sems, spans[:low])
+    hidden_copy = pltpu.make_async_copy(hidden_any, hidden_ref, out_sems.at[3])
+    hidden_copy.start()
+    copies += fetch(w_any, w_ref, sems, spans[low:], first=low)
     rank_mid, rank_tail = ranks
     n_dp, per = 2 * codes_ref.shape[0] // quarters, quarters // 2
     depth = rank_mid // per
@@ -163,43 +200,41 @@
     z_ref[quarters] = jnp.concatenate(
         [code[rank_mid : rank_mid + rank_tail] for code in codes], axis=0
     ).astype(BF16)
-    for k, (start, size) in enumerate(spans):
+
+    def weight(k):
         copies[k].wait()
-        weight = w_ref[:, start : start + size]
-        if k < quarters:
-            part = dot(z_ref[k], weight, 0, 0)
-            mid_ref[...] = part if k == 0 else mid_ref[...] + part
-        elif k == quarters:
-            tail_ref[...] = dot(z_ref[k], weight, 0, 0)
-        else:
-            part = dot(hidden_ref[k - quarters - 1], weight, 0, 0)
-            head_ref[...] = part if k == quarters + 1 else head_ref[...] + part
-
-    tiers = ((head_ref, target_head), (mid_ref, target_mid), (tail_ref, target_tail))
-
-    def body(block):
-        pairs = [(s[block, :], t[block, :].astype(F32)) for s, t in tiers]
-        position = position_ref[block, :]
-        top_s = top_t = None
-        for s, t in pairs:
-            here_s, here_t = (jnp.max(a, axis=1, keepdims=True) for a in (s, t))
-            top_s = here_s if top_s is None else jnp.maximum(top_s, here_s)
-            top_t = here_t if top_t is None else jnp.maximum(top_t, here_t)
-        mass_s = mass_t = cross = picked = jnp.zeros_like(top_s)
-        for k, (s, t) in enumerate(pairs):
-            hit = hits_of(bases_ref[k], position, s.shape)
-            weight = jnp.exp(t - top_t)
-            mass_s += jnp.sum(jnp.exp(s - top_s), axis=1, keepdims=True)
-            mass_t += jnp.sum(weight, axis=1, keepdims=True)
-            cross += jnp.sum(weight * (t - s), axis=1, keepdims=True)
-            picked += jnp.sum(jnp.where(hit, s, 0.0), axis=1, keepdims=True)
-        lane = lax.broadcasted_iota(jnp.int32, (ROWS, stats_ref.shape[1]), 1)
-        out = jnp.zeros(lane.shape, F32)
-        for k, value in enumerate((top_s, top_t, mass_s, mass_t, cross, picked)):
-            out = jnp.where(lane == k, value, out)
-        stats_ref[block, :] = out
-
-    row_blocks(head_ref.shape[0], body)
+        return w_ref[:, spans[k][0] : spans[k][0] + spans[k][1]]
+
+    outs = [
+        pltpu.make_async_copy(ref, out, out_sems.at[k])
+        for k, (ref, out) in enumerate(
+            ((mid_ref, mid_any), (tail_ref, tail_any), (head_ref, head_any))
+        )
+    ]
+    for q in range(quarters):
+        part = dot(z_ref[q], weight(q), 0, 0)
+        mid_ref[...] = part if q == 0 else mid_ref[...] + part
+    outs[0].start()
+    tail_ref[...] = dot(z_ref[quarters], weight(quarters), 0, 0)
+    outs[1].start()
+    rows = head_ref.shape[0]
+    tiers = ((1, mid_ref, target_mid), (2, tail_ref, target_tail))
+    row_blocks(
+        rows,
+        lambda block: add_statistics(bases_ref, tiers, position_ref, stats_ref, block, True),
+    )
+    hidden_copy.wait()
+    for k in range(low, len(spans)):
+        part = dot(hidden_ref[k - low], weight(k), 0, 0)
+        head_ref[...] = part if k == low else head_ref[...] + part
+    outs[2].start()
+    tiers_head = ((0, head_ref, target_head),)
+    row_blocks(
+        rows,
+        lambda block: add_statistics(bases_ref, tiers_head, position_ref, stats_ref, block, False),
+    )
+    for copy in outs:
+        copy.wait()
 
 
 def backward_kernel(
@@ -240,16 +275,21 @@
         dz_ref[k] = jnp.concatenate(pieces, axis=0).astype(BF16)
 
 
-def weight_grads_kernel(spans, z_ref, mid_ref, tail_ref, out_ref):
+def weight_grads_kernel(spans, z_ref, mid_ref, tail_ref, out_any, out_ref, sems):
+    copies = []
     for q, (start, size) in enumerate(spans):
         grad = tail_ref if q == len(spans) - 1 else mid_ref
-        out_ref[:, start : start + size] = dot(z_ref[q], grad[...], 1, 0).astype(BF16)
-
-
-def hidden_kernel(
-    spans, depth, me_ref, w_any, g_ref, proj_ref, dz_ref,
-    a_own, a_near, a_lo, a_hi, a_other, b_own, b_near, b_lo, b_hi, b_other, out_ref, w_ref, sems,
-):
+        columns = pl.ds(start, size)
+        out_ref[:, columns] = dot(z_ref[q], grad[...], 1, 0).astype(BF16)
+        copies.append(
+            pltpu.make_async_copy(out_ref.at[:, columns], out_any.at[:, columns], sems.at[q])
+        )
+        copies[-1].start()
+    for copy in copies:
+        copy.wait()
+
+
+def hidden_head_kernel(spans, depth, me_ref, w_any, g_ref, out_ref, w_ref, sems):
     copies = fetch(w_any, w_ref, sems, spans, spans[0][0])
     n_out, height, _ = out_ref.shape
     n_dp = w_ref.shape[0] // depth
@@ -264,14 +304,25 @@
             k = j * (n_out // n_dp) + half
             rows = slice(j * depth, (j + 1) * depth)
             head = jnp.concatenate([part[rows] for part in parts], axis=0)
-            out_ref[me_ref[0] ^ k] = (head + dot(proj_ref[k], dz_ref[...], 1, 0)).astype(BF16)
-    cut = height // 2
-    for k in range(4):
-        a_own[k], a_near[k], a_other[k] = (out_ref[4 * z + k, :cut] for z in (0, 1, 3))
-        b_own[k], b_near[k], b_other[k] = (out_ref[4 * k + y, cut:] for y in (0, 1, 3))
-    for k in range(2):
-        a_lo[k], a_hi[k] = out_ref[8 + k, :cut], out_ref[10 + k, :cut]
-        b_lo[k], b_hi[k] = out_ref[4 * k + 2, cut:], out_ref[4 * k + 10, cut:]
+            out_ref[me_ref[0] ^ k] = head.astype(BF16)
+
+
+def hidden_kernel(
+    me_ref, head_ref, proj_ref, dz_ref,
+    a_own, a_near, a_lo, a_hi, a_other, b_own, b_near, b_lo, b_hi, b_other,
+):
+    cut = head_ref.shape[1] // 2
+    a_refs = (a_own, a_near, (a_lo, a_hi), a_other)
+    b_refs = (b_own, b_near, (b_lo, b_hi), b_other)
+    for flip in range(head_ref.shape[0]):
+        proj = proj_ref[me_ref[0] ^ flip]
+        term = (head_ref[flip].astype(F32) + dot(proj, dz_ref[...], 1, 0)).astype(BF16)
+        z, y = flip // 4, flip % 4
+        for refs, chunk, k, part in ((a_refs, z, y, term[:cut]), (b_refs, y, z, term[cut:])):
+            if chunk == 2:
+                refs[2][k // 2][k % 2] = part
+            else:
+                refs[chunk][k] = part
 
 
 def fold_kernel(*refs):
@@ -299,7 +350,7 @@
 
 def end_kernel(*refs):
     total = jnp.concatenate([total_of(refs[:4]), total_of(refs[4:8])], axis=0)
-    refs[8][...] = total.T.astype(BF16)
+    refs[8][...] = total.astype(BF16)
 
 
 def fold(*rings, beside):
@@ -321,8 +372,11 @@
     ] + [beside]
 
 
-def ring_sums(a, b, early, late):
-    (a_near, a_other), (b_near, b_other), early = fold((*a[1:], 4), (*b[1:], 1), beside=early)
+def ring_sums(a, b, early, dz, middle, late):
+    (a_near, a_other), (b_near, b_other), (early, dz) = fold(
+        (*a[1:], 4), (*b[1:], 1), beside=(early, dz)
+    )
+    middle = middle(dz)
     chunk = a[0].shape[1:]
     out = in_vmem(
         turn_kernel,
@@ -334,11 +388,11 @@
         for step, parts in ((1, out[:4]), (4, out[4:]))
         for flip, part in enumerate(parts)
     ]
-    moved[0], late = lax.optimization_barrier((moved[0], late))
+    moved[0], middle, late = lax.optimization_barrier((moved[0], middle, late))
     total = in_vmem(
-        end_kernel, jax.ShapeDtypeStruct((chunk[1], 2 * chunk[0]), BF16), *moved
-    )
-    return total, early, late
+        end_kernel, jax.ShapeDtypeStruct((2 * chunk[0], chunk[1]), BF16), *moved
+    )
+    return total.T, early, middle, late
 
 
 def spread_vocab(block):
@@ -438,11 +492,18 @@
             target_head,
             target_mid,
             target_tail,
-            in_specs=[smem, anywhere] + [vmem] * 6,
+            in_specs=[smem, anywhere, vmem, anywhere] + [vmem] * 4,
+            out_specs=(vmem, anywhere, anywhere, anywhere, vmem),
             scratch_shapes=[
                 pltpu.VMEM((height, packed_width), BF16),
+                pltpu.VMEM(hidden_t.shape, BF16),
+                pltpu.VMEM((rows, widths[0]), F32),
+                pltpu.VMEM((rows, widths[1]), F32),
+                pltpu.VMEM((rows, widths[2]), F32),
                 pltpu.SemaphoreType.DMA((len(spans),)),
+                pltpu.SemaphoreType.DMA((4,)),
             ],
+            mib=48,
         )
     with jax.named_scope("spread_statistics"):
         stats = spread_vocab(stats[:, :8].T)
@@ -481,10 +542,31 @@
                 pltpu.VMEM((height, low_width), BF16),
                 pltpu.SemaphoreType.DMA((len(low),)),
             ],
+            mib=48,
         )
         x_all = x_all.reshape(n_dp * rows, depth)
+    with jax.named_scope("hidden_head"):
+        me = v.astype(jnp.int32).reshape(1)
+        cut = width // n_vocab // 2
+        head_term = in_vmem(
+            functools.partial(hidden_head_kernel, head_spans, depth_tail),
+            shaped(n_vocab, 2 * cut, rows),
+            me,
+            weights,
+            g_head,
+            in_specs=[smem, anywhere, vmem],
+            scratch_shapes=[
+                pltpu.VMEM((height, packed_width - low_width), BF16),
+                pltpu.SemaphoreType.DMA((len(head_spans),)),
+            ],
+            mib=48,
+        )
     with jax.named_scope("head_grad"):
-        g_all = gather_dp(g_head.reshape(n_vocab, piece, -1), 1, n_vocab // 2)
+        g_rows = g_head.reshape(n_vocab, piece, -1)
+        g_near, g_other = ring_near(g_rows, "dp", 2)
+        g_near, g_other, head_term = lax.optimization_barrier((g_near, g_other, head_term))
+        g_far = ring_far(g_near, g_other, "dp", 2, n_vocab // 2)
+        g_all = both_cores([g_rows, g_near, g_far, g_other], 1)
         g_all = g_all.reshape(n_dp * rows, -1)
     with jax.named_scope("code_grads"):
         dz = lax.all_to_all(dz, "vocab", 0, 0)
@@ -497,6 +579,12 @@
             z,
             g_mid,
             g_tail,
+            out_specs=anywhere,
+            scratch_shapes=[
+                pltpu.VMEM((height, low_width), BF16),
+                pltpu.SemaphoreType.DMA((len(low),)),
+            ],
+            mib=48,
         )
         packed_grad = lax.psum_scatter(packed_grad, "dp", scatter_dimension=0, tiled=True)
         mid_grad, tail_grad = in_vmem(
@@ -505,38 +593,35 @@
             packed_grad,
         )
     with jax.named_scope("hidden_grad"):
-        cut = width // n_vocab // 2
         chunks = [shaped(4, cut, rows)] * 2 + [shaped(2, cut, rows)] * 2 + [shaped(4, cut, rows)]
         pieces = in_vmem(
-            functools.partial(hidden_kernel, head_spans, depth_tail),
+            hidden_kernel,
             tuple(chunks * 2),
-            v.astype(jnp.int32).reshape(1),
-            weights,
-            g_head,
+            me,
+            head_term,
             proj_rows,
             dz,
-            in_specs=[smem, anywhere] + [vmem] * 3,
-            scratch_shapes=[
-                pltpu.VMEM((n_vocab, 2 * cut, rows), BF16),
-                pltpu.VMEM((height, packed_width - low_width), BF16),
-                pltpu.SemaphoreType.DMA((len(head_spans),)),
-            ],
+            in_specs=[smem] + [vmem] * 3,
+            mib=48,
         )
     with jax.named_scope("head_proj_grads"):
         head_grad = dot(x_all, g_all, 0, 0).astype(BF16)
-        dz_all = jnp.broadcast_to(dz.T[None], (n_dp, rows, ranks + pad))
-        dz_all = lax.all_to_all(dz_all, "dp", 0, 0).reshape(n_dp, n_vocab, piece, -1)
-        dz_all = dz_all.transpose(1, 0, 2, 3).reshape(n_dp * rows, -1)
-        proj_grad = dot(x_all, dz_all, 0, 0).astype(BF16)
+
+    def proj_grads(dz):
+        with jax.named_scope("head_proj_grads"):
+            dz_all = jnp.broadcast_to(dz.T[None], (n_dp, rows, ranks + pad))
+            dz_all = lax.all_to_all(dz_all, "dp", 0, 0).reshape(n_dp, n_vocab, piece, -1)
+            dz_all = dz_all.transpose(1, 0, 2, 3).reshape(n_dp * rows, -1)
+            return dot(dz_all, x_all, 0, 0).astype(BF16)
+
     with jax.named_scope("hidden_grad_sum"):
-        hidden_grad, head_grad, late = ring_sums(
-            pieces[:5], pieces[5:], head_grad, (proj_grad, mid_grad, tail_grad)
-        )
-        proj_grad, mid_grad, tail_grad = late
+        hidden_grad, head_grad, proj_grad, (mid_grad, tail_grad) = ring_sums(
+            pieces[:5], pieces[5:], head_grad, dz, proj_grads, (mid_grad, tail_grad)
+        )
     return (
         head_grad,
-        proj_grad[:, :rank_mid],
-        proj_grad[:, rank_mid:ranks],
+        proj_grad[:rank_mid].T,
+        proj_grad[rank_mid:ranks].T,
         mid_grad,
         tail_grad,
         hidden_grad,

time: 242 us -> 234 us (0.967)
  waiting for transfers between devices: 38.4 us -> 31.3 us
  Pallas kernels: 50.1 us -> 46 us
    ppermute x30, waiting for transfers between devices: 38.3 us -> 31.2 us  [swap(): return lax.ppermute(block, axis_name, pairs)]
    pallas_call x9 -> x10, Pallas kernels: 48.4 us -> 44.3 us  [in_vmem(): pl.pallas_call(kernel, out_shape=out_shape, in_specs=specs, out_specs=out...]
    unnamed x65 -> x64, local copies, waits for them, and re-layouts: 25 us -> 25.9 us
  transfers between devices with their start and end apart: 36 -> 36, of which waited for: 17 -> 14; matrix products, arithmetic and copies ran while one was open for 13% -> 15% of each run, Pallas kernels for 20% -> 19%
where the time goes in v4:
time: 234 us; the launch traced here: 233 us
  Pallas kernels  46 us (20%)
  starting transfers between devices  44.4 us (19%)
  local copies, waits for them, and re-layouts  43.8 us (19%)
  blocking collectives  43.1 us (18%)
  waiting for transfers between devices  31.3 us (13%)
  between operations  14.2 us (6%)
  matrix products  7.93 us (3%)
  other arithmetic  2.38 us (1%)
    pallas_call x10, Pallas kernels, in_vmem(): pl.pallas_call(kernel, out_shape=out_shape, in_specs=specs, out_specs=out...  44.3 us
    all_to_all x2, blocking collectives, spread_vocab(): lax.all_to_all(jnp.broadcast_to(block[None], (size,) + block.shape), 'voc...  43.1 us
    ppermute x30, waiting for transfers between devices, swap(): return lax.ppermute(block, axis_name, pairs)  31.2 us
    ppermute x30, starting transfers between devices, swap(): return lax.ppermute(block, axis_name, pairs)  31 us
    unnamed x64, local copies, waits for them, and re-layouts  25.9 us
    dot_general x3, matrix products, dot(): lax.dot_general(left, right, (((left_dim,), (right_dim,)), ((), ())), pre...  7.93 us
  transfers between devices with their start and end apart: 36, of which 14 were waited for; matrix products, arithmetic and copies ran while one was open for 15% of the time, Pallas kernels for 19%

profile of v4, /device:TPU:0, one launch (start us, length us, event | category | flops | bytes accessed | tf_op | source)
XLA Modules:
  0.0 233.1 jit_solution(15509694898171402566)
XLA Ops:
  7.2 1.2 copy-done.21
  8.4 1.1 copy-done.23
  9.5 0.9 copy-done.24
  10.5 1.3 gather_weights.1
  12.0 2.9 %collective-permute-start.3 = (bf16[144,896]{1,0:T(8,128)(2,1)S(1)}, bf16[144,896]{1,0:T(8,128)(2,1)S(1)}, u32[]{:S(2)}, u32[]{:S(2)}) collective-permute-start(bf16[144,896]{1,0:T(8,128)(2,1)S(1)} %maximum_maximum_fusion.refs_0_), channel_id=1, source_target_pairs={{0,96},{16,112},{32,64},{48,80},{64,32},{80,48},{96,0},{112,16},{1... | collective-permute-start | bytes 774152 | tf_op jit(solution)/shard_map/gather_proj/ppermute | solution.py:22
  15.2 6.0 %collective-permute-done.3.refs_6_ = bf16[144,896]{1,0:T(8,128)(2,1)S(1)} collective-permute-done((bf16[144,896]{1,0:T(8,128)(2,1)S(1)}, bf16[144,896]{1,0:T(8,128)(2,1)S(1)}, u32[]{:S(2)}, u32[]{:S(2)}) %collective-permute-start.3) | collective-permute-done | bytes 258080 | tf_op jit(solution)/shard_map/gather_proj/ppermute | solution.py:22
  22.6 1.7 collective-permute-start.5
  24.8 1.2 collective-permute-done.4
  26.0 3.0 %collective-permute-done.5 = bf16[80,896]{1,0:T(8,128)(2,1)S(1)} collective-permute-done((bf16[80,896]{1,0:T(8,128)(2,1)S(1)}, bf16[80,896]{1,0:T(8,128)(2,1)S(1)}, u32[]{:S(2)}, u32[]{:S(2)}) %collective-permute-start.5) | collective-permute-done | bytes 143392 | tf_op jit(solution)/shard_map/gather_proj/ppermute | solution.py:22
  29.1 1.0 constant_dynamic-slice_fusion
  30.8 4.6 %all-to-all-start = ((bf16[8,16,896]{2,1,0:T(8,128)(2,1)}), bf16[8,16,896]{2,1,0:T(8,128)(2,1)}, u32[]{:S(2)}, u32[]{:S(2)}) async-start(bf16[8,16,896]{2,1,0:T(8,128)(2,1)} %copy.74), calls=%async_computation | async-start | bytes 458752 | tf_op jit(solution)/shard_map/spread_hidden/all_to_all | solution.py:463
  38.4 0.9 copy-done.14
  39.3 1.1 copy-done.16
  40.4 1.0 copy-done.18
  41.4 1.0 copy-done.20
  42.3 0.9 gather_proj.1
  43.2 1.1 copy-done.25
  44.4 2.0 convolution_convert_fusion.2
  46.4 1.0 broadcast_in_dim.17
  47.3 28.7 %all_to_all.25.codes_ref = bf16[16,144,256]{2,1,0:T(8,128)(2,1)} all-to-all(bf16[16,144,256]{2,1,0:T(8,128)(2,1)S(1)} %broadcast_in_dim.17), channel_id=1, replica_groups=mesh['dp'=8,'vocab'=16] {'vocab'}, dimensions={0} | all-to-all | bytes 2359296 | tf_op jit(solution)/shard_map/spread_codes/all_to_all | solution.py:400
  76.1 5.9 %copy.75 = bf16[256,7168]{0,1:T(8,128)(2,1)} copy(bf16[256,7168]{1,0:T(8,128)(2,1)} %param.11) | data formatting | bytes 7340032 | tf_op args[0]
  82.0 4.3 %copy.76 = bf16[16,8,56,256]{3,2,1,0:T(8,128)(2,1)} copy(bf16[16,8,56,256]{3,2,0,1:T(8,128)(2,1)} %bitcast.90) | data formatting | bytes 7340032 | tf_op jit(solution)/shard_map/arrange/transpose | solution.py:467
  86.3 1.7 gather_fusion
  88.1 3.0 %copy.77 = bf16[7168,144]{1,0:T(8,128)(2,1)} copy(bf16[7168,144]{0,1:T(8,128)(2,1)S(1)} %bitcast.83) | data formatting | bytes 4128768 | tf_op jit(solution)/shard_map/arrange/transpose | solution.py:469
  91.3 1.3 copy-done.4
  92.5 1.1 copy-done.5
  93.6 0.9 copy-done.7
  94.6 13.5 %logits.1 = (bf16[5,448,256]{2,1,0:T(8,128)(2,1)S(1)}, f32[256,512]{1,0:T(8,128)S(1)}, f32[256,1280]{1,0:T(8,128)}, f32[256,2304]{1,0:T(8,128)}, f32[256,128]{1,0:T(8,128)S(1)}) custom-call(s32[3]{0:T(128)S(1)} %pad_add_fusion.bases_ref, bf16[448,15616]{1,0:T(8,128)(2,1)} %all-gather.3.cloned.1.call-done.w_any, bf16[16,144,256]{2,1,0:T(8,128)(2,1)S(1)} %copy-done.4, ...), custom_call_target="tpu_custom_call" | custom-call | flops 2000000000 | bytes 26412044 | tf_op jit(solution)/shard_map/logits/pallas_call | solution.py:81
  108.9 14.3 %all_to_all.26 = f32[16,8,256]{2,1,0:T(8,128)S(1)} all-to-all(f32[16,8,256]{2,1,0:T(8,128)S(1)} %broadcast_in_dim.36), channel_id=1, replica_groups=mesh['dp'=8,'vocab'=16] {'vocab'}, dimensions={0} | all-to-all | bytes 262144 | tf_op jit(solution)/shard_map/spread_statistics/all_to_all | solution.py:400
  124.2 1.0 copy-done.12
  125.2 9.5 %grad_logits.1 = (bf16[256,512]{1,0:T(8,128)(2,1)S(1)}, bf16[256,1280]{1,0:T(8,128)(2,1)S(1)}, bf16[256,2304]{1,0:T(8,128)(2,1)S(1)}, bf16[16,144,256]{2,1,0:T(8,128)(2,1)}) custom-call(s32[3]{0:T(128)S(1)} %pad_add_fusion.bases_ref, bf16[448,15616]{1,0:T(8,128)(2,1)} %all-gather.3.cloned.1.call-done.w_any, f32[256,2]{1,0:T(8,128)S(1)} %copy.83.lse_ref, ...), custom_call_target="tpu_custom_call" | custom-call | flops 2000000000 | bytes 23563276 | tf_op jit(solution)/shard_map/grad_logits/pallas_call | solution.py:81
  135.4 3.4 %mid_tail_grads.2 = bf16[448,7424]{1,0:T(8,128)(2,1)} custom-call(bf16[5,448,256]{2,1,0:T(8,128)(2,1)S(1)} %get-tuple-element.99.z_ref, bf16[256,1280]{1,0:T(8,128)(2,1)S(1)} %get-tuple-element.100.mid_ref, bf16[256,2304]{1,0:T(8,128)(2,1)S(1)} %get-tuple-element.101.tail_ref), custom_call_target="tpu_custom_call" | custom-call | flops 2000000000 | bytes 9633792 | tf_op jit(solution)/shard_map/mid_tail_grads/pallas_call | solution.py:81
  138.8 4.5 %all-to-all-start.3 = ((bf16[16,144,256]{2,1,0:T(8,128)(2,1)}), bf16[16,144,256]{2,1,0:T(8,128)(2,1)}, u32[]{:S(2)}, u32[]{:S(2)}) async-start(bf16[16,144,256]{2,1,0:T(8,128)(2,1)} %get-tuple-element.74), calls=%async_computation.3 | async-start | bytes 2359296 | tf_op jit(solution)/shard_map/code_grads/all_to_all | solution.py:572
  143.6 2.0 collective-permute-start.9
  145.6 7.9 %hidden_head.1.head_ref = bf16[16,448,256]{2,1,0:T(8,128)(2,1)S(1)} custom-call(s32[1]{0:T(128)} %bitcast.me_ref, bf16[448,15616]{1,0:T(8,128)(2,1)} %all-gather.3.cloned.1.call-done.w_any, bf16[256,512]{1,0:T(8,128)(2,1)S(1)} %copy-done.10), custom_call_target="tpu_custom_call" | custom-call | flops 2000000000 | bytes 17924100 | tf_op jit(solution)/shard_map/hidden_head/pallas_call | solution.py:81
  153.6 1.8 copy-done.2
  156.0 2.0 collective-permute-start.13
  158.5 3.5 %collective-permute-done.12 = bf16[8,16,512]{2,1,0:T(8,128)(2,1)S(1)} collective-permute-done((bf16[8,16,512]{2,1,0:T(8,128)(2,1)S(1)}, bf16[8,16,512]{2,1,0:T(8,128)(2,1)S(1)}, u32[]{:S(2)}, u32[]{:S(2)}) %collective-permute-start.12) | collective-permute-done | bytes 131104 | tf_op jit(solution)/shard_map/head_grad/ppermute | solution.py:22
  162.0 1.7 collective-permute-done.13
  163.8 1.5 collective-permute-done.14.refs_5_
  166.1 1.5 reduce_sum.50.dz_ref
  167.6 4.5 %hidden_grad.1 = (bf16[4,224,256]{2,1,0:T(8,128)(2,1)S(1)}, bf16[4,224,256]{2,1,0:T(8,128)(2,1)S(1)}, bf16[2,224,256]{2,1,0:T(8,128)(2,1)S(1)}, bf16[2,224,256]{...) custom-call(s32[1]{0:T(128)} %bitcast.me_ref, ...), custom_call_target="tpu_custom_call" | custom-call | flops 2000000000 | bytes 9478148 | tf_op jit(solution)/shard_map/hidden_grad/pallas_call | solution.py:81
  172.2 3.1 %collective-permute-start.16 = (bf16[2,224,256]{2,1,0:T(8,128)(2,1)S(1)}, bf16[2,224,256]{2,1,0:T(8,128)(2,1)S(1)}, u32[]{:S(2)}, u32[]{:S(2)}) collective-permute-start(bf16[2,224,256]{2,1,0:T(8,128)(2,1)S(1)} %get-tuple-element.79), channel_id=1, source_target_pairs={{0,12},{1,13},{2,14},{3,15},{4,8},{5,9},{6,10},{7,11},{8,4},{9,5},... | collective-permute-start | bytes 688136 | tf_op jit(solution)/shard_map/hidden_grad_sum/ppermute | solution.py:22
  175.5 2.7 %collective-permute-start.18 = (bf16[2,224,256]{2,1,0:T(8,128)(2,1)S(1)}, bf16[2,224,256]{2,1,0:T(8,128)(2,1)S(1)}, u32[]{:S(2)}, u32[]{:S(2)}) collective-permute-start(bf16[2,224,256]{2,1,0:T(8,128)(2,1)S(1)} %get-tuple-element.89), channel_id=1, source_target_pairs={{0,3},{1,2},{2,1},{3,0},{4,7},{5,6},{6,5},{7,4},{8,11},{9,10},{10,... | collective-permute-start | bytes 688136 | tf_op jit(solution)/shard_map/hidden_grad_sum/ppermute | solution.py:22
  178.4 3.0 %convolution_convert_fusion = bf16[896,512]{1,0:T(8,128)(2,1)} fusion(bf16[2048,896]{1,0:T(8,128)(2,1)S(1)} %bitcast.96, bf16[2048,512]{1,0:T(8,128)(2,1)S(1)} %bitcast.84), kind=kOutput, calls=%fused_computation.1 | convolution fusion | flops 1879506944 | bytes 6684672 | tf_op jit(solution)/shard_map/head_proj_grads/dot_general | solution.py:15
  181.5 1.2 collective-permute-done.17.refs_3_
  182.6 1.2 collective-permute-done.18.refs_5_
  183.8 1.2 collective-permute-done.19.refs_7_
  185.0 1.1 hidden_grad_sum.3
  186.2 1.7 collective-permute-start.20
  188.8 1.2 collective-permute-start.23
  190.9 4.2 %all-to-all-start.4 = ((bf16[8,256,144]{1,2,0:T(8,128)(2,1)}), bf16[8,256,144]{1,2,0:T(8,128)(2,1)}, u32[]{:S(2)}, u32[]{:S(2)}) async-start(bf16[8,256,144]{1,2,0:T(8,128)(2,1)} %broadcast_in_dim.37), calls=%async_computation.4 | async-start | bytes 1179648 | tf_op jit(solution)/shard_map/hidden_grad_sum/head_proj_grads/all_to_all | solution.py:613
  195.1 2.2 collective-permute-done.20.refs_1_
  197.3 2.6 %collective-permute-done.21.refs_2_ = bf16[4,224,256]{2,1,0:T(8,128)(2,1)S(1)} collective-permute-done((bf16[4,224,256]{2,1,0:T(8,128)(2,1)}, bf16[4,224,256]{2,1,0:T(8,128)(2,1)S(1)}, u32[]{:S(2)}, u32[]{:S(2)}) %collective-permute-start.21) | collective-permute-done | bytes 458784 | tf_op jit(solution)/shard_map/hidden_grad_sum/ppermute | solution.py:22
  200.3 1.3 hidden_grad_sum.4
  202.2 2.7 %collective-permute-start.25 = (bf16[224,256]{1,0:T(8,128)(2,1)S(1)}, bf16[224,256]{1,0:T(8,128)(2,1)S(1)}, u32[]{:S(2)}, u32[]{:S(2)}) collective-permute-start(bf16[224,256]{1,0:T(8,128)(2,1)S(1)} %get-tuple-element.109), channel_id=1, source_target_pairs={{0,2},{1,3},{2,0},{3,1},{4,6},{5,7},{6,4},{7,5},{8,10},{9,11},{10,... | collective-permute-start | bytes 344072 | tf_op jit(solution)/shard_map/hidden_grad_sum/ppermute | solution.py:22
  205.0 1.5 collective-permute-start.26
  206.6 3.8 %collective-permute-start.28 = (bf16[224,256]{1,0:T(8,128)(2,1)S(1)}, bf16[224,256]{1,0:T(8,128)(2,1)S(1)}, u32[]{:S(2)}, u32[]{:S(2)}) collective-permute-start(bf16[224,256]{1,0:T(8,128)(2,1)S(1)} %get-tuple-element.113), channel_id=1, source_target_pairs={{0,8},{1,9},{2,10},{3,11},{4,12},{5,13},{6,14},{7,15},{8,0},{9,1},... | collective-permute-start | bytes 344072 | tf_op jit(solution)/shard_map/hidden_grad_sum/ppermute | solution.py:22
  210.4 2.2 copy.85
  212.6 1.3 copy.86
  213.9 2.9 %convolution_convert_fusion.1 = bf16[144,896]{1,0:T(8,128)(2,1)S(1)} fusion(bf16[2048,144]{1,0:T(8,128)(2,1)S(1)} %bitcast.94, bf16[2048,896]{1,0:T(8,128)(2,1)} %bitcast.95), kind=kOutput, calls=%fused_computation.2 | convolution fusion | flops 528611328 | bytes 4517888 | tf_op jit(solution)/shard_map/hidden_grad_sum/head_proj_grads/dot_general | solution.py:15
  216.9 1.1 copy-done.22
  218.0 0.9 mid_tail_grads.3
  221.0 4.6 %collective-permute-done.29.refs_7_ = bf16[224,256]{1,0:T(8,128)(2,1)S(1)} collective-permute-done((bf16[224,256]{1,0:T(8,128)(2,1)S(1)}, bf16[224,256]{1,0:T(8,128)(2,1)S(1)}, u32[]{:S(2)}, u32[]{:S(2)}) %collective-permute-start.29) | collective-permute-done | bytes 114720 | tf_op jit(solution)/shard_map/hidden_grad_sum/ppermute | solution.py:22
  (127 shorter events, 17.8 us)
Async XLA Ops:
  7.2 79.1 %copy-start = (s32[65536]{0:T(1024)S(1)}, s32[65536]{0:T(1024)}, u32[]{:S(2)}) copy-start(s32[65536]{0:T(1024)} %param.21) | copy-start | bytes 786436
  7.2 84.1 %all-gather.3.cloned.1.call-start = ((), (), s32[]{:S(2)}) async-start(), calls=%async_computation.6 | async-start | bytes 15740928 | tf_op jit(solution)/shard_map/gather_weights/all_gather | solution.py:447
  7.2 1.2 copy-start.21
  8.4 1.1 copy-start.23
  9.5 0.9 copy-start.24
  10.5 1.4 copy-start.27
  10.5 1.4 copy-start.28
  12.0 9.1 %collective-permute-start.3 = (bf16[144,896]{1,0:T(8,128)(2,1)S(1)}, bf16[144,896]{1,0:T(8,128)(2,1)S(1)}, u32[]{:S(2)}, u32[]{:S(2)}) collective-permute-start(bf16[144,896]{1,0:T(8,128)(2,1)S(1)} %maximum_maximum_fusion.refs_0_), channel_id=1, source_target_pairs={{0,96},{16,112},{32,64},{48,80},{64,32},{80,48},{96,0},{112,16},{1... | collective-permute-start | bytes 774152 | tf_op jit(solution)/shard_map/gather_proj/ppermute | solution.py:22
  14.9 7.7 %collective-permute-start.1 = (bf16[144,896]{1,0:T(8,128)(2,1)S(1)}, bf16[144,896]{1,0:T(8,128)(2,1)S(1)}, u32[]{:S(2)}, u32[]{:S(2)}) collective-permute-start(bf16[144,896]{1,0:T(8,128)(2,1)S(1)} %maximum_maximum_fusion.refs_0_), channel_id=1, source_target_pairs={{0,32},{16,48},{32,0},{48,16},{64,96},{80,112},{96,64},{112,80},{1... | collective-permute-start | bytes 774152 | tf_op jit(solution)/shard_map/gather_proj/ppermute | solution.py:22
  21.2 4.9 %collective-permute-start.4 = (bf16[64,896]{1,0:T(8,128)(2,1)S(1)}, bf16[64,896]{1,0:T(8,128)(2,1)S(1)}, u32[]{:S(2)}, u32[]{:S(2)}) collective-permute-start(bf16[64,896]{1,0:T(8,128)(2,1)S(1)} %slice.54), channel_id=1, source_target_pairs={{0,32},{16,48},{32,0},{48,16},{64,96},{80,112},{96,64},{112,80},{1... | collective-permute-start | bytes 344072 | tf_op jit(solution)/shard_map/gather_proj/ppermute | solution.py:22
  22.6 6.4 %collective-permute-start.5 = (bf16[80,896]{1,0:T(8,128)(2,1)S(1)}, bf16[80,896]{1,0:T(8,128)(2,1)S(1)}, u32[]{:S(2)}, u32[]{:S(2)}) collective-permute-start(bf16[80,896]{1,0:T(8,128)(2,1)S(1)} %slice.55), channel_id=1, source_target_pairs={{0,96},{16,112},{32,64},{48,80},{64,32},{80,48},{96,0},{112,16},{1... | collective-permute-start | bytes 430088 | tf_op jit(solution)/shard_map/gather_proj/ppermute | solution.py:22
  24.3 11.3 %collective-permute-start = (bf16[144,896]{1,0:T(8,128)(2,1)S(1)}, bf16[144,896]{1,0:T(8,128)(2,1)S(1)}, u32[]{:S(2)}, u32[]{:S(2)}) collective-permute-start(bf16[144,896]{1,0:T(8,128)(2,1)S(1)} %maximum_maximum_fusion.refs_0_), channel_id=1, source_target_pairs={{0,16},{16,0},{32,48},{48,32},{64,80},{80,64},{96,112},{112,96},{1... | collective-permute-start | bytes 774152 | tf_op jit(solution)/shard_map/gather_proj/ppermute | solution.py:22
  24.3 12.0 %collective-permute-start.2 = (bf16[144,896]{1,0:T(8,128)(2,1)S(1)}, bf16[144,896]{1,0:T(8,128)(2,1)S(1)}, u32[]{:S(2)}, u32[]{:S(2)}) collective-permute-start(bf16[144,896]{1,0:T(8,128)(2,1)S(1)} %collective-permute-done.1.refs_2_), channel_id=1, source_target_pairs={{0,16},{16,0},{32,48},{48,32},{64,80},{80,64},{96,112},{112,96},{1... | collective-permute-start | bytes 774152 | tf_op jit(solution)/shard_map/gather_proj/ppermute | solution.py:22
  24.8 12.1 %collective-permute-start.7 = (bf16[144,896]{1,0:T(8,128)(2,1)S(1)}, bf16[144,896]{1,0:T(8,128)(2,1)S(1)}, u32[]{:S(2)}, u32[]{:S(2)}) collective-permute-start(bf16[144,896]{1,0:T(8,128)(2,1)S(1)} %collective-permute-done.3.refs_6_), channel_id=1, source_target_pairs={{0,16},{16,0},{32,48},{48,32},{64,80},{80,64},{96,112},{112,96},{1... | collective-permute-start | bytes 774152 | tf_op jit(solution)/shard_map/gather_proj/ppermute | solution.py:22
  29.0 8.7 %collective-permute-start.6 = (bf16[144,896]{1,0:T(8,128)(2,1)S(1)}, bf16[144,896]{1,0:T(8,128)(2,1)S(1)}, u32[]{:S(2)}, u32[]{:S(2)}) collective-permute-start(bf16[144,896]{1,0:T(8,128)(2,1)S(1)} %constant_dynamic-update-slice_fusion.refs_4_), channel_id=1, source_target_pairs={{0,16},{16,0},{32,48},{48,32},{64,80},{80,64},{96,112},{112,96},{1... | collective-permute-start | bytes 774152 | tf_op jit(solution)/shard_map/gather_proj/ppermute | solution.py:22
  30.8 15.5 %all-to-all-start = ((bf16[8,16,896]{2,1,0:T(8,128)(2,1)}), bf16[8,16,896]{2,1,0:T(8,128)(2,1)}, u32[]{:S(2)}, u32[]{:S(2)}) async-start(bf16[8,16,896]{2,1,0:T(8,128)(2,1)} %copy.74), calls=%async_computation | async-start | bytes 458752 | tf_op jit(solution)/shard_map/spread_hidden/all_to_all | solution.py:463
  35.4 132.2 %all-gather.5.cloned.1.call-start = ((), (), s32[]{:S(2)}) async-start(), calls=%async_computation.7 | async-start | bytes 3899392 | tf_op jit(solution)/shard_map/spread_hidden/all_gather | solution.py:465
  35.6 0.7 copy-start.13
  37.0 0.7 copy-start.17
  38.4 0.9 copy-start.14
  39.3 1.1 copy-start.16
  40.4 1.0 copy-start.18
  41.4 1.0 copy-start.20
  42.3 2.0 copy-start.25
  76.1 140.8 %reduce-scatter.2.cloned.1.call-start = ((), (), s32[]{:S(2)}) async-start(), calls=%async_computation.8 | async-start | bytes 7483392 | tf_op jit(solution)/shard_map/mid_tail_grads/reduce_scatter | solution.py:589
  82.0 4.3 %copy-start.29 = (s32[256]{0:T(256)S(1)}, s32[256]{0:T(256)}, u32[]{:S(2)}) copy-start(s32[256]{0:T(256)} %param.20) | copy-start | bytes 3076
  88.1 3.2 %copy-start.3 = (bf16[256,2304]{1,0:T(8,128)(2,1)S(1)}, bf16[256,2304]{1,0:T(8,128)(2,1)}, u32[]{:S(2)}) copy-start(bf16[256,2304]{1,0:T(8,128)(2,1)} %target_tail.3) | copy-start | bytes 3538948
  91.3 1.3 copy-start.4
  92.5 1.1 copy-start.5
  93.6 0.9 copy-start.7
  94.6 29.6 %copy-start.6 = (bf16[256,1280]{1,0:T(8,128)(2,1)S(1)}, bf16[256,1280]{1,0:T(8,128)(2,1)}, u32[]{:S(2)}) copy-start(bf16[256,1280]{1,0:T(8,128)(2,1)} %target_mid.3) | copy-start | bytes 1966084
  94.6 29.6 %copy-start.8 = (bf16[256,512]{1,0:T(8,128)(2,1)S(1)}, bf16[256,512]{1,0:T(8,128)(2,1)}, u32[]{:S(2)}) copy-start(bf16[256,512]{1,0:T(8,128)(2,1)} %target_head.3) | copy-start | bytes 786436
  108.0 0.8 copy-start.11
  124.2 1.0 copy-start.12
  134.7 0.7 copy-start.9
  138.8 4.5 %copy-start.10 = (bf16[256,512]{1,0:T(8,128)(2,1)S(1)}, bf16[256,512]{1,0:T(8,128)(2,1)}, u32[]{:S(2)}) copy-start(bf16[256,512]{1,0:T(8,128)(2,1)} %copy-done.9) | copy-start | bytes 786436
  138.8 27.3 %all-to-all-start.3 = ((bf16[16,144,256]{2,1,0:T(8,128)(2,1)}), bf16[16,144,256]{2,1,0:T(8,128)(2,1)}, u32[]{:S(2)}, u32[]{:S(2)}) async-start(bf16[16,144,256]{2,1,0:T(8,128)(2,1)} %get-tuple-element.74), calls=%async_computation.3 | async-start | bytes 2359296 | tf_op jit(solution)/shard_map/code_grads/all_to_all | solution.py:572
  143.3 12.0 %collective-permute-start.8 = (bf16[16,16,512]{2,1,0:T(8,128)(2,1)S(1)}, bf16[16,16,512]{2,1,0:T(8,128)(2,1)S(1)}, u32[]{:S(2)}, u32[]{:S(2)}) collective-permute-start(bf16[16,16,512]{2,1,0:T(8,128)(2,1)S(1)} %bitcast.85), channel_id=1, source_target_pairs={{0,32},{16,48},{32,0},{48,16},{64,96},{80,112},{96,64},{112,80},{1... | collective-permute-start | bytes 786440 | tf_op jit(solution)/shard_map/head_grad/ppermute | solution.py:22
  143.6 11.7 %collective-permute-start.9 = (bf16[16,16,512]{2,1,0:T(8,128)(2,1)S(1)}, bf16[16,16,512]{2,1,0:T(8,128)(2,1)S(1)}, u32[]{:S(2)}, u32[]{:S(2)}) collective-permute-start(bf16[16,16,512]{2,1,0:T(8,128)(2,1)S(1)} %bitcast.86), channel_id=1, source_target_pairs={{0,96},{16,112},{32,64},{48,80},{64,32},{80,48},{96,0},{112,16},{1... | collective-permute-start | bytes 786440 | tf_op jit(solution)/shard_map/head_grad/ppermute | solution.py:22
  153.6 1.8 copy-start.2
  155.4 6.6 %collective-permute-start.12 = (bf16[8,16,512]{2,1,0:T(8,128)(2,1)S(1)}, bf16[8,16,512]{2,1,0:T(8,128)(2,1)S(1)}, u32[]{:S(2)}, u32[]{:S(2)}) collective-permute-start(bf16[8,16,512]{2,1,0:T(8,128)(2,1)S(1)} %slice.46), channel_id=1, source_target_pairs={{0,32},{16,48},{32,0},{48,16},{64,96},{80,112},{96,64},{112,80},{1... | collective-permute-start | bytes 393224 | tf_op jit(solution)/shard_map/head_grad/ppermute | solution.py:22
  156.0 7.7 %collective-permute-start.13 = (bf16[8,16,512]{2,1,0:T(8,128)(2,1)S(1)}, bf16[8,16,512]{2,1,0:T(8,128)(2,1)S(1)}, u32[]{:S(2)}, u32[]{:S(2)}) collective-permute-start(bf16[8,16,512]{2,1,0:T(8,128)(2,1)S(1)} %slice.47), channel_id=1, source_target_pairs={{0,96},{16,112},{32,64},{48,80},{64,32},{80,48},{96,0},{112,16},{1... | collective-permute-start | bytes 393224 | tf_op jit(solution)/shard_map/head_grad/ppermute | solution.py:22
  158.0 5.8 %collective-permute-start.10 = (bf16[16,16,512]{2,1,0:T(8,128)(2,1)S(1)}, bf16[16,16,512]{2,1,0:T(8,128)(2,1)S(1)}, u32[]{:S(2)}, u32[]{:S(2)}) collective-permute-start(bf16[16,16,512]{2,1,0:T(8,128)(2,1)S(1)} %bitcast.87), channel_id=1, source_target_pairs={{0,16},{16,0},{32,48},{48,32},{64,80},{80,64},{96,112},{112,96},{1... | collective-permute-start | bytes 786440 | tf_op jit(solution)/shard_map/head_grad/ppermute | solution.py:22
  158.0 5.8 %collective-permute-start.11 = (bf16[16,16,512]{2,1,0:T(8,128)(2,1)S(1)}, bf16[16,16,512]{2,1,0:T(8,128)(2,1)S(1)}, u32[]{:S(2)}, u32[]{:S(2)}) collective-permute-start(bf16[16,16,512]{2,1,0:T(8,128)(2,1)S(1)} %collective-permute-done.8.refs_2_), channel_id=1, source_target_pairs={{0,16},{16,0},{32,48},{48,32},{64,80},{80,64},{96,112},{112,96},{1... | collective-permute-start | bytes 786440 | tf_op jit(solution)/shard_map/head_grad/ppermute | solution.py:22
  158.5 5.3 %collective-permute-start.15 = (bf16[16,16,512]{2,1,0:T(8,128)(2,1)S(1)}, bf16[16,16,512]{2,1,0:T(8,128)(2,1)S(1)}, u32[]{:S(2)}, u32[]{:S(2)}) collective-permute-start(bf16[16,16,512]{2,1,0:T(8,128)(2,1)S(1)} %collective-permute-done.9.refs_6_), channel_id=1, source_target_pairs={{0,16},{16,0},{32,48},{48,32},{64,80},{80,64},{96,112},{112,96},{1... | collective-permute-start | bytes 786440 | tf_op jit(solution)/shard_map/head_grad/ppermute | solution.py:22
  163.7 1.6 collective-permute-start.14
  167.6 10.8 %copy-start.26 = (bf16[16,128,896]{2,1,0:T(8,128)(2,1)S(1)}, bf16[16,128,896]{2,1,0:T(8,128)(2,1)}, u32[]{:S(2)}) copy-start(bf16[16,128,896]{2,1,0:T(8,128)(2,1)} %all-gather.5.cloned.1.call-done) | copy-start | bytes 11010052
  172.2 9.3 %collective-permute-start.16 = (bf16[2,224,256]{2,1,0:T(8,128)(2,1)S(1)}, bf16[2,224,256]{2,1,0:T(8,128)(2,1)S(1)}, u32[]{:S(2)}, u32[]{:S(2)}) collective-permute-start(bf16[2,224,256]{2,1,0:T(8,128)(2,1)S(1)} %get-tuple-element.79), channel_id=1, source_target_pairs={{0,12},{1,13},{2,14},{3,15},{4,8},{5,9},{6,10},{7,11},{8,4},{9,5},... | collective-permute-start | bytes 688136 | tf_op jit(solution)/shard_map/hidden_grad_sum/ppermute | solution.py:22
  175.2 7.4 %collective-permute-start.17 = (bf16[2,224,256]{2,1,0:T(8,128)(2,1)S(1)}, bf16[2,224,256]{2,1,0:T(8,128)(2,1)S(1)}, u32[]{:S(2)}, u32[]{:S(2)}) collective-permute-start(bf16[2,224,256]{2,1,0:T(8,128)(2,1)S(1)} %get-tuple-element.87), channel_id=1, source_target_pairs={{0,4},{1,5},{2,6},{3,7},{4,0},{5,1},{6,2},{7,3},{8,12},{9,13},{10,... | collective-permute-start | bytes 688136 | tf_op jit(solution)/shard_map/hidden_grad_sum/ppermute | solution.py:22
  175.5 8.3 %collective-permute-start.18 = (bf16[2,224,256]{2,1,0:T(8,128)(2,1)S(1)}, bf16[2,224,256]{2,1,0:T(8,128)(2,1)S(1)}, u32[]{:S(2)}, u32[]{:S(2)}) collective-permute-start(bf16[2,224,256]{2,1,0:T(8,128)(2,1)S(1)} %get-tuple-element.89), channel_id=1, source_target_pairs={{0,3},{1,2},{2,1},{3,0},{4,7},{5,6},{6,5},{7,4},{8,11},{9,10},{10,... | collective-permute-start | bytes 688136 | tf_op jit(solution)/shard_map/hidden_grad_sum/ppermute | solution.py:22
  178.2 6.9 %collective-permute-start.19 = (bf16[2,224,256]{2,1,0:T(8,128)(2,1)S(1)}, bf16[2,224,256]{2,1,0:T(8,128)(2,1)S(1)}, u32[]{:S(2)}, u32[]{:S(2)}) collective-permute-start(bf16[2,224,256]{2,1,0:T(8,128)(2,1)S(1)} %get-tuple-element.91), channel_id=1, source_target_pairs={{0,1},{1,0},{2,3},{3,2},{4,5},{5,4},{6,7},{7,6},{8,9},{9,8},{10,11... | collective-permute-start | bytes 688136 | tf_op jit(solution)/shard_map/hidden_grad_sum/ppermute | solution.py:22
  186.2 11.2 %collective-permute-start.20 = (bf16[4,224,256]{2,1,0:T(8,128)(2,1)}, bf16[4,224,256]{2,1,0:T(8,128)(2,1)S(1)}, u32[]{:S(2)}, u32[]{:S(2)}) collective-permute-start(bf16[4,224,256]{2,1,0:T(8,128)(2,1)} %get-tuple-element.92), channel_id=1, source_target_pairs={{0,4},{1,5},{2,6},{3,7},{4,0},{5,1},{6,2},{7,3},{8,12},{9,13},{10,... | collective-permute-start | bytes 1376264 | tf_op jit(solution)/shard_map/hidden_grad_sum/ppermute | solution.py:22
  187.9 12.0 %collective-permute-start.21 = (bf16[4,224,256]{2,1,0:T(8,128)(2,1)}, bf16[4,224,256]{2,1,0:T(8,128)(2,1)S(1)}, u32[]{:S(2)}, u32[]{:S(2)}) collective-permute-start(bf16[4,224,256]{2,1,0:T(8,128)(2,1)} %get-tuple-element.93), channel_id=1, source_target_pairs={{0,12},{1,13},{2,14},{3,15},{4,8},{5,9},{6,10},{7,11},{8,4},{9,5},... | collective-permute-start | bytes 1376264 | tf_op jit(solution)/shard_map/hidden_grad_sum/ppermute | solution.py:22
  188.5 11.4 %collective-permute-start.22 = (bf16[4,224,256]{2,1,0:T(8,128)(2,1)S(1)}, bf16[4,224,256]{2,1,0:T(8,128)(2,1)S(1)}, u32[]{:S(2)}, u32[]{:S(2)}) collective-permute-start(bf16[4,224,256]{2,1,0:T(8,128)(2,1)S(1)} %get-tuple-element.95), channel_id=1, source_target_pairs={{0,1},{1,0},{2,3},{3,2},{4,5},{5,4},{6,7},{7,6},{8,9},{9,8},{10,11... | collective-permute-start | bytes 1376264 | tf_op jit(solution)/shard_map/hidden_grad_sum/ppermute | solution.py:22
  188.8 11.5 %collective-permute-start.23 = (bf16[4,224,256]{2,1,0:T(8,128)(2,1)S(1)}, bf16[4,224,256]{2,1,0:T(8,128)(2,1)}, u32[]{:S(2)}, u32[]{:S(2)}) collective-permute-start(bf16[4,224,256]{2,1,0:T(8,128)(2,1)S(1)} %get-tuple-element.96), channel_id=1, source_target_pairs={{0,3},{1,2},{2,1},{3,0},{4,7},{5,6},{6,5},{7,4},{8,11},{9,10},{10,... | collective-permute-start | bytes 1376264 | tf_op jit(solution)/shard_map/hidden_grad_sum/ppermute | solution.py:22
  190.9 19.6 %all-to-all-start.4 = ((bf16[8,256,144]{1,2,0:T(8,128)(2,1)}), bf16[8,256,144]{1,2,0:T(8,128)(2,1)}, u32[]{:S(2)}, u32[]{:S(2)}) async-start(bf16[8,256,144]{1,2,0:T(8,128)(2,1)} %broadcast_in_dim.37), calls=%async_computation.4 | async-start | bytes 1179648 | tf_op jit(solution)/shard_map/hidden_grad_sum/head_proj_grads/all_to_all | solution.py:613
  201.7 18.0 %collective-permute-start.24 = (bf16[224,256]{1,0:T(8,128)(2,1)S(1)}, bf16[224,256]{1,0:T(8,128)(2,1)S(1)}, u32[]{:S(2)}, u32[]{:S(2)}) collective-permute-start(bf16[224,256]{1,0:T(8,128)(2,1)S(1)} %get-tuple-element.108), channel_id=1, source_target_pairs={{0,1},{1,0},{2,3},{3,2},{4,5},{5,4},{6,7},{7,6},{8,9},{9,8},{10,11... | collective-permute-start | bytes 344072 | tf_op jit(solution)/shard_map/hidden_grad_sum/ppermute | solution.py:22
  202.2 18.8 %collective-permute-start.25 = (bf16[224,256]{1,0:T(8,128)(2,1)S(1)}, bf16[224,256]{1,0:T(8,128)(2,1)S(1)}, u32[]{:S(2)}, u32[]{:S(2)}) collective-permute-start(bf16[224,256]{1,0:T(8,128)(2,1)S(1)} %get-tuple-element.109), channel_id=1, source_target_pairs={{0,2},{1,3},{2,0},{3,1},{4,6},{5,7},{6,4},{7,5},{8,10},{9,11},{10,... | collective-permute-start | bytes 344072 | tf_op jit(solution)/shard_map/hidden_grad_sum/ppermute | solution.py:22
  205.0 16.0 %collective-permute-start.26 = (bf16[224,256]{1,0:T(8,128)(2,1)S(1)}, bf16[224,256]{1,0:T(8,128)(2,1)S(1)}, u32[]{:S(2)}, u32[]{:S(2)}) collective-permute-start(bf16[224,256]{1,0:T(8,128)(2,1)S(1)} %get-tuple-element.110), channel_id=1, source_target_pairs={{0,3},{1,2},{2,1},{3,0},{4,7},{5,6},{6,5},{7,4},{8,11},{9,10},{10,... | collective-permute-start | bytes 344072 | tf_op jit(solution)/shard_map/hidden_grad_sum/ppermute | solution.py:22
  206.4 14.6 %collective-permute-start.27 = (bf16[224,256]{1,0:T(8,128)(2,1)S(1)}, bf16[224,256]{1,0:T(8,128)(2,1)S(1)}, u32[]{:S(2)}, u32[]{:S(2)}) collective-permute-start(bf16[224,256]{1,0:T(8,128)(2,1)S(1)} %get-tuple-element.112), channel_id=1, source_target_pairs={{0,4},{1,5},{2,6},{3,7},{4,0},{5,1},{6,2},{7,3},{8,12},{9,13},{10,... | collective-permute-start | bytes 344072 | tf_op jit(solution)/shard_map/hidden_grad_sum/ppermute | solution.py:22
  206.6 14.4 %collective-permute-start.28 = (bf16[224,256]{1,0:T(8,128)(2,1)S(1)}, bf16[224,256]{1,0:T(8,128)(2,1)S(1)}, u32[]{:S(2)}, u32[]{:S(2)}) collective-permute-start(bf16[224,256]{1,0:T(8,128)(2,1)S(1)} %get-tuple-element.113), channel_id=1, source_target_pairs={{0,8},{1,9},{2,10},{3,11},{4,12},{5,13},{6,14},{7,15},{8,0},{9,1},... | collective-permute-start | bytes 344072 | tf_op jit(solution)/shard_map/hidden_grad_sum/ppermute | solution.py:22
  216.9 1.1 copy-start.22
  219.6 6.0 %collective-permute-start.29 = (bf16[224,256]{1,0:T(8,128)(2,1)S(1)}, bf16[224,256]{1,0:T(8,128)(2,1)S(1)}, u32[]{:S(2)}, u32[]{:S(2)}) collective-permute-start(bf16[224,256]{1,0:T(8,128)(2,1)S(1)} %get-tuple-element.114), channel_id=1, source_target_pairs={{0,12},{1,13},{2,14},{3,15},{4,8},{5,9},{6,10},{7,11},{8,4},{9,5},... | collective-permute-start | bytes 344072 | tf_op jit(solution)/shard_map/hidden_grad_sum/ppermute | solution.py:22
  225.7 1.0 copy-start.1
  (2 other events, 1.4 us)
Sparse Core Ops, SparseCore 0:
  11.9 78.1 all-gather.2
  92.2 50.5 all-gather.4
  145.2 46.0 reduce-scatter.1

commit v5 on v4

--- a/solution.py
+++ b/solution.py
@@ -443,6 +443,7 @@
             mid_weight,
             tail_weight,
             head_weight,
+            mib=60,
         )
         weights = lax.all_gather(packed, "dp", axis=0, tiled=True)
     with jax.named_scope("gather_proj"):
@@ -503,7 +504,7 @@
                 pltpu.SemaphoreType.DMA((len(spans),)),
                 pltpu.SemaphoreType.DMA((4,)),
             ],
-            mib=48,
+            mib=60,
         )
     with jax.named_scope("spread_statistics"):
         stats = spread_vocab(stats[:, :8].T)

time: 234 us -> 231 us (0.987)
  local copies, waits for them, and re-layouts: 43.8 us -> 36.7 us
  Pallas kernels: 46 us -> 50.4 us
    unnamed x64 -> x52, local copies, waits for them, and re-layouts: 25.9 us -> 18.1 us
    pallas_call x10, Pallas kernels: 44.3 us -> 48.7 us  [in_vmem(): pl.pallas_call(kernel, out_shape=out_shape, in_specs=specs, out_specs=out...]
  transfers between devices with their start and end apart: 36 -> 36, of which waited for: 14 -> 14; matrix products, arithmetic and copies ran while one was open for 15% -> 15% of each run, Pallas kernels for 19% -> 20%
where the time goes in v5:
time: 231 us; the launch traced here: 230 us
  Pallas kernels  50.4 us (22%)
  starting transfers between devices  44.3 us (19%)
  blocking collectives  43.2 us (19%)
  local copies, waits for them, and re-layouts  36.7 us (16%)
  waiting for transfers between devices  31.4 us (14%)
  between operations  14.2 us (6%)
  matrix products  7.27 us (3%)
  other arithmetic  2.9 us (1%)
    pallas_call x10, Pallas kernels, in_vmem(): pl.pallas_call(kernel, out_shape=out_shape, in_specs=specs, out_specs=out...  48.7 us
    all_to_all x2, blocking collectives, spread_vocab(): lax.all_to_all(jnp.broadcast_to(block[None], (size,) + block.shape), 'voc...  43.2 us
    ppermute x30, waiting for transfers between devices, swap(): return lax.ppermute(block, axis_name, pairs)  31.2 us
    ppermute x30, starting transfers between devices, swap(): return lax.ppermute(block, axis_name, pairs)  31 us
    unnamed x52, local copies, waits for them, and re-layouts  18.1 us
    dot_general x3, matrix products, dot(): lax.dot_general(left, right, (((left_dim,), (right_dim,)), ((), ())), pre...  7.27 us
  transfers between devices with their start and end apart: 36, of which 14 were waited for; matrix products, arithmetic and copies ran while one was open for 15% of the time, Pallas kernels for 20%

profile of v5, /device:TPU:0, one launch (start us, length us, event | category | flops | bytes accessed | tf_op | source)
XLA Modules:
  0.0 230.3 jit_solution(15168858100404957384)
XLA Ops:
  7.3 2.9 %gather_weights.1 = bf16[56,15616]{1,0:T(8,128)(2,1)} custom-call(bf16[224,1280]{1,0:T(8,128)(2,1)} %mid_ref.1, bf16[56,2304]{1,0:T(8,128)(2,1)} %tail_ref.1, bf16[896,512]{1,0:T(8,128)(2,1)} %head_ref.1), custom_call_target="tpu_custom_call" | custom-call | flops 2000000000 | bytes 3497984 | tf_op jit(solution)/shard_map/gather_weights/pallas_call | solution.py:81
  10.3 2.9 %collective-permute-start.3 = (bf16[144,896]{1,0:T(8,128)(2,1)S(1)}, bf16[144,896]{1,0:T(8,128)(2,1)S(1)}, u32[]{:S(2)}, u32[]{:S(2)}) collective-permute-start(bf16[144,896]{1,0:T(8,128)(2,1)S(1)} %maximum_maximum_fusion.refs_0_), channel_id=1, source_target_pairs={{0,96},{16,112},{32,64},{48,80},{64,32},{80,48},{96,0},{112,16},{1... | collective-permute-start | bytes 774152 | tf_op jit(solution)/shard_map/gather_proj/ppermute | solution.py:22
  13.5 6.0 %collective-permute-done.3.refs_6_ = bf16[144,896]{1,0:T(8,128)(2,1)S(1)} collective-permute-done((bf16[144,896]{1,0:T(8,128)(2,1)S(1)}, bf16[144,896]{1,0:T(8,128)(2,1)S(1)}, u32[]{:S(2)}, u32[]{:S(2)}) %collective-permute-start.3) | collective-permute-done | bytes 258080 | tf_op jit(solution)/shard_map/gather_proj/ppermute | solution.py:22
  20.1 0.9 collective-permute-done.1.refs_2_
  21.0 1.7 collective-permute-start.5
  23.2 1.2 collective-permute-done.4
  24.4 3.0 %collective-permute-done.5 = bf16[80,896]{1,0:T(8,128)(2,1)S(1)} collective-permute-done((bf16[80,896]{1,0:T(8,128)(2,1)S(1)}, bf16[80,896]{1,0:T(8,128)(2,1)S(1)}, u32[]{:S(2)}, u32[]{:S(2)}) %collective-permute-start.5) | collective-permute-done | bytes 143392 | tf_op jit(solution)/shard_map/gather_proj/ppermute | solution.py:22
  27.5 1.0 constant_dynamic-slice_fusion
  29.2 4.6 %all-to-all-start = ((bf16[8,16,896]{2,1,0:T(8,128)(2,1)}), bf16[8,16,896]{2,1,0:T(8,128)(2,1)}, u32[]{:S(2)}, u32[]{:S(2)}) async-start(bf16[8,16,896]{2,1,0:T(8,128)(2,1)} %copy.74), calls=%async_computation | async-start | bytes 458752 | tf_op jit(solution)/shard_map/spread_hidden/all_to_all | solution.py:464
  36.7 0.9 copy-done.10
  37.7 1.0 copy-done.12
  38.7 1.0 copy-done.14
  39.7 1.0 copy-done.16
  40.6 0.9 gather_proj.1
  41.6 1.1 copy-done.19
  42.7 1.4 convolution_convert_fusion.2
  44.1 28.7 %all_to_all.25.codes_ref = bf16[16,144,256]{2,1,0:T(8,128)(2,1)} all-to-all(bf16[16,144,256]{2,1,0:T(8,128)(2,1)S(1)} %broadcast_in_dim.17), channel_id=1, replica_groups=mesh['dp'=8,'vocab'=16] {'vocab'}, dimensions={0} | all-to-all | bytes 2359296 | tf_op jit(solution)/shard_map/spread_codes/all_to_all | solution.py:400
  72.9 6.0 %copy.75 = bf16[256,7168]{0,1:T(8,128)(2,1)} copy(bf16[256,7168]{1,0:T(8,128)(2,1)} %param.11) | data formatting | bytes 7340032 | tf_op args[0]
  79.0 4.2 %copy.76 = bf16[16,8,56,256]{3,2,1,0:T(8,128)(2,1)} copy(bf16[16,8,56,256]{3,2,0,1:T(8,128)(2,1)} %bitcast.90) | data formatting | bytes 7340032 | tf_op jit(solution)/shard_map/arrange/transpose | solution.py:468
  83.3 1.7 gather_fusion
  85.6 3.0 %copy.77 = bf16[7168,144]{1,0:T(8,128)(2,1)} copy(bf16[7168,144]{0,1:T(8,128)(2,1)S(1)} %bitcast.83) | data formatting | bytes 4128768 | tf_op jit(solution)/shard_map/arrange/transpose | solution.py:470
  88.5 0.8 copy.78.position_ref
  89.4 16.2 %logits.1 = (bf16[5,448,256]{2,1,0:T(8,128)(2,1)}, f32[256,512]{1,0:T(8,128)}, f32[256,1280]{1,0:T(8,128)}, f32[256,2304]{1,0:T(8,128)}, f32[256,128]{1,0:T(8,128)}) custom-call(s32[3]{0:T(128)} %pad_add_fusion.bases_ref, bf16[448,15616]{1,0:T(8,128)(2,1)} %all-gather.3.cloned.1.call-done.w_any, bf16[16,144,256]{2,1,0:T(8,128)(2,1)} %all_to_all.25.codes_ref, ...), custom_call_target="tpu_custom_call" | custom-call | flops 2000000000 | bytes 26412044 | tf_op jit(solution)/shard_map/logits/pallas_call | solution.py:81
  105.6 0.9 slice_bitcast_fusion.1
  106.6 14.4 %all_to_all.26 = f32[16,8,256]{2,1,0:T(8,128)S(1)} all-to-all(f32[16,8,256]{2,1,0:T(8,128)S(1)} %broadcast_in_dim.36), channel_id=1, replica_groups=mesh['dp'=8,'vocab'=16] {'vocab'}, dimensions={0} | all-to-all | bytes 262144 | tf_op jit(solution)/shard_map/spread_statistics/all_to_all | solution.py:400
  121.9 1.1 copy-done.8
  123.0 9.5 %grad_logits.1 = (bf16[256,512]{1,0:T(8,128)(2,1)S(1)}, bf16[256,1280]{1,0:T(8,128)(2,1)S(1)}, bf16[256,2304]{1,0:T(8,128)(2,1)S(1)}, bf16[16,144,256]{2,1,0:T(8,128)(2,1)}) custom-call(s32[3]{0:T(128)S(1)} %copy-done.17, bf16[448,15616]{1,0:T(8,128)(2,1)} %all-gather.3.cloned.1.call-done.w_any, f32[256,2]{1,0:T(8,128)S(1)} %copy.83.lse_ref, ...), custom_call_target="tpu_custom_call" | custom-call | flops 2000000000 | bytes 23563276 | tf_op jit(solution)/shard_map/grad_logits/pallas_call | solution.py:81
  132.6 3.4 %mid_tail_grads.2 = bf16[448,7424]{1,0:T(8,128)(2,1)} custom-call(bf16[5,448,256]{2,1,0:T(8,128)(2,1)S(1)} %copy-done.6, bf16[256,1280]{1,0:T(8,128)(2,1)S(1)} %get-tuple-element.100.mid_ref, bf16[256,2304]{1,0:T(8,128)(2,1)S(1)} %get-tuple-element.101.tail_ref), custom_call_target="tpu_custom_call" | custom-call | flops 2000000000 | bytes 9633792 | tf_op jit(solution)/shard_map/mid_tail_grads/pallas_call | solution.py:81
  136.0 4.4 %all-to-all-start.3 = ((bf16[16,144,256]{2,1,0:T(8,128)(2,1)}), bf16[16,144,256]{2,1,0:T(8,128)(2,1)}, u32[]{:S(2)}, u32[]{:S(2)}) async-start(bf16[16,144,256]{2,1,0:T(8,128)(2,1)} %get-tuple-element.74), calls=%async_computation.3 | async-start | bytes 2359296 | tf_op jit(solution)/shard_map/code_grads/all_to_all | solution.py:573
  140.8 2.0 collective-permute-start.9
  142.8 7.9 %hidden_head.1.head_ref = bf16[16,448,256]{2,1,0:T(8,128)(2,1)S(1)} custom-call(s32[1]{0:T(128)} %bitcast.me_ref, bf16[448,15616]{1,0:T(8,128)(2,1)} %all-gather.3.cloned.1.call-done.w_any, bf16[256,512]{1,0:T(8,128)(2,1)S(1)} %get-tuple-element.71.g_ref), custom_call_target="tpu_custom_call" | custom-call | flops 2000000000 | bytes 17924100 | tf_op jit(solution)/shard_map/hidden_head/pallas_call | solution.py:81
  150.8 1.8 copy-done.2
  153.2 1.9 collective-permute-start.13
  155.6 3.4 %collective-permute-done.12 = bf16[8,16,512]{2,1,0:T(8,128)(2,1)S(1)} collective-permute-done((bf16[8,16,512]{2,1,0:T(8,128)(2,1)S(1)}, bf16[8,16,512]{2,1,0:T(8,128)(2,1)S(1)}, u32[]{:S(2)}, u32[]{:S(2)}) %collective-permute-start.12) | collective-permute-done | bytes 131104 | tf_op jit(solution)/shard_map/head_grad/ppermute | solution.py:22
  159.0 1.8 collective-permute-done.13
  161.0 1.5 collective-permute-done.14.refs_5_
  162.5 0.8 head_grad.1
  163.3 1.5 reduce_sum.50.dz_ref
  164.8 4.5 %hidden_grad.1 = (bf16[4,224,256]{2,1,0:T(8,128)(2,1)S(1)}, bf16[4,224,256]{2,1,0:T(8,128)(2,1)S(1)}, bf16[2,224,256]{2,1,0:T(8,128)(2,1)S(1)}, bf16[2,224,256]{...) custom-call(s32[1]{0:T(128)} %bitcast.me_ref, ...), custom_call_target="tpu_custom_call" | custom-call | flops 2000000000 | bytes 9478148 | tf_op jit(solution)/shard_map/hidden_grad/pallas_call | solution.py:81
  169.3 3.0 %collective-permute-start.16 = (bf16[2,224,256]{2,1,0:T(8,128)(2,1)S(1)}, bf16[2,224,256]{2,1,0:T(8,128)(2,1)S(1)}, u32[]{:S(2)}, u32[]{:S(2)}) collective-permute-start(bf16[2,224,256]{2,1,0:T(8,128)(2,1)S(1)} %get-tuple-element.79), channel_id=1, source_target_pairs={{0,12},{1,13},{2,14},{3,15},{4,8},{5,9},{6,10},{7,11},{8,4},{9,5},... | collective-permute-start | bytes 688136 | tf_op jit(solution)/shard_map/hidden_grad_sum/ppermute | solution.py:22
  172.6 2.7 %collective-permute-start.18 = (bf16[2,224,256]{2,1,0:T(8,128)(2,1)S(1)}, bf16[2,224,256]{2,1,0:T(8,128)(2,1)S(1)}, u32[]{:S(2)}, u32[]{:S(2)}) collective-permute-start(bf16[2,224,256]{2,1,0:T(8,128)(2,1)S(1)} %get-tuple-element.89), channel_id=1, source_target_pairs={{0,3},{1,2},{2,1},{3,0},{4,7},{5,6},{6,5},{7,4},{8,11},{9,10},{10,... | collective-permute-start | bytes 688136 | tf_op jit(solution)/shard_map/hidden_grad_sum/ppermute | solution.py:22
  175.6 3.0 %convolution_convert_fusion = bf16[896,512]{1,0:T(8,128)(2,1)} fusion(bf16[2048,896]{1,0:T(8,128)(2,1)S(1)} %bitcast.96, bf16[2048,512]{1,0:T(8,128)(2,1)S(1)} %bitcast.84), kind=kOutput, calls=%fused_computation.1 | convolution fusion | flops 1879506944 | bytes 6684672 | tf_op jit(solution)/shard_map/head_proj_grads/dot_general | solution.py:15
  178.6 1.2 collective-permute-done.17.refs_3_
  179.7 1.2 collective-permute-done.18.refs_5_
  181.0 1.2 collective-permute-done.19.refs_7_
  182.2 1.1 hidden_grad_sum.3
  183.3 1.7 collective-permute-start.20
  185.9 1.2 collective-permute-start.23
  187.1 0.9 broadcast_in_dim.37
  188.0 4.2 %all-to-all-start.4 = ((bf16[8,256,144]{1,2,0:T(8,128)(2,1)}), bf16[8,256,144]{1,2,0:T(8,128)(2,1)}, u32[]{:S(2)}, u32[]{:S(2)}) async-start(bf16[8,256,144]{1,2,0:T(8,128)(2,1)} %broadcast_in_dim.37), calls=%async_computation.4 | async-start | bytes 1179648 | tf_op jit(solution)/shard_map/hidden_grad_sum/head_proj_grads/all_to_all | solution.py:614
  192.3 2.2 collective-permute-done.20.refs_1_
  194.5 2.6 %collective-permute-done.21.refs_2_ = bf16[4,224,256]{2,1,0:T(8,128)(2,1)S(1)} collective-permute-done((bf16[4,224,256]{2,1,0:T(8,128)(2,1)}, bf16[4,224,256]{2,1,0:T(8,128)(2,1)S(1)}, u32[]{:S(2)}, u32[]{:S(2)}) %collective-permute-start.21) | collective-permute-done | bytes 458784 | tf_op jit(solution)/shard_map/hidden_grad_sum/ppermute | solution.py:22
  197.4 1.3 hidden_grad_sum.4
  199.4 2.7 %collective-permute-start.25 = (bf16[224,256]{1,0:T(8,128)(2,1)S(1)}, bf16[224,256]{1,0:T(8,128)(2,1)S(1)}, u32[]{:S(2)}, u32[]{:S(2)}) collective-permute-start(bf16[224,256]{1,0:T(8,128)(2,1)S(1)} %get-tuple-element.109), channel_id=1, source_target_pairs={{0,2},{1,3},{2,0},{3,1},{4,6},{5,7},{6,4},{7,5},{8,10},{9,11},{10,... | collective-permute-start | bytes 344072 | tf_op jit(solution)/shard_map/hidden_grad_sum/ppermute | solution.py:22
  202.1 1.5 collective-permute-start.26
  203.7 3.8 %collective-permute-start.28 = (bf16[224,256]{1,0:T(8,128)(2,1)S(1)}, bf16[224,256]{1,0:T(8,128)(2,1)S(1)}, u32[]{:S(2)}, u32[]{:S(2)}) collective-permute-start(bf16[224,256]{1,0:T(8,128)(2,1)S(1)} %get-tuple-element.113), channel_id=1, source_target_pairs={{0,8},{1,9},{2,10},{3,11},{4,12},{5,13},{6,14},{7,15},{8,0},{9,1},... | collective-permute-start | bytes 344072 | tf_op jit(solution)/shard_map/hidden_grad_sum/ppermute | solution.py:22
  207.6 2.2 copy.85
  209.7 1.3 copy.86
  211.1 2.9 %convolution_convert_fusion.1 = bf16[144,896]{1,0:T(8,128)(2,1)S(1)} fusion(bf16[2048,144]{1,0:T(8,128)(2,1)S(1)} %bitcast.94, bf16[2048,896]{1,0:T(8,128)(2,1)} %bitcast.95), kind=kOutput, calls=%fused_computation.2 | convolution fusion | flops 528611328 | bytes 4517888 | tf_op jit(solution)/shard_map/hidden_grad_sum/head_proj_grads/dot_general | solution.py:15
  214.0 1.1 copy-done.18
  215.1 0.9 mid_tail_grads.3
  216.8 0.7 collective-permute-start.29
  218.2 4.6 %collective-permute-done.29.refs_7_ = bf16[224,256]{1,0:T(8,128)(2,1)S(1)} collective-permute-done((bf16[224,256]{1,0:T(8,128)(2,1)S(1)}, bf16[224,256]{1,0:T(8,128)(2,1)S(1)}, u32[]{:S(2)}, u32[]{:S(2)}) %collective-permute-start.29) | collective-permute-done | bytes 114720 | tf_op jit(solution)/shard_map/hidden_grad_sum/ppermute | solution.py:22
  222.8 0.8 hidden_grad_sum.5
  (115 shorter events, 12.8 us)
Async XLA Ops:
  7.2 76.1 %copy-start = (s32[65536]{0:T(1024)S(1)}, s32[65536]{0:T(1024)}, u32[]{:S(2)}) copy-start(s32[65536]{0:T(1024)} %param.21) | copy-start | bytes 786436
  7.2 3.0 %copy-start.21 = (bf16[896,112]{0,1:T(8,128)(2,1)S(1)}, bf16[896,112]{0,1:T(8,128)(2,1)}, u32[]{:S(2)}) copy-start(bf16[896,112]{0,1:T(8,128)(2,1)} %param.13) | copy-start | bytes 602116
  7.2 3.0 %copy-start.22 = (bf16[896,28]{0,1:T(8,128)(2,1)S(1)}, bf16[896,28]{0,1:T(8,128)(2,1)}, u32[]{:S(2)}) copy-start(bf16[896,28]{0,1:T(8,128)(2,1)} %param.14) | copy-start | bytes 150532
  7.2 82.2 %all-gather.3.cloned.1.call-start = ((), (), s32[]{:S(2)}) async-start(), calls=%async_computation.6 | async-start | bytes 15740928 | tf_op jit(solution)/shard_map/gather_weights/all_gather | solution.py:448
  10.3 9.1 %collective-permute-start.3 = (bf16[144,896]{1,0:T(8,128)(2,1)S(1)}, bf16[144,896]{1,0:T(8,128)(2,1)S(1)}, u32[]{:S(2)}, u32[]{:S(2)}) collective-permute-start(bf16[144,896]{1,0:T(8,128)(2,1)S(1)} %maximum_maximum_fusion.refs_0_), channel_id=1, source_target_pairs={{0,96},{16,112},{32,64},{48,80},{64,32},{80,48},{96,0},{112,16},{1... | collective-permute-start | bytes 774152 | tf_op jit(solution)/shard_map/gather_proj/ppermute | solution.py:22
  13.3 7.7 %collective-permute-start.1 = (bf16[144,896]{1,0:T(8,128)(2,1)S(1)}, bf16[144,896]{1,0:T(8,128)(2,1)S(1)}, u32[]{:S(2)}, u32[]{:S(2)}) collective-permute-start(bf16[144,896]{1,0:T(8,128)(2,1)S(1)} %maximum_maximum_fusion.refs_0_), channel_id=1, source_target_pairs={{0,32},{16,48},{32,0},{48,16},{64,96},{80,112},{96,64},{112,80},{1... | collective-permute-start | bytes 774152 | tf_op jit(solution)/shard_map/gather_proj/ppermute | solution.py:22
  19.5 4.9 %collective-permute-start.4 = (bf16[64,896]{1,0:T(8,128)(2,1)S(1)}, bf16[64,896]{1,0:T(8,128)(2,1)S(1)}, u32[]{:S(2)}, u32[]{:S(2)}) collective-permute-start(bf16[64,896]{1,0:T(8,128)(2,1)S(1)} %slice.54), channel_id=1, source_target_pairs={{0,32},{16,48},{32,0},{48,16},{64,96},{80,112},{96,64},{112,80},{1... | collective-permute-start | bytes 344072 | tf_op jit(solution)/shard_map/gather_proj/ppermute | solution.py:22
  21.0 6.4 %collective-permute-start.5 = (bf16[80,896]{1,0:T(8,128)(2,1)S(1)}, bf16[80,896]{1,0:T(8,128)(2,1)S(1)}, u32[]{:S(2)}, u32[]{:S(2)}) collective-permute-start(bf16[80,896]{1,0:T(8,128)(2,1)S(1)} %slice.55), channel_id=1, source_target_pairs={{0,96},{16,112},{32,64},{48,80},{64,32},{80,48},{96,0},{112,16},{1... | collective-permute-start | bytes 430088 | tf_op jit(solution)/shard_map/gather_proj/ppermute | solution.py:22
  22.7 11.3 %collective-permute-start = (bf16[144,896]{1,0:T(8,128)(2,1)S(1)}, bf16[144,896]{1,0:T(8,128)(2,1)S(1)}, u32[]{:S(2)}, u32[]{:S(2)}) collective-permute-start(bf16[144,896]{1,0:T(8,128)(2,1)S(1)} %maximum_maximum_fusion.refs_0_), channel_id=1, source_target_pairs={{0,16},{16,0},{32,48},{48,32},{64,80},{80,64},{96,112},{112,96},{1... | collective-permute-start | bytes 774152 | tf_op jit(solution)/shard_map/gather_proj/ppermute | solution.py:22
  22.7 12.0 %collective-permute-start.2 = (bf16[144,896]{1,0:T(8,128)(2,1)S(1)}, bf16[144,896]{1,0:T(8,128)(2,1)S(1)}, u32[]{:S(2)}, u32[]{:S(2)}) collective-permute-start(bf16[144,896]{1,0:T(8,128)(2,1)S(1)} %collective-permute-done.1.refs_2_), channel_id=1, source_target_pairs={{0,16},{16,0},{32,48},{48,32},{64,80},{80,64},{96,112},{112,96},{1... | collective-permute-start | bytes 774152 | tf_op jit(solution)/shard_map/gather_proj/ppermute | solution.py:22
  23.2 12.1 %collective-permute-start.7 = (bf16[144,896]{1,0:T(8,128)(2,1)S(1)}, bf16[144,896]{1,0:T(8,128)(2,1)S(1)}, u32[]{:S(2)}, u32[]{:S(2)}) collective-permute-start(bf16[144,896]{1,0:T(8,128)(2,1)S(1)} %collective-permute-done.3.refs_6_), channel_id=1, source_target_pairs={{0,16},{16,0},{32,48},{48,32},{64,80},{80,64},{96,112},{112,96},{1... | collective-permute-start | bytes 774152 | tf_op jit(solution)/shard_map/gather_proj/ppermute | solution.py:22
  27.4 8.7 %collective-permute-start.6 = (bf16[144,896]{1,0:T(8,128)(2,1)S(1)}, bf16[144,896]{1,0:T(8,128)(2,1)S(1)}, u32[]{:S(2)}, u32[]{:S(2)}) collective-permute-start(bf16[144,896]{1,0:T(8,128)(2,1)S(1)} %constant_dynamic-update-slice_fusion.refs_4_), channel_id=1, source_target_pairs={{0,16},{16,0},{32,48},{48,32},{64,80},{80,64},{96,112},{112,96},{1... | collective-permute-start | bytes 774152 | tf_op jit(solution)/shard_map/gather_proj/ppermute | solution.py:22
  29.2 14.9 %all-to-all-start = ((bf16[8,16,896]{2,1,0:T(8,128)(2,1)}), bf16[8,16,896]{2,1,0:T(8,128)(2,1)}, u32[]{:S(2)}, u32[]{:S(2)}) async-start(bf16[8,16,896]{2,1,0:T(8,128)(2,1)} %copy.74), calls=%async_computation | async-start | bytes 458752 | tf_op jit(solution)/shard_map/spread_hidden/all_to_all | solution.py:464
  33.8 131.0 %all-gather.5.cloned.1.call-start = ((), (), s32[]{:S(2)}) async-start(), calls=%async_computation.7 | async-start | bytes 3899392 | tf_op jit(solution)/shard_map/spread_hidden/all_gather | solution.py:466
  33.9 0.7 copy-start.9
  34.6 0.7 copy-start.11
  35.3 0.7 copy-start.13
  36.0 0.7 copy-start.15
  36.7 0.9 copy-start.10
  37.7 1.1 copy-start.12
  38.7 1.0 copy-start.14
  39.7 1.0 copy-start.16
  40.6 2.0 copy-start.19
  72.9 141.1 %reduce-scatter.2.cloned.1.call-start = ((), (), s32[]{:S(2)}) async-start(), calls=%async_computation.8 | async-start | bytes 7483392 | tf_op jit(solution)/shard_map/mid_tail_grads/reduce_scatter | solution.py:590
  79.0 4.3 %copy-start.23 = (s32[256]{0:T(256)S(1)}, s32[256]{0:T(256)}, u32[]{:S(2)}) copy-start(s32[256]{0:T(256)} %param.20) | copy-start | bytes 3076
  89.3 32.5 %copy-start.3 = (bf16[256,2304]{1,0:T(8,128)(2,1)S(1)}, bf16[256,2304]{1,0:T(8,128)(2,1)}, u32[]{:S(2)}) copy-start(bf16[256,2304]{1,0:T(8,128)(2,1)} %target_tail.3) | copy-start | bytes 3538948
  89.3 32.5 %copy-start.4 = (bf16[256,1280]{1,0:T(8,128)(2,1)S(1)}, bf16[256,1280]{1,0:T(8,128)(2,1)}, u32[]{:S(2)}) copy-start(bf16[256,1280]{1,0:T(8,128)(2,1)} %target_mid.3) | copy-start | bytes 1966084
  89.3 32.6 %copy-start.5 = (s32[256,1]{1,0:T(8,128)S(1)}, s32[256,1]{1,0:T(8,128)}, u32[]{:S(2)}) copy-start(s32[256,1]{1,0:T(8,128)} %copy.78.position_ref) | copy-start | bytes 3076
  89.3 32.6 %copy-start.7 = (bf16[256,512]{1,0:T(8,128)(2,1)S(1)}, bf16[256,512]{1,0:T(8,128)(2,1)}, u32[]{:S(2)}) copy-start(bf16[256,512]{1,0:T(8,128)(2,1)} %target_head.3) | copy-start | bytes 786436
  89.3 32.6 %copy-start.17 = (s32[3]{0:T(128)S(1)}, s32[3]{0:T(128)}, u32[]{:S(2)}) copy-start(s32[3]{0:T(128)} %pad_add_fusion.bases_ref) | copy-start | bytes 40
  121.9 1.1 copy-start.8
  123.0 9.5 %copy-start.6 = (bf16[5,448,256]{2,1,0:T(8,128)(2,1)S(1)}, bf16[5,448,256]{2,1,0:T(8,128)(2,1)}, u32[]{:S(2)}) copy-start(bf16[5,448,256]{2,1,0:T(8,128)(2,1)} %get-tuple-element.99.z_ref) | copy-start | bytes 3440644
  136.0 27.3 %all-to-all-start.3 = ((bf16[16,144,256]{2,1,0:T(8,128)(2,1)}), bf16[16,144,256]{2,1,0:T(8,128)(2,1)}, u32[]{:S(2)}, u32[]{:S(2)}) async-start(bf16[16,144,256]{2,1,0:T(8,128)(2,1)} %get-tuple-element.74), calls=%async_computation.3 | async-start | bytes 2359296 | tf_op jit(solution)/shard_map/code_grads/all_to_all | solution.py:573
  140.4 12.2 %collective-permute-start.8 = (bf16[16,16,512]{2,1,0:T(8,128)(2,1)S(1)}, bf16[16,16,512]{2,1,0:T(8,128)(2,1)S(1)}, u32[]{:S(2)}, u32[]{:S(2)}) collective-permute-start(bf16[16,16,512]{2,1,0:T(8,128)(2,1)S(1)} %bitcast.85), channel_id=1, source_target_pairs={{0,32},{16,48},{32,0},{48,16},{64,96},{80,112},{96,64},{112,80},{1... | collective-permute-start | bytes 786440 | tf_op jit(solution)/shard_map/head_grad/ppermute | solution.py:22
  140.8 11.8 %collective-permute-start.9 = (bf16[16,16,512]{2,1,0:T(8,128)(2,1)S(1)}, bf16[16,16,512]{2,1,0:T(8,128)(2,1)S(1)}, u32[]{:S(2)}, u32[]{:S(2)}) collective-permute-start(bf16[16,16,512]{2,1,0:T(8,128)(2,1)S(1)} %bitcast.86), channel_id=1, source_target_pairs={{0,96},{16,112},{32,64},{48,80},{64,32},{80,48},{96,0},{112,16},{1... | collective-permute-start | bytes 786440 | tf_op jit(solution)/shard_map/head_grad/ppermute | solution.py:22
  150.8 1.8 copy-start.2
  152.6 6.4 %collective-permute-start.12 = (bf16[8,16,512]{2,1,0:T(8,128)(2,1)S(1)}, bf16[8,16,512]{2,1,0:T(8,128)(2,1)S(1)}, u32[]{:S(2)}, u32[]{:S(2)}) collective-permute-start(bf16[8,16,512]{2,1,0:T(8,128)(2,1)S(1)} %slice.46), channel_id=1, source_target_pairs={{0,32},{16,48},{32,0},{48,16},{64,96},{80,112},{96,64},{112,80},{1... | collective-permute-start | bytes 393224 | tf_op jit(solution)/shard_map/head_grad/ppermute | solution.py:22
  153.2 7.6 %collective-permute-start.13 = (bf16[8,16,512]{2,1,0:T(8,128)(2,1)S(1)}, bf16[8,16,512]{2,1,0:T(8,128)(2,1)S(1)}, u32[]{:S(2)}, u32[]{:S(2)}) collective-permute-start(bf16[8,16,512]{2,1,0:T(8,128)(2,1)S(1)} %slice.47), channel_id=1, source_target_pairs={{0,96},{16,112},{32,64},{48,80},{64,32},{80,48},{96,0},{112,16},{1... | collective-permute-start | bytes 393224 | tf_op jit(solution)/shard_map/head_grad/ppermute | solution.py:22
  155.1 5.9 %collective-permute-start.10 = (bf16[16,16,512]{2,1,0:T(8,128)(2,1)S(1)}, bf16[16,16,512]{2,1,0:T(8,128)(2,1)S(1)}, u32[]{:S(2)}, u32[]{:S(2)}) collective-permute-start(bf16[16,16,512]{2,1,0:T(8,128)(2,1)S(1)} %bitcast.87), channel_id=1, source_target_pairs={{0,16},{16,0},{32,48},{48,32},{64,80},{80,64},{96,112},{112,96},{1... | collective-permute-start | bytes 786440 | tf_op jit(solution)/shard_map/head_grad/ppermute | solution.py:22
  155.1 5.9 %collective-permute-start.11 = (bf16[16,16,512]{2,1,0:T(8,128)(2,1)S(1)}, bf16[16,16,512]{2,1,0:T(8,128)(2,1)S(1)}, u32[]{:S(2)}, u32[]{:S(2)}) collective-permute-start(bf16[16,16,512]{2,1,0:T(8,128)(2,1)S(1)} %collective-permute-done.8.refs_2_), channel_id=1, source_target_pairs={{0,16},{16,0},{32,48},{48,32},{64,80},{80,64},{96,112},{112,96},{1... | collective-permute-start | bytes 786440 | tf_op jit(solution)/shard_map/head_grad/ppermute | solution.py:22
  155.6 5.4 %collective-permute-start.15 = (bf16[16,16,512]{2,1,0:T(8,128)(2,1)S(1)}, bf16[16,16,512]{2,1,0:T(8,128)(2,1)S(1)}, u32[]{:S(2)}, u32[]{:S(2)}) collective-permute-start(bf16[16,16,512]{2,1,0:T(8,128)(2,1)S(1)} %collective-permute-done.9.refs_6_), channel_id=1, source_target_pairs={{0,16},{16,0},{32,48},{48,32},{64,80},{80,64},{96,112},{112,96},{1... | collective-permute-start | bytes 786440 | tf_op jit(solution)/shard_map/head_grad/ppermute | solution.py:22
  160.9 1.6 collective-permute-start.14
  164.8 10.8 %copy-start.20 = (bf16[16,128,896]{2,1,0:T(8,128)(2,1)S(1)}, bf16[16,128,896]{2,1,0:T(8,128)(2,1)}, u32[]{:S(2)}) copy-start(bf16[16,128,896]{2,1,0:T(8,128)(2,1)} %all-gather.5.cloned.1.call-done) | copy-start | bytes 11010052
  169.3 9.3 %collective-permute-start.16 = (bf16[2,224,256]{2,1,0:T(8,128)(2,1)S(1)}, bf16[2,224,256]{2,1,0:T(8,128)(2,1)S(1)}, u32[]{:S(2)}, u32[]{:S(2)}) collective-permute-start(bf16[2,224,256]{2,1,0:T(8,128)(2,1)S(1)} %get-tuple-element.79), channel_id=1, source_target_pairs={{0,12},{1,13},{2,14},{3,15},{4,8},{5,9},{6,10},{7,11},{8,4},{9,5},... | collective-permute-start | bytes 688136 | tf_op jit(solution)/shard_map/hidden_grad_sum/ppermute | solution.py:22
  172.4 7.4 %collective-permute-start.17 = (bf16[2,224,256]{2,1,0:T(8,128)(2,1)S(1)}, bf16[2,224,256]{2,1,0:T(8,128)(2,1)S(1)}, u32[]{:S(2)}, u32[]{:S(2)}) collective-permute-start(bf16[2,224,256]{2,1,0:T(8,128)(2,1)S(1)} %get-tuple-element.87), channel_id=1, source_target_pairs={{0,4},{1,5},{2,6},{3,7},{4,0},{5,1},{6,2},{7,3},{8,12},{9,13},{10,... | collective-permute-start | bytes 688136 | tf_op jit(solution)/shard_map/hidden_grad_sum/ppermute | solution.py:22
  172.6 8.3 %collective-permute-start.18 = (bf16[2,224,256]{2,1,0:T(8,128)(2,1)S(1)}, bf16[2,224,256]{2,1,0:T(8,128)(2,1)S(1)}, u32[]{:S(2)}, u32[]{:S(2)}) collective-permute-start(bf16[2,224,256]{2,1,0:T(8,128)(2,1)S(1)} %get-tuple-element.89), channel_id=1, source_target_pairs={{0,3},{1,2},{2,1},{3,0},{4,7},{5,6},{6,5},{7,4},{8,11},{9,10},{10,... | collective-permute-start | bytes 688136 | tf_op jit(solution)/shard_map/hidden_grad_sum/ppermute | solution.py:22
  175.3 6.9 %collective-permute-start.19 = (bf16[2,224,256]{2,1,0:T(8,128)(2,1)S(1)}, bf16[2,224,256]{2,1,0:T(8,128)(2,1)S(1)}, u32[]{:S(2)}, u32[]{:S(2)}) collective-permute-start(bf16[2,224,256]{2,1,0:T(8,128)(2,1)S(1)} %get-tuple-element.91), channel_id=1, source_target_pairs={{0,1},{1,0},{2,3},{3,2},{4,5},{5,4},{6,7},{7,6},{8,9},{9,8},{10,11... | collective-permute-start | bytes 688136 | tf_op jit(solution)/shard_map/hidden_grad_sum/ppermute | solution.py:22
  183.3 11.2 %collective-permute-start.20 = (bf16[4,224,256]{2,1,0:T(8,128)(2,1)}, bf16[4,224,256]{2,1,0:T(8,128)(2,1)S(1)}, u32[]{:S(2)}, u32[]{:S(2)}) collective-permute-start(bf16[4,224,256]{2,1,0:T(8,128)(2,1)} %get-tuple-element.92), channel_id=1, source_target_pairs={{0,4},{1,5},{2,6},{3,7},{4,0},{5,1},{6,2},{7,3},{8,12},{9,13},{10,... | collective-permute-start | bytes 1376264 | tf_op jit(solution)/shard_map/hidden_grad_sum/ppermute | solution.py:22
  185.0 12.0 %collective-permute-start.21 = (bf16[4,224,256]{2,1,0:T(8,128)(2,1)}, bf16[4,224,256]{2,1,0:T(8,128)(2,1)S(1)}, u32[]{:S(2)}, u32[]{:S(2)}) collective-permute-start(bf16[4,224,256]{2,1,0:T(8,128)(2,1)} %get-tuple-element.93), channel_id=1, source_target_pairs={{0,12},{1,13},{2,14},{3,15},{4,8},{5,9},{6,10},{7,11},{8,4},{9,5},... | collective-permute-start | bytes 1376264 | tf_op jit(solution)/shard_map/hidden_grad_sum/ppermute | solution.py:22
  185.6 11.5 %collective-permute-start.22 = (bf16[4,224,256]{2,1,0:T(8,128)(2,1)S(1)}, bf16[4,224,256]{2,1,0:T(8,128)(2,1)S(1)}, u32[]{:S(2)}, u32[]{:S(2)}) collective-permute-start(bf16[4,224,256]{2,1,0:T(8,128)(2,1)S(1)} %get-tuple-element.95), channel_id=1, source_target_pairs={{0,1},{1,0},{2,3},{3,2},{4,5},{5,4},{6,7},{7,6},{8,9},{9,8},{10,11... | collective-permute-start | bytes 1376264 | tf_op jit(solution)/shard_map/hidden_grad_sum/ppermute | solution.py:22
  185.9 11.5 %collective-permute-start.23 = (bf16[4,224,256]{2,1,0:T(8,128)(2,1)S(1)}, bf16[4,224,256]{2,1,0:T(8,128)(2,1)}, u32[]{:S(2)}, u32[]{:S(2)}) collective-permute-start(bf16[4,224,256]{2,1,0:T(8,128)(2,1)S(1)} %get-tuple-element.96), channel_id=1, source_target_pairs={{0,3},{1,2},{2,1},{3,0},{4,7},{5,6},{6,5},{7,4},{8,11},{9,10},{10,... | collective-permute-start | bytes 1376264 | tf_op jit(solution)/shard_map/hidden_grad_sum/ppermute | solution.py:22
  188.0 19.5 %all-to-all-start.4 = ((bf16[8,256,144]{1,2,0:T(8,128)(2,1)}), bf16[8,256,144]{1,2,0:T(8,128)(2,1)}, u32[]{:S(2)}, u32[]{:S(2)}) async-start(bf16[8,256,144]{1,2,0:T(8,128)(2,1)} %broadcast_in_dim.37), calls=%async_computation.4 | async-start | bytes 1179648 | tf_op jit(solution)/shard_map/hidden_grad_sum/head_proj_grads/all_to_all | solution.py:614
  198.8 18.0 %collective-permute-start.24 = (bf16[224,256]{1,0:T(8,128)(2,1)S(1)}, bf16[224,256]{1,0:T(8,128)(2,1)S(1)}, u32[]{:S(2)}, u32[]{:S(2)}) collective-permute-start(bf16[224,256]{1,0:T(8,128)(2,1)S(1)} %get-tuple-element.108), channel_id=1, source_target_pairs={{0,1},{1,0},{2,3},{3,2},{4,5},{5,4},{6,7},{7,6},{8,9},{9,8},{10,11... | collective-permute-start | bytes 344072 | tf_op jit(solution)/shard_map/hidden_grad_sum/ppermute | solution.py:22
  199.4 18.8 %collective-permute-start.25 = (bf16[224,256]{1,0:T(8,128)(2,1)S(1)}, bf16[224,256]{1,0:T(8,128)(2,1)S(1)}, u32[]{:S(2)}, u32[]{:S(2)}) collective-permute-start(bf16[224,256]{1,0:T(8,128)(2,1)S(1)} %get-tuple-element.109), channel_id=1, source_target_pairs={{0,2},{1,3},{2,0},{3,1},{4,6},{5,7},{6,4},{7,5},{8,10},{9,11},{10,... | collective-permute-start | bytes 344072 | tf_op jit(solution)/shard_map/hidden_grad_sum/ppermute | solution.py:22
  202.1 16.0 %collective-permute-start.26 = (bf16[224,256]{1,0:T(8,128)(2,1)S(1)}, bf16[224,256]{1,0:T(8,128)(2,1)S(1)}, u32[]{:S(2)}, u32[]{:S(2)}) collective-permute-start(bf16[224,256]{1,0:T(8,128)(2,1)S(1)} %get-tuple-element.110), channel_id=1, source_target_pairs={{0,3},{1,2},{2,1},{3,0},{4,7},{5,6},{6,5},{7,4},{8,11},{9,10},{10,... | collective-permute-start | bytes 344072 | tf_op jit(solution)/shard_map/hidden_grad_sum/ppermute | solution.py:22
  203.6 14.6 %collective-permute-start.27 = (bf16[224,256]{1,0:T(8,128)(2,1)S(1)}, bf16[224,256]{1,0:T(8,128)(2,1)S(1)}, u32[]{:S(2)}, u32[]{:S(2)}) collective-permute-start(bf16[224,256]{1,0:T(8,128)(2,1)S(1)} %get-tuple-element.112), channel_id=1, source_target_pairs={{0,4},{1,5},{2,6},{3,7},{4,0},{5,1},{6,2},{7,3},{8,12},{9,13},{10,... | collective-permute-start | bytes 344072 | tf_op jit(solution)/shard_map/hidden_grad_sum/ppermute | solution.py:22
  203.7 14.4 %collective-permute-start.28 = (bf16[224,256]{1,0:T(8,128)(2,1)S(1)}, bf16[224,256]{1,0:T(8,128)(2,1)S(1)}, u32[]{:S(2)}, u32[]{:S(2)}) collective-permute-start(bf16[224,256]{1,0:T(8,128)(2,1)S(1)} %get-tuple-element.113), channel_id=1, source_target_pairs={{0,8},{1,9},{2,10},{3,11},{4,12},{5,13},{6,14},{7,15},{8,0},{9,1},... | collective-permute-start | bytes 344072 | tf_op jit(solution)/shard_map/hidden_grad_sum/ppermute | solution.py:22
  214.0 1.1 copy-start.18
  216.8 6.0 %collective-permute-start.29 = (bf16[224,256]{1,0:T(8,128)(2,1)S(1)}, bf16[224,256]{1,0:T(8,128)(2,1)S(1)}, u32[]{:S(2)}, u32[]{:S(2)}) collective-permute-start(bf16[224,256]{1,0:T(8,128)(2,1)S(1)} %get-tuple-element.114), channel_id=1, source_target_pairs={{0,12},{1,13},{2,14},{3,15},{4,8},{5,9},{6,10},{7,11},{8,4},{9,5},... | collective-permute-start | bytes 344072 | tf_op jit(solution)/shard_map/hidden_grad_sum/ppermute | solution.py:22
  222.8 1.0 copy-start.1
Sparse Core Ops, SparseCore 0:
  10.3 78.1 all-gather.2
  90.6 50.6 all-gather.4
  143.7 46.0 reduce-scatter.1

commit v6 on v5

--- a/solution.py
+++ b/solution.py
@@ -567,12 +567,10 @@
         g_near, g_other = ring_near(g_rows, "dp", 2)
         g_near, g_other, head_term = lax.optimization_barrier((g_near, g_other, head_term))
         g_far = ring_far(g_near, g_other, "dp", 2, n_vocab // 2)
-        g_all = both_cores([g_rows, g_near, g_far, g_other], 1)
-        g_all = g_all.reshape(n_dp * rows, -1)
     with jax.named_scope("code_grads"):
         dz = lax.all_to_all(dz, "vocab", 0, 0)
         dz = jnp.sum(dz.astype(F32), axis=0).astype(BF16)
-        dz, g_all, x_all = lax.optimization_barrier((dz, g_all, x_all))
+        dz, g_far, x_all = lax.optimization_barrier((dz, g_far, x_all))
     with jax.named_scope("mid_tail_grads"):
         packed_grad = in_vmem(
             functools.partial(weight_grads_kernel, low),
@@ -606,6 +604,8 @@
             mib=48,
         )
     with jax.named_scope("head_proj_grads"):
+        g_all = both_cores([g_rows, g_near, g_far, g_other], 1)
+        g_all = g_all.reshape(n_dp * rows, -1)
         head_grad = dot(x_all, g_all, 0, 0).astype(BF16)
 
     def proj_grads(dz):

time: 231 us -> 227 us (0.983)
    unnamed x52 -> x55, local copies, waits for them, and re-layouts: 18.1 us -> 18.1 us
  transfers between devices with their start and end apart: 36 -> 36, of which waited for: 14 -> 13; matrix products, arithmetic and copies ran while one was open for 15% -> 14% of each run, Pallas kernels for 20% -> 21%
where the time goes in v6:
time: 227 us; the launch traced here: 226 us
  Pallas kernels  50.3 us (22%)
  starting transfers between devices  43.3 us (19%)
  blocking collectives  43.2 us (19%)
  local copies, waits for them, and re-layouts  34.6 us (15%)
  waiting for transfers between devices  30.2 us (13%)
  between operations  14.2 us (6%)
  matrix products  7.29 us (3%)
  other arithmetic  2.89 us (1%)
    pallas_call x10, Pallas kernels, in_vmem(): pl.pallas_call(kernel, out_shape=out_shape, in_specs=specs, out_specs=out...  48.6 us
    all_to_all x2, blocking collectives, spread_vocab(): lax.all_to_all(jnp.broadcast_to(block[None], (size,) + block.shape), 'voc...  43.2 us
    ppermute x30, waiting for transfers between devices, swap(): return lax.ppermute(block, axis_name, pairs)  30.1 us
    ppermute x30, starting transfers between devices, swap(): return lax.ppermute(block, axis_name, pairs)  30 us
    unnamed x55, local copies, waits for them, and re-layouts  18.1 us
    dot_general x3, matrix products, dot(): lax.dot_general(left, right, (((left_dim,), (right_dim,)), ((), ())), pre...  7.29 us
    all_to_all x1, starting transfers between devices, per_device(): mine = lax.all_to_all(mine, 'dp', 0, 0)  4.59 us
  transfers between devices with their start and end apart: 36, of which 13 were waited for; matrix products, arithmetic and copies ran while one was open for 14% of the time, Pallas kernels for 21%

profile of v6, /device:TPU:0, one launch (start us, length us, event | category | flops | bytes accessed | tf_op | source)
XLA Modules:
  0.0 226.1 jit_solution(4202951263439848405)
XLA Ops:
  7.3 2.9 %gather_weights.1 = bf16[56,15616]{1,0:T(8,128)(2,1)} custom-call(bf16[224,1280]{1,0:T(8,128)(2,1)} %mid_ref.1, bf16[56,2304]{1,0:T(8,128)(2,1)} %tail_ref.1, bf16[896,512]{1,0:T(8,128)(2,1)} %head_ref.1), custom_call_target="tpu_custom_call" | custom-call | flops 2000000000 | bytes 3497984 | tf_op jit(solution)/shard_map/gather_weights/pallas_call | solution.py:81
  10.4 2.9 %collective-permute-start.3 = (bf16[144,896]{1,0:T(8,128)(2,1)S(1)}, bf16[144,896]{1,0:T(8,128)(2,1)S(1)}, u32[]{:S(2)}, u32[]{:S(2)}) collective-permute-start(bf16[144,896]{1,0:T(8,128)(2,1)S(1)} %maximum_maximum_fusion.refs_0_), channel_id=1, source_target_pairs={{0,96},{16,112},{32,64},{48,80},{64,32},{80,48},{96,0},{112,16},{1... | collective-permute-start | bytes 774152 | tf_op jit(solution)/shard_map/gather_proj/ppermute | solution.py:22
  13.5 6.0 %collective-permute-done.3.refs_6_ = bf16[144,896]{1,0:T(8,128)(2,1)S(1)} collective-permute-done((bf16[144,896]{1,0:T(8,128)(2,1)S(1)}, bf16[144,896]{1,0:T(8,128)(2,1)S(1)}, u32[]{:S(2)}, u32[]{:S(2)}) %collective-permute-start.3) | collective-permute-done | bytes 258080 | tf_op jit(solution)/shard_map/gather_proj/ppermute | solution.py:22
  20.1 0.9 collective-permute-done.1.refs_2_
  21.0 1.7 collective-permute-start.5
  23.2 1.2 collective-permute-done.4
  24.4 3.0 %collective-permute-done.5 = bf16[80,896]{1,0:T(8,128)(2,1)S(1)} collective-permute-done((bf16[80,896]{1,0:T(8,128)(2,1)S(1)}, bf16[80,896]{1,0:T(8,128)(2,1)S(1)}, u32[]{:S(2)}, u32[]{:S(2)}) %collective-permute-start.5) | collective-permute-done | bytes 143392 | tf_op jit(solution)/shard_map/gather_proj/ppermute | solution.py:22
  27.5 1.0 constant_dynamic-slice_fusion
  28.5 0.7 copy.74
  29.2 4.6 %all-to-all-start = ((bf16[8,16,896]{2,1,0:T(8,128)(2,1)}), bf16[8,16,896]{2,1,0:T(8,128)(2,1)}, u32[]{:S(2)}, u32[]{:S(2)}) async-start(bf16[8,16,896]{2,1,0:T(8,128)(2,1)} %copy.74), calls=%async_computation | async-start | bytes 458752 | tf_op jit(solution)/shard_map/spread_hidden/all_to_all | solution.py:464
  34.6 0.7 copy-done.11
  35.3 0.7 copy-done.13
  36.0 0.7 copy-done.15
  36.7 0.9 copy-done.10
  37.7 1.1 copy-done.12
  38.8 1.0 copy-done.14
  39.7 1.0 copy-done.16
  40.7 0.9 gather_proj.1
  41.6 1.1 copy-done.21
  42.7 1.4 convolution_convert_fusion.2
  44.2 28.7 %all_to_all.25.codes_ref = bf16[16,144,256]{2,1,0:T(8,128)(2,1)} all-to-all(bf16[16,144,256]{2,1,0:T(8,128)(2,1)S(1)} %broadcast_in_dim.17), channel_id=1, replica_groups=mesh['dp'=8,'vocab'=16] {'vocab'}, dimensions={0} | all-to-all | bytes 2359296 | tf_op jit(solution)/shard_map/spread_codes/all_to_all | solution.py:400
  73.0 6.0 %copy.75 = bf16[256,7168]{0,1:T(8,128)(2,1)} copy(bf16[256,7168]{1,0:T(8,128)(2,1)} %param.11) | data formatting | bytes 7340032 | tf_op args[0]
  79.0 4.2 %copy.76 = bf16[16,8,56,256]{3,2,1,0:T(8,128)(2,1)} copy(bf16[16,8,56,256]{3,2,0,1:T(8,128)(2,1)} %bitcast.90) | data formatting | bytes 7340032 | tf_op jit(solution)/shard_map/arrange/transpose | solution.py:468
  83.2 1.7 gather_fusion
  85.6 3.0 %copy.77 = bf16[7168,144]{1,0:T(8,128)(2,1)} copy(bf16[7168,144]{0,1:T(8,128)(2,1)S(1)} %bitcast.83) | data formatting | bytes 4128768 | tf_op jit(solution)/shard_map/arrange/transpose | solution.py:470
  88.5 0.8 copy.78.position_ref
  89.4 16.2 %logits.1 = (bf16[5,448,256]{2,1,0:T(8,128)(2,1)}, f32[256,512]{1,0:T(8,128)}, f32[256,1280]{1,0:T(8,128)}, f32[256,2304]{1,0:T(8,128)}, f32[256,128]{1,0:T(8,128)}) custom-call(s32[3]{0:T(128)} %pad_add_fusion.bases_ref, bf16[448,15616]{1,0:T(8,128)(2,1)} %all-gather.3.cloned.1.call-done.w_any, bf16[16,144,256]{2,1,0:T(8,128)(2,1)} %all_to_all.25.codes_ref, ...), custom_call_target="tpu_custom_call" | custom-call | flops 2000000000 | bytes 26412044 | tf_op jit(solution)/shard_map/logits/pallas_call | solution.py:81
  105.5 0.9 slice_bitcast_fusion.1
  106.5 14.5 %all_to_all.26 = f32[16,8,256]{2,1,0:T(8,128)S(1)} all-to-all(f32[16,8,256]{2,1,0:T(8,128)S(1)} %broadcast_in_dim.36), channel_id=1, replica_groups=mesh['dp'=8,'vocab'=16] {'vocab'}, dimensions={0} | all-to-all | bytes 262144 | tf_op jit(solution)/shard_map/spread_statistics/all_to_all | solution.py:400
  121.9 1.1 copy-done.8
  123.0 9.5 %grad_logits.1 = (bf16[256,512]{1,0:T(8,128)(2,1)S(1)}, bf16[256,1280]{1,0:T(8,128)(2,1)S(1)}, bf16[256,2304]{1,0:T(8,128)(2,1)S(1)}, bf16[16,144,256]{2,1,0:T(8,128)(2,1)}) custom-call(s32[3]{0:T(128)S(1)} %copy-done.17, bf16[448,15616]{1,0:T(8,128)(2,1)} %all-gather.3.cloned.1.call-done.w_any, f32[256,2]{1,0:T(8,128)S(1)} %copy.83.lse_ref, ...), custom_call_target="tpu_custom_call" | custom-call | flops 2000000000 | bytes 23563276 | tf_op jit(solution)/shard_map/grad_logits/pallas_call | solution.py:81
  132.6 3.4 %mid_tail_grads.2 = bf16[448,7424]{1,0:T(8,128)(2,1)} custom-call(bf16[5,448,256]{2,1,0:T(8,128)(2,1)S(1)} %copy-done.6, bf16[256,1280]{1,0:T(8,128)(2,1)S(1)} %get-tuple-element.100.mid_ref, bf16[256,2304]{1,0:T(8,128)(2,1)S(1)} %get-tuple-element.101.tail_ref), custom_call_target="tpu_custom_call" | custom-call | flops 2000000000 | bytes 9633792 | tf_op jit(solution)/shard_map/mid_tail_grads/pallas_call | solution.py:81
  136.0 4.4 %all-to-all-start.3 = ((bf16[16,144,256]{2,1,0:T(8,128)(2,1)}), bf16[16,144,256]{2,1,0:T(8,128)(2,1)}, u32[]{:S(2)}, u32[]{:S(2)}) async-start(bf16[16,144,256]{2,1,0:T(8,128)(2,1)} %get-tuple-element.74), calls=%async_computation.3 | async-start | bytes 2359296 | tf_op jit(solution)/shard_map/code_grads/all_to_all | solution.py:571
  140.8 2.0 collective-permute-start.9
  142.8 7.9 %hidden_head.1.head_ref = bf16[16,448,256]{2,1,0:T(8,128)(2,1)S(1)} custom-call(s32[1]{0:T(128)} %bitcast.me_ref, bf16[448,15616]{1,0:T(8,128)(2,1)} %all-gather.3.cloned.1.call-done.w_any, bf16[256,512]{1,0:T(8,128)(2,1)S(1)} %get-tuple-element.71.g_ref), custom_call_target="tpu_custom_call" | custom-call | flops 2000000000 | bytes 17924100 | tf_op jit(solution)/shard_map/hidden_head/pallas_call | solution.py:81
  150.8 1.8 copy-done.2
  152.6 1.3 collective-permute-start.11
  155.0 5.2 %collective-permute-done.11 = bf16[8,16,512]{2,1,0:T(8,128)(2,1)S(1)} collective-permute-done((bf16[8,16,512]{2,1,0:T(8,128)(2,1)S(1)}, bf16[8,16,512]{2,1,0:T(8,128)(2,1)S(1)}, u32[]{:S(2)}, u32[]{:S(2)}) %collective-permute-start.11) | collective-permute-done | bytes 131104 | tf_op jit(solution)/shard_map/head_grad/ppermute | solution.py:22
  160.4 1.4 reduce_sum.50.dz_ref
  161.9 4.4 %hidden_grad.1 = (bf16[4,224,256]{2,1,0:T(8,128)(2,1)S(1)}, bf16[4,224,256]{2,1,0:T(8,128)(2,1)S(1)}, bf16[2,224,256]{2,1,0:T(8,128)(2,1)S(1)}, bf16[2,224,256]{...) custom-call(s32[1]{0:T(128)} %bitcast.me_ref, ...), custom_call_target="tpu_custom_call" | custom-call | flops 2000000000 | bytes 9478148 | tf_op jit(solution)/shard_map/hidden_grad/pallas_call | solution.py:81
  166.4 3.0 %collective-permute-start.12 = (bf16[2,224,256]{2,1,0:T(8,128)(2,1)S(1)}, bf16[2,224,256]{2,1,0:T(8,128)(2,1)S(1)}, u32[]{:S(2)}, u32[]{:S(2)}) collective-permute-start(bf16[2,224,256]{2,1,0:T(8,128)(2,1)S(1)} %get-tuple-element.79), channel_id=1, source_target_pairs={{0,12},{1,13},{2,14},{3,15},{4,8},{5,9},{6,10},{7,11},{8,4},{9,5},... | collective-permute-start | bytes 688136 | tf_op jit(solution)/shard_map/hidden_grad_sum/ppermute | solution.py:22
  169.6 2.8 %collective-permute-start.18 = (bf16[2,224,256]{2,1,0:T(8,128)(2,1)S(1)}, bf16[2,224,256]{2,1,0:T(8,128)(2,1)S(1)}, u32[]{:S(2)}, u32[]{:S(2)}) collective-permute-start(bf16[2,224,256]{2,1,0:T(8,128)(2,1)S(1)} %get-tuple-element.89), channel_id=1, source_target_pairs={{0,3},{1,2},{2,1},{3,0},{4,7},{5,6},{6,5},{7,4},{8,11},{9,10},{10,... | collective-permute-start | bytes 688136 | tf_op jit(solution)/shard_map/hidden_grad_sum/ppermute | solution.py:22
  172.7 0.8 head_proj_grads.1
  173.5 3.0 %convolution_convert_fusion = bf16[896,512]{1,0:T(8,128)(2,1)} fusion(bf16[2048,896]{1,0:T(8,128)(2,1)S(1)} %bitcast.96, bf16[2048,512]{1,0:T(8,128)(2,1)S(1)} %bitcast.84), kind=kOutput, calls=%fused_computation.1 | convolution fusion | flops 1879506944 | bytes 6684672 | tf_op jit(solution)/shard_map/head_proj_grads/dot_general | solution.py:15
  177.1 1.5 collective-permute-done.18.refs_5_
  178.7 1.2 collective-permute-done.19.refs_7_
  179.9 1.2 hidden_grad_sum.3
  181.1 1.4 collective-permute-start.20
  183.3 1.2 collective-permute-start.23
  184.5 0.9 broadcast_in_dim.37
  185.4 4.2 %all-to-all-start.4 = ((bf16[8,256,144]{1,2,0:T(8,128)(2,1)}), bf16[8,256,144]{1,2,0:T(8,128)(2,1)}, u32[]{:S(2)}, u32[]{:S(2)}) async-start(bf16[8,256,144]{1,2,0:T(8,128)(2,1)} %broadcast_in_dim.37), calls=%async_computation.4 | async-start | bytes 1179648 | tf_op jit(solution)/shard_map/hidden_grad_sum/head_proj_grads/all_to_all | solution.py:614
  189.6 3.3 %collective-permute-done.20.refs_1_ = bf16[4,224,256]{2,1,0:T(8,128)(2,1)S(1)} collective-permute-done((bf16[4,224,256]{2,1,0:T(8,128)(2,1)}, bf16[4,224,256]{2,1,0:T(8,128)(2,1)S(1)}, u32[]{:S(2)}, u32[]{:S(2)}) %collective-permute-start.20) | collective-permute-done | bytes 458784 | tf_op jit(solution)/shard_map/hidden_grad_sum/ppermute | solution.py:22
  192.9 2.1 collective-permute-done.21.refs_2_
  195.1 1.3 hidden_grad_sum.4
  197.0 2.7 %collective-permute-start.25 = (bf16[224,256]{1,0:T(8,128)(2,1)S(1)}, bf16[224,256]{1,0:T(8,128)(2,1)S(1)}, u32[]{:S(2)}, u32[]{:S(2)}) collective-permute-start(bf16[224,256]{1,0:T(8,128)(2,1)S(1)} %get-tuple-element.109), channel_id=1, source_target_pairs={{0,2},{1,3},{2,0},{3,1},{4,6},{5,7},{6,4},{7,5},{8,10},{9,11},{10,... | collective-permute-start | bytes 344072 | tf_op jit(solution)/shard_map/hidden_grad_sum/ppermute | solution.py:22
  199.7 1.5 collective-permute-start.26
  201.2 0.7 collective-permute-start.27
  201.9 3.5 %collective-permute-start.28 = (bf16[224,256]{1,0:T(8,128)(2,1)S(1)}, bf16[224,256]{1,0:T(8,128)(2,1)S(1)}, u32[]{:S(2)}, u32[]{:S(2)}) collective-permute-start(bf16[224,256]{1,0:T(8,128)(2,1)S(1)} %get-tuple-element.113), channel_id=1, source_target_pairs={{0,8},{1,9},{2,10},{3,11},{4,12},{5,13},{6,14},{7,15},{8,0},{9,1},... | collective-permute-start | bytes 344072 | tf_op jit(solution)/shard_map/hidden_grad_sum/ppermute | solution.py:22
  205.4 1.4 copy.85
  206.9 2.9 %convolution_convert_fusion.1 = bf16[144,896]{1,0:T(8,128)(2,1)S(1)} fusion(bf16[2048,144]{1,0:T(8,128)(2,1)S(1)} %bitcast.94, bf16[2048,896]{1,0:T(8,128)(2,1)} %bitcast.95), kind=kOutput, calls=%fused_computation.2 | convolution fusion | flops 528611328 | bytes 4517888 | tf_op jit(solution)/shard_map/hidden_grad_sum/head_proj_grads/dot_general | solution.py:15
  209.9 1.1 copy-done.18
  211.0 0.9 mid_tail_grads.3
  213.8 4.9 %collective-permute-done.29.refs_7_ = bf16[224,256]{1,0:T(8,128)(2,1)S(1)} collective-permute-done((bf16[224,256]{1,0:T(8,128)(2,1)S(1)}, bf16[224,256]{1,0:T(8,128)(2,1)S(1)}, u32[]{:S(2)}, u32[]{:S(2)}) %collective-permute-start.29) | collective-permute-done | bytes 114720 | tf_op jit(solution)/shard_map/hidden_grad_sum/ppermute | solution.py:22
  218.7 0.8 hidden_grad_sum.5
  (118 shorter events, 10.6 us)
Async XLA Ops:
  7.2 76.1 %copy-start = (s32[65536]{0:T(1024)S(1)}, s32[65536]{0:T(1024)}, u32[]{:S(2)}) copy-start(s32[65536]{0:T(1024)} %param.21) | copy-start | bytes 786436
  7.2 3.0 %copy-start.23 = (bf16[896,112]{0,1:T(8,128)(2,1)S(1)}, bf16[896,112]{0,1:T(8,128)(2,1)}, u32[]{:S(2)}) copy-start(bf16[896,112]{0,1:T(8,128)(2,1)} %param.13) | copy-start | bytes 602116
  7.2 3.0 %copy-start.24 = (bf16[896,28]{0,1:T(8,128)(2,1)S(1)}, bf16[896,28]{0,1:T(8,128)(2,1)}, u32[]{:S(2)}) copy-start(bf16[896,28]{0,1:T(8,128)(2,1)} %param.14) | copy-start | bytes 150532
  7.2 82.2 %all-gather.3.cloned.1.call-start = ((), (), s32[]{:S(2)}) async-start(), calls=%async_computation.6 | async-start | bytes 15740928 | tf_op jit(solution)/shard_map/gather_weights/all_gather | solution.py:448
  10.4 9.1 %collective-permute-start.3 = (bf16[144,896]{1,0:T(8,128)(2,1)S(1)}, bf16[144,896]{1,0:T(8,128)(2,1)S(1)}, u32[]{:S(2)}, u32[]{:S(2)}) collective-permute-start(bf16[144,896]{1,0:T(8,128)(2,1)S(1)} %maximum_maximum_fusion.refs_0_), channel_id=1, source_target_pairs={{0,96},{16,112},{32,64},{48,80},{64,32},{80,48},{96,0},{112,16},{1... | collective-permute-start | bytes 774152 | tf_op jit(solution)/shard_map/gather_proj/ppermute | solution.py:22
  13.3 7.7 %collective-permute-start.1 = (bf16[144,896]{1,0:T(8,128)(2,1)S(1)}, bf16[144,896]{1,0:T(8,128)(2,1)S(1)}, u32[]{:S(2)}, u32[]{:S(2)}) collective-permute-start(bf16[144,896]{1,0:T(8,128)(2,1)S(1)} %maximum_maximum_fusion.refs_0_), channel_id=1, source_target_pairs={{0,32},{16,48},{32,0},{48,16},{64,96},{80,112},{96,64},{112,80},{1... | collective-permute-start | bytes 774152 | tf_op jit(solution)/shard_map/gather_proj/ppermute | solution.py:22
  19.5 4.9 %collective-permute-start.4 = (bf16[64,896]{1,0:T(8,128)(2,1)S(1)}, bf16[64,896]{1,0:T(8,128)(2,1)S(1)}, u32[]{:S(2)}, u32[]{:S(2)}) collective-permute-start(bf16[64,896]{1,0:T(8,128)(2,1)S(1)} %slice.54), channel_id=1, source_target_pairs={{0,32},{16,48},{32,0},{48,16},{64,96},{80,112},{96,64},{112,80},{1... | collective-permute-start | bytes 344072 | tf_op jit(solution)/shard_map/gather_proj/ppermute | solution.py:22
  21.0 6.4 %collective-permute-start.5 = (bf16[80,896]{1,0:T(8,128)(2,1)S(1)}, bf16[80,896]{1,0:T(8,128)(2,1)S(1)}, u32[]{:S(2)}, u32[]{:S(2)}) collective-permute-start(bf16[80,896]{1,0:T(8,128)(2,1)S(1)} %slice.55), channel_id=1, source_target_pairs={{0,96},{16,112},{32,64},{48,80},{64,32},{80,48},{96,0},{112,16},{1... | collective-permute-start | bytes 430088 | tf_op jit(solution)/shard_map/gather_proj/ppermute | solution.py:22
  22.7 11.3 %collective-permute-start = (bf16[144,896]{1,0:T(8,128)(2,1)S(1)}, bf16[144,896]{1,0:T(8,128)(2,1)S(1)}, u32[]{:S(2)}, u32[]{:S(2)}) collective-permute-start(bf16[144,896]{1,0:T(8,128)(2,1)S(1)} %maximum_maximum_fusion.refs_0_), channel_id=1, source_target_pairs={{0,16},{16,0},{32,48},{48,32},{64,80},{80,64},{96,112},{112,96},{1... | collective-permute-start | bytes 774152 | tf_op jit(solution)/shard_map/gather_proj/ppermute | solution.py:22
  22.7 12.0 %collective-permute-start.2 = (bf16[144,896]{1,0:T(8,128)(2,1)S(1)}, bf16[144,896]{1,0:T(8,128)(2,1)S(1)}, u32[]{:S(2)}, u32[]{:S(2)}) collective-permute-start(bf16[144,896]{1,0:T(8,128)(2,1)S(1)} %collective-permute-done.1.refs_2_), channel_id=1, source_target_pairs={{0,16},{16,0},{32,48},{48,32},{64,80},{80,64},{96,112},{112,96},{1... | collective-permute-start | bytes 774152 | tf_op jit(solution)/shard_map/gather_proj/ppermute | solution.py:22
  23.2 12.1 %collective-permute-start.7 = (bf16[144,896]{1,0:T(8,128)(2,1)S(1)}, bf16[144,896]{1,0:T(8,128)(2,1)S(1)}, u32[]{:S(2)}, u32[]{:S(2)}) collective-permute-start(bf16[144,896]{1,0:T(8,128)(2,1)S(1)} %collective-permute-done.3.refs_6_), channel_id=1, source_target_pairs={{0,16},{16,0},{32,48},{48,32},{64,80},{80,64},{96,112},{112,96},{1... | collective-permute-start | bytes 774152 | tf_op jit(solution)/shard_map/gather_proj/ppermute | solution.py:22
  27.4 8.7 %collective-permute-start.6 = (bf16[144,896]{1,0:T(8,128)(2,1)S(1)}, bf16[144,896]{1,0:T(8,128)(2,1)S(1)}, u32[]{:S(2)}, u32[]{:S(2)}) collective-permute-start(bf16[144,896]{1,0:T(8,128)(2,1)S(1)} %constant_dynamic-update-slice_fusion.refs_4_), channel_id=1, source_target_pairs={{0,16},{16,0},{32,48},{48,32},{64,80},{80,64},{96,112},{112,96},{1... | collective-permute-start | bytes 774152 | tf_op jit(solution)/shard_map/gather_proj/ppermute | solution.py:22
  29.2 14.9 %all-to-all-start = ((bf16[8,16,896]{2,1,0:T(8,128)(2,1)}), bf16[8,16,896]{2,1,0:T(8,128)(2,1)}, u32[]{:S(2)}, u32[]{:S(2)}) async-start(bf16[8,16,896]{2,1,0:T(8,128)(2,1)} %copy.74), calls=%async_computation | async-start | bytes 458752 | tf_op jit(solution)/shard_map/spread_hidden/all_to_all | solution.py:464
  33.8 128.1 %all-gather.5.cloned.1.call-start = ((), (), s32[]{:S(2)}) async-start(), calls=%async_computation.7 | async-start | bytes 3899392 | tf_op jit(solution)/shard_map/spread_hidden/all_gather | solution.py:466
  33.9 0.7 copy-start.9
  34.6 0.7 copy-start.11
  35.3 0.7 copy-start.13
  36.0 0.7 copy-start.15
  36.7 0.9 copy-start.10
  37.7 1.1 copy-start.12
  38.8 1.0 copy-start.14
  39.7 1.0 copy-start.16
  40.7 2.0 copy-start.21
  72.9 136.9 %reduce-scatter.2.cloned.1.call-start = ((), (), s32[]{:S(2)}) async-start(), calls=%async_computation.8 | async-start | bytes 7483392 | tf_op jit(solution)/shard_map/mid_tail_grads/reduce_scatter | solution.py:588
  79.0 4.2 %copy-start.25 = (s32[256]{0:T(256)S(1)}, s32[256]{0:T(256)}, u32[]{:S(2)}) copy-start(s32[256]{0:T(256)} %param.20) | copy-start | bytes 3076
  89.3 32.6 %copy-start.3 = (bf16[256,2304]{1,0:T(8,128)(2,1)S(1)}, bf16[256,2304]{1,0:T(8,128)(2,1)}, u32[]{:S(2)}) copy-start(bf16[256,2304]{1,0:T(8,128)(2,1)} %target_tail.3) | copy-start | bytes 3538948
  89.3 32.6 %copy-start.4 = (bf16[256,1280]{1,0:T(8,128)(2,1)S(1)}, bf16[256,1280]{1,0:T(8,128)(2,1)}, u32[]{:S(2)}) copy-start(bf16[256,1280]{1,0:T(8,128)(2,1)} %target_mid.3) | copy-start | bytes 1966084
  89.3 32.6 %copy-start.5 = (s32[256,1]{1,0:T(8,128)S(1)}, s32[256,1]{1,0:T(8,128)}, u32[]{:S(2)}) copy-start(s32[256,1]{1,0:T(8,128)} %copy.78.position_ref) | copy-start | bytes 3076
  89.3 32.6 %copy-start.7 = (bf16[256,512]{1,0:T(8,128)(2,1)S(1)}, bf16[256,512]{1,0:T(8,128)(2,1)}, u32[]{:S(2)}) copy-start(bf16[256,512]{1,0:T(8,128)(2,1)} %target_head.3) | copy-start | bytes 786436
  89.3 32.6 %copy-start.17 = (s32[3]{0:T(128)S(1)}, s32[3]{0:T(128)}, u32[]{:S(2)}) copy-start(s32[3]{0:T(128)} %pad_add_fusion.bases_ref) | copy-start | bytes 40
  121.9 1.1 copy-start.8
  123.0 9.6 %copy-start.6 = (bf16[5,448,256]{2,1,0:T(8,128)(2,1)S(1)}, bf16[5,448,256]{2,1,0:T(8,128)(2,1)}, u32[]{:S(2)}) copy-start(bf16[5,448,256]{2,1,0:T(8,128)(2,1)} %get-tuple-element.99.z_ref) | copy-start | bytes 3440644
  136.0 24.4 %all-to-all-start.3 = ((bf16[16,144,256]{2,1,0:T(8,128)(2,1)}), bf16[16,144,256]{2,1,0:T(8,128)(2,1)}, u32[]{:S(2)}, u32[]{:S(2)}) async-start(bf16[16,144,256]{2,1,0:T(8,128)(2,1)} %get-tuple-element.74), calls=%async_computation.3 | async-start | bytes 2359296 | tf_op jit(solution)/shard_map/code_grads/all_to_all | solution.py:571
  140.4 12.2 %collective-permute-start.8 = (bf16[16,16,512]{2,1,0:T(8,128)(2,1)S(1)}, bf16[16,16,512]{2,1,0:T(8,128)(2,1)S(1)}, u32[]{:S(2)}, u32[]{:S(2)}) collective-permute-start(bf16[16,16,512]{2,1,0:T(8,128)(2,1)S(1)} %bitcast.85), channel_id=1, source_target_pairs={{0,32},{16,48},{32,0},{48,16},{64,96},{80,112},{96,64},{112,80},{1... | collective-permute-start | bytes 786440 | tf_op jit(solution)/shard_map/head_grad/ppermute | solution.py:22
  140.8 11.8 %collective-permute-start.9 = (bf16[16,16,512]{2,1,0:T(8,128)(2,1)S(1)}, bf16[16,16,512]{2,1,0:T(8,128)(2,1)S(1)}, u32[]{:S(2)}, u32[]{:S(2)}) collective-permute-start(bf16[16,16,512]{2,1,0:T(8,128)(2,1)S(1)} %bitcast.86), channel_id=1, source_target_pairs={{0,96},{16,112},{32,64},{48,80},{64,32},{80,48},{96,0},{112,16},{1... | collective-permute-start | bytes 786440 | tf_op jit(solution)/shard_map/head_grad/ppermute | solution.py:22
  150.8 1.8 copy-start.2
  152.6 7.6 %collective-permute-start.11 = (bf16[8,16,512]{2,1,0:T(8,128)(2,1)S(1)}, bf16[8,16,512]{2,1,0:T(8,128)(2,1)S(1)}, u32[]{:S(2)}, u32[]{:S(2)}) collective-permute-start(bf16[8,16,512]{2,1,0:T(8,128)(2,1)S(1)} %slice.47), channel_id=1, source_target_pairs={{0,96},{16,112},{32,64},{48,80},{64,32},{80,48},{96,0},{112,16},{1... | collective-permute-start | bytes 393224 | tf_op jit(solution)/shard_map/head_grad/ppermute | solution.py:22
  153.9 6.4 %collective-permute-start.10 = (bf16[8,16,512]{2,1,0:T(8,128)(2,1)S(1)}, bf16[8,16,512]{2,1,0:T(8,128)(2,1)S(1)}, u32[]{:S(2)}, u32[]{:S(2)}) collective-permute-start(bf16[8,16,512]{2,1,0:T(8,128)(2,1)S(1)} %slice.46), channel_id=1, source_target_pairs={{0,32},{16,48},{32,0},{48,16},{64,96},{80,112},{96,64},{112,80},{1... | collective-permute-start | bytes 393224 | tf_op jit(solution)/shard_map/head_grad/ppermute | solution.py:22
  154.5 14.9 %collective-permute-start.13 = (bf16[16,16,512]{2,1,0:T(8,128)(2,1)S(1)}, bf16[16,16,512]{2,1,0:T(8,128)(2,1)S(1)}, u32[]{:S(2)}, u32[]{:S(2)}) collective-permute-start(bf16[16,16,512]{2,1,0:T(8,128)(2,1)S(1)} %bitcast.87), channel_id=1, source_target_pairs={{0,16},{16,0},{32,48},{48,32},{64,80},{80,64},{96,112},{112,96},{1... | collective-permute-start | bytes 786440 | tf_op jit(solution)/shard_map/head_proj_grads/ppermute | solution.py:22
  154.5 15.2 %collective-permute-start.14 = (bf16[16,16,512]{2,1,0:T(8,128)(2,1)S(1)}, bf16[16,16,512]{2,1,0:T(8,128)(2,1)S(1)}, u32[]{:S(2)}, u32[]{:S(2)}) collective-permute-start(bf16[16,16,512]{2,1,0:T(8,128)(2,1)S(1)} %collective-permute-done.8.refs_2_), channel_id=1, source_target_pairs={{0,16},{16,0},{32,48},{48,32},{64,80},{80,64},{96,112},{112,96},{1... | collective-permute-start | bytes 786440 | tf_op jit(solution)/shard_map/head_proj_grads/ppermute | solution.py:22
  155.0 17.4 %collective-permute-start.16 = (bf16[16,16,512]{2,1,0:T(8,128)(2,1)S(1)}, bf16[16,16,512]{2,1,0:T(8,128)(2,1)S(1)}, u32[]{:S(2)}, u32[]{:S(2)}) collective-permute-start(bf16[16,16,512]{2,1,0:T(8,128)(2,1)S(1)} %collective-permute-done.9.refs_6_), channel_id=1, source_target_pairs={{0,16},{16,0},{32,48},{48,32},{64,80},{80,64},{96,112},{112,96},{1... | collective-permute-start | bytes 786440 | tf_op jit(solution)/shard_map/head_proj_grads/ppermute | solution.py:22
  161.9 10.8 %collective-permute-start.15 = (bf16[16,16,512]{2,1,0:T(8,128)(2,1)S(1)}, bf16[16,16,512]{2,1,0:T(8,128)(2,1)S(1)}, u32[]{:S(2)}, u32[]{:S(2)}) collective-permute-start(bf16[16,16,512]{2,1,0:T(8,128)(2,1)S(1)} %pad_maximum_fusion.refs_4_), channel_id=1, source_target_pairs={{0,16},{16,0},{32,48},{48,32},{64,80},{80,64},{96,112},{112,96},{1... | collective-permute-start | bytes 786440 | tf_op jit(solution)/shard_map/head_proj_grads/ppermute | solution.py:22
  166.4 10.2 %copy-start.19 = (bf16[4,224,256]{2,1,0:T(8,128)(2,1)}, bf16[4,224,256]{2,1,0:T(8,128)(2,1)S(1)}, u32[]{:S(2)}) copy-start(bf16[4,224,256]{2,1,0:T(8,128)(2,1)S(1)} %get-tuple-element.94.refs_3_) | copy-start | bytes 1376260
  166.4 7.1 %copy-start.22 = (bf16[16,128,896]{2,1,0:T(8,128)(2,1)S(1)}, bf16[16,128,896]{2,1,0:T(8,128)(2,1)}, u32[]{:S(2)}) copy-start(bf16[16,128,896]{2,1,0:T(8,128)(2,1)} %all-gather.5.cloned.1.call-done) | copy-start | bytes 11010052
  166.4 10.1 %collective-permute-start.12 = (bf16[2,224,256]{2,1,0:T(8,128)(2,1)S(1)}, bf16[2,224,256]{2,1,0:T(8,128)(2,1)S(1)}, u32[]{:S(2)}, u32[]{:S(2)}) collective-permute-start(bf16[2,224,256]{2,1,0:T(8,128)(2,1)S(1)} %get-tuple-element.79), channel_id=1, source_target_pairs={{0,12},{1,13},{2,14},{3,15},{4,8},{5,9},{6,10},{7,11},{8,4},{9,5},... | collective-permute-start | bytes 688136 | tf_op jit(solution)/shard_map/hidden_grad_sum/ppermute | solution.py:22
  169.4 7.7 %collective-permute-start.17 = (bf16[2,224,256]{2,1,0:T(8,128)(2,1)S(1)}, bf16[2,224,256]{2,1,0:T(8,128)(2,1)S(1)}, u32[]{:S(2)}, u32[]{:S(2)}) collective-permute-start(bf16[2,224,256]{2,1,0:T(8,128)(2,1)S(1)} %get-tuple-element.87), channel_id=1, source_target_pairs={{0,4},{1,5},{2,6},{3,7},{4,0},{5,1},{6,2},{7,3},{8,12},{9,13},{10,... | collective-permute-start | bytes 688136 | tf_op jit(solution)/shard_map/hidden_grad_sum/ppermute | solution.py:22
  169.6 9.0 %collective-permute-start.18 = (bf16[2,224,256]{2,1,0:T(8,128)(2,1)S(1)}, bf16[2,224,256]{2,1,0:T(8,128)(2,1)S(1)}, u32[]{:S(2)}, u32[]{:S(2)}) collective-permute-start(bf16[2,224,256]{2,1,0:T(8,128)(2,1)S(1)} %get-tuple-element.89), channel_id=1, source_target_pairs={{0,3},{1,2},{2,1},{3,0},{4,7},{5,6},{6,5},{7,4},{8,11},{9,10},{10,... | collective-permute-start | bytes 688136 | tf_op jit(solution)/shard_map/hidden_grad_sum/ppermute | solution.py:22
  172.4 7.4 %collective-permute-start.19 = (bf16[2,224,256]{2,1,0:T(8,128)(2,1)S(1)}, bf16[2,224,256]{2,1,0:T(8,128)(2,1)S(1)}, u32[]{:S(2)}, u32[]{:S(2)}) collective-permute-start(bf16[2,224,256]{2,1,0:T(8,128)(2,1)S(1)} %get-tuple-element.91), channel_id=1, source_target_pairs={{0,1},{1,0},{2,3},{3,2},{4,5},{5,4},{6,7},{7,6},{8,9},{9,8},{10,11... | collective-permute-start | bytes 688136 | tf_op jit(solution)/shard_map/hidden_grad_sum/ppermute | solution.py:22
  179.9 15.2 %copy-start.20 = (bf16[4,224,256]{2,1,0:T(8,128)(2,1)S(1)}, bf16[4,224,256]{2,1,0:T(8,128)(2,1)}, u32[]{:S(2)}) copy-start(bf16[4,224,256]{2,1,0:T(8,128)(2,1)} %copy-done.19) | copy-start | bytes 1376260
  181.1 11.8 %collective-permute-start.20 = (bf16[4,224,256]{2,1,0:T(8,128)(2,1)}, bf16[4,224,256]{2,1,0:T(8,128)(2,1)S(1)}, u32[]{:S(2)}, u32[]{:S(2)}) collective-permute-start(bf16[4,224,256]{2,1,0:T(8,128)(2,1)} %get-tuple-element.92), channel_id=1, source_target_pairs={{0,4},{1,5},{2,6},{3,7},{4,0},{5,1},{6,2},{7,3},{8,12},{9,13},{10,... | collective-permute-start | bytes 1376264 | tf_op jit(solution)/shard_map/hidden_grad_sum/ppermute | solution.py:22
  182.5 12.4 %collective-permute-start.21 = (bf16[4,224,256]{2,1,0:T(8,128)(2,1)}, bf16[4,224,256]{2,1,0:T(8,128)(2,1)S(1)}, u32[]{:S(2)}, u32[]{:S(2)}) collective-permute-start(bf16[4,224,256]{2,1,0:T(8,128)(2,1)} %get-tuple-element.93), channel_id=1, source_target_pairs={{0,12},{1,13},{2,14},{3,15},{4,8},{5,9},{6,10},{7,11},{8,4},{9,5},... | collective-permute-start | bytes 1376264 | tf_op jit(solution)/shard_map/hidden_grad_sum/ppermute | solution.py:22
  183.0 11.9 %collective-permute-start.22 = (bf16[4,224,256]{2,1,0:T(8,128)(2,1)}, bf16[4,224,256]{2,1,0:T(8,128)(2,1)S(1)}, u32[]{:S(2)}, u32[]{:S(2)}) collective-permute-start(bf16[4,224,256]{2,1,0:T(8,128)(2,1)} %get-tuple-element.95), channel_id=1, source_target_pairs={{0,1},{1,0},{2,3},{3,2},{4,5},{5,4},{6,7},{7,6},{8,9},{9,8},{10,11... | collective-permute-start | bytes 1376264 | tf_op jit(solution)/shard_map/hidden_grad_sum/ppermute | solution.py:22
  183.3 11.8 %collective-permute-start.23 = (bf16[4,224,256]{2,1,0:T(8,128)(2,1)S(1)}, bf16[4,224,256]{2,1,0:T(8,128)(2,1)}, u32[]{:S(2)}, u32[]{:S(2)}) collective-permute-start(bf16[4,224,256]{2,1,0:T(8,128)(2,1)S(1)} %get-tuple-element.96), channel_id=1, source_target_pairs={{0,3},{1,2},{2,1},{3,0},{4,7},{5,6},{6,5},{7,4},{8,11},{9,10},{10,... | collective-permute-start | bytes 1376264 | tf_op jit(solution)/shard_map/hidden_grad_sum/ppermute | solution.py:22
  185.4 20.0 %all-to-all-start.4 = ((bf16[8,256,144]{1,2,0:T(8,128)(2,1)}), bf16[8,256,144]{1,2,0:T(8,128)(2,1)}, u32[]{:S(2)}, u32[]{:S(2)}) async-start(bf16[8,256,144]{1,2,0:T(8,128)(2,1)} %broadcast_in_dim.37), calls=%async_computation.4 | async-start | bytes 1179648 | tf_op jit(solution)/shard_map/hidden_grad_sum/head_proj_grads/all_to_all | solution.py:614
  196.4 16.2 %collective-permute-start.24 = (bf16[224,256]{1,0:T(8,128)(2,1)S(1)}, bf16[224,256]{1,0:T(8,128)(2,1)S(1)}, u32[]{:S(2)}, u32[]{:S(2)}) collective-permute-start(bf16[224,256]{1,0:T(8,128)(2,1)S(1)} %get-tuple-element.108), channel_id=1, source_target_pairs={{0,1},{1,0},{2,3},{3,2},{4,5},{5,4},{6,7},{7,6},{8,9},{9,8},{10,11... | collective-permute-start | bytes 344072 | tf_op jit(solution)/shard_map/hidden_grad_sum/ppermute | solution.py:22
  197.0 16.8 %collective-permute-start.25 = (bf16[224,256]{1,0:T(8,128)(2,1)S(1)}, bf16[224,256]{1,0:T(8,128)(2,1)S(1)}, u32[]{:S(2)}, u32[]{:S(2)}) collective-permute-start(bf16[224,256]{1,0:T(8,128)(2,1)S(1)} %get-tuple-element.109), channel_id=1, source_target_pairs={{0,2},{1,3},{2,0},{3,1},{4,6},{5,7},{6,4},{7,5},{8,10},{9,11},{10,... | collective-permute-start | bytes 344072 | tf_op jit(solution)/shard_map/hidden_grad_sum/ppermute | solution.py:22
  199.7 14.0 %collective-permute-start.26 = (bf16[224,256]{1,0:T(8,128)(2,1)S(1)}, bf16[224,256]{1,0:T(8,128)(2,1)S(1)}, u32[]{:S(2)}, u32[]{:S(2)}) collective-permute-start(bf16[224,256]{1,0:T(8,128)(2,1)S(1)} %get-tuple-element.110), channel_id=1, source_target_pairs={{0,3},{1,2},{2,1},{3,0},{4,7},{5,6},{6,5},{7,4},{8,11},{9,10},{10,... | collective-permute-start | bytes 344072 | tf_op jit(solution)/shard_map/hidden_grad_sum/ppermute | solution.py:22
  201.2 12.6 %collective-permute-start.27 = (bf16[224,256]{1,0:T(8,128)(2,1)S(1)}, bf16[224,256]{1,0:T(8,128)(2,1)S(1)}, u32[]{:S(2)}, u32[]{:S(2)}) collective-permute-start(bf16[224,256]{1,0:T(8,128)(2,1)S(1)} %get-tuple-element.112), channel_id=1, source_target_pairs={{0,4},{1,5},{2,6},{3,7},{4,0},{5,1},{6,2},{7,3},{8,12},{9,13},{10,... | collective-permute-start | bytes 344072 | tf_op jit(solution)/shard_map/hidden_grad_sum/ppermute | solution.py:22
  201.9 11.8 %collective-permute-start.28 = (bf16[224,256]{1,0:T(8,128)(2,1)S(1)}, bf16[224,256]{1,0:T(8,128)(2,1)S(1)}, u32[]{:S(2)}, u32[]{:S(2)}) collective-permute-start(bf16[224,256]{1,0:T(8,128)(2,1)S(1)} %get-tuple-element.113), channel_id=1, source_target_pairs={{0,8},{1,9},{2,10},{3,11},{4,12},{5,13},{6,14},{7,15},{8,0},{9,1},... | collective-permute-start | bytes 344072 | tf_op jit(solution)/shard_map/hidden_grad_sum/ppermute | solution.py:22
  209.9 1.1 copy-start.18
  212.6 6.0 %collective-permute-start.29 = (bf16[224,256]{1,0:T(8,128)(2,1)S(1)}, bf16[224,256]{1,0:T(8,128)(2,1)S(1)}, u32[]{:S(2)}, u32[]{:S(2)}) collective-permute-start(bf16[224,256]{1,0:T(8,128)(2,1)S(1)} %get-tuple-element.114), channel_id=1, source_target_pairs={{0,12},{1,13},{2,14},{3,15},{4,8},{5,9},{6,10},{7,11},{8,4},{9,5},... | collective-permute-start | bytes 344072 | tf_op jit(solution)/shard_map/hidden_grad_sum/ppermute | solution.py:22
  218.7 1.0 copy-start.1
Sparse Core Ops, SparseCore 0:
  10.3 78.1 all-gather.2
  90.6 50.6 all-gather.4
  143.7 46.0 reduce-scatter.1
